TPU v7x, 512 devices: a whole 4x8x8 slice. The times are simulated.
512 devices in a mesh: row: 32 (over y, z_hi), col: 16 (over z_lo, x, core).
Axes of the slice: x: 4, y: 8, z: 8 (z_hi: 4, z_lo: 2; z = z_hi * 2 + z_lo), core: 2. Of those that a mesh axis runs over, the one named last changes fastest.
Arguments:
- right_side: float32 [1, 256, 256, 256], P(None, 'row', 'col'), may hold values from -6 to 6
- lift_scale: float32 [16], replicated, may hold values from 0.5 to 2
- lift_shift: float32 [16], replicated, may hold values from -1.5 to 1.5
- spectral_weight: bfloat16 [64, 64, 16, 16, 128], P('row', 'col'), may hold values from -4 to 4
- local_weight: float32 [16, 16], replicated, may hold values from -1.5 to 1.5
- local_bias: float32 [16], replicated, may hold values from -3 to 3
- readout: float32 [16], replicated, may hold values from -1.5 to 1.5
Outputs:
- residual: float32 [1, 256, 256, 256], P(None, 'row', 'col')
- spectral_grad: bfloat16 [64, 64, 16, 16, 128], P('row', 'col')
All inputs are finite; a program needn't handle non-finite values.
Results may differ from a plain program's by a relative error of at most 0.001.
Values sent between devices are 32-bit elements; how exact they have to be, the bound alone decides.
No kernel may reach another device: no remote copies, remote signals or barrier semaphores. Data moves between devices by JAX's collectives and lax.ppermute only.
A program may use at most 64 MiB of HBM per device.

v0:
```python
import math

import jax
import jax.numpy as jnp
import numpy as np
from jax import lax
from jax.experimental import pallas as pl
from jax.experimental.pallas import tpu as pltpu
from jax.sharding import Mesh
from jax.sharding import PartitionSpec as P

MODES = 64
GRID = 256
WIDTH = 16
HALF = 8
ROWS = 32
PLANES = 8
COLS = 16
ROW = ("y", "zh")
COL = ("zl", "x", "core")
F32 = jnp.float32
BF16 = jnp.bfloat16
VMEM_LIMIT = 40 * 1024 * 1024


def halves(table):
    high = table.astype(jnp.bfloat16)
    low = (table - high.astype(np.float64)).astype(jnp.bfloat16)
    return high, low


def wave(frequencies, points):
    phase = (np.outer(frequencies, points) % GRID) * (2.0 * math.pi / GRID)
    return np.cos(phase) / 16.0, np.sin(phase) / 16.0


def tables():
    points = np.arange(GRID)
    cos_z, sin_z = wave(np.arange(MODES), points)
    z_forward = np.concatenate([cos_z, -sin_z], axis=0)
    weight = np.where(np.arange(MODES) == 0, 1.0, 2.0)[:, None]
    z_inverse = np.concatenate([cos_z * weight, -sin_z * weight], axis=0).T
    ky = np.array([2 * r + a - MODES // 2 for a in range(2) for r in range(ROWS)])
    cos_y, sin_y = wave(ky, points)
    y_table = np.concatenate(
        [np.concatenate([cos_y, sin_y], axis=1), np.concatenate([-sin_y, cos_y], axis=1)], axis=0
    )
    places = np.array([8 * r + q for q in range(PLANES) for r in range(ROWS)])
    cos_x, sin_x = wave(np.arange(MODES) - MODES // 2, places)
    x_table = np.concatenate([cos_x.T, -sin_x.T], axis=1)
    return halves(z_forward), halves(z_inverse), halves(y_table), halves(x_table)


def split(value):
    high = value.astype(BF16)
    return high, (value - high.astype(F32)).astype(BF16)


def dot(left, right, dims):
    return lax.dot_general(left, right, (dims, ((), ())), preferred_element_type=F32)


NN = ((1,), (0,))
NT = ((1,), (1,))


def dot3(left, right, dims):
    total = dot(left[0], right[1], dims) + dot(left[1], right[0], dims)
    return total + dot(left[0], right[0], dims)


ROOT = math.sqrt(2.0 / math.pi)
CUBE = 0.044715


def gelu(value):
    inner = value * (ROOT + (ROOT * CUBE) * (value * value))
    half = 0.5 * value
    return half + half * jnp.tanh(inner)


def gelu_both(value):
    square = value * value
    inner = value * (ROOT + (ROOT * CUBE) * square)
    bent = jnp.tanh(inner)
    cdf = 0.5 + 0.5 * bent
    slope = ROOT + (3.0 * ROOT * CUBE) * square
    return value * cdf, cdf + (0.5 * value) * ((1.0 - bent * bent) * slope)


def lift(field, scale, shift):
    scaled = scale * field
    return gelu(shift + scaled) - gelu(shift - scaled)


def lane_index(shape):
    return lax.broadcasted_iota(jnp.int32, shape, len(shape) - 1)


def swapped(value):
    return pltpu.roll(value, MODES, 1)


def plane_forward(fill, zf, yt, stage_high, stage_low, lines, out):
    for channel in range(HALF):
        fill(channel, stage_high, stage_low)
        z = dot3((zf[0][...], zf[1][...]), (stage_high[...], stage_low[...]), NN)
        lines[:, channel, 0:GRID] = z[:MODES]
        lines[:, channel, GRID:] = z[MODES:]
    modes = split(lines[...].reshape(MODES * HALF, 2 * GRID))
    spectrum = dot3((yt[0][...], yt[1][...]), modes, NT)
    lane = lane_index((ROWS, 128)) // 32
    for tile in range(4):
        parts = [spectrum[b * 32 : b * 32 + 32, tile * 128 : tile * 128 + 128] for b in range(4)]
        for e in range(4):
            total = None
            for b in range(4):
                turn = ((b - e) % 4) * 32
                moved = pltpu.roll(parts[b], turn, 1) if turn else parts[b]
                total = moved if total is None else jnp.where(lane == b, moved, total)
            column = 4 * tile + e
            out[column * 32 : column * 32 + 32, :] = total


def lift_kernel(place, scale, shift, plane, zf0, zf1, yt0, yt1, out, turned, high, low, lines):
    core = place[0]
    turned[...] = plane[...].T

    def fill(channel, stage_high, stage_low):
        gain, offset = scale[core * HALF + channel], shift[core * HALF + channel]
        for t in range(8):
            rows = slice(32 * t, 32 * t + 32)
            stage_high[rows, :], stage_low[rows, :] = split(lift(turned[rows, :], gain, offset))

    plane_forward(fill, (zf0, zf1), (yt0, yt1), high, low, lines, out)


def grad_kernel(adjoint, slope, zf0, zf1, yt0, yt1, out, turned, high, low, lines):
    turned[...] = adjoint[...].T

    def fill(channel, stage_high, stage_low):
        for t in range(8):
            rows = slice(32 * t, 32 * t + 32)
            stage_high[rows, :], stage_low[rows, :] = split(turned[rows, :] * slope[channel, rows, :])

    plane_forward(fill, (zf0, zf1), (yt0, yt1), high, low, lines, out)


def local_kernel(place, scale, shift, weight, bias, plane, out, turned):
    first = place[0] * HALF
    turned[...] = plane[...].T

    def step(t, carry):
        rows = pl.ds(pl.multiple_of(t * 8, 8), 8)
        field = turned[rows, :]
        sums = [jnp.full((8, GRID), bias[first + o], F32) for o in range(HALF)]
        for i in range(WIDTH):
            lifted = lift(field, scale[i], shift[i])
            sums = [sums[o] + weight[i, first + o] * lifted for o in range(HALF)]
        for o in range(HALF):
            out[o, rows, :] = sums[o]
        return carry

    lax.fori_loop(0, GRID // 8, step, 0)


def inverse_kernel(
    place, readout, received, local, plane, zi0, zi1, yt0, yt1, out, slope, grid, lines, spectral, total, padded
):
    core = place[0]
    lane = lane_index((ROWS, 128)) // 32
    for tile in range(4):
        parts = [received[(4 * tile + e) * 32 : (4 * tile + e) * 32 + 32, :] for e in range(4)]
        for b in range(4):
            whole = None
            for e in range(4):
                turn = ((e - b) % 4) * 32
                moved = pltpu.roll(parts[e], turn, 1) if turn else parts[e]
                whole = moved if whole is None else jnp.where(lane == e, moved, whole)
            grid[b * 32 : b * 32 + 32, tile * 128 : tile * 128 + 128] = whole
    lines[...] = dot3(split(grid[...].T), (yt0[...], yt1[...]), NN).reshape(MODES, HALF, 2 * GRID)
    for o in range(HALF):
        modes = jnp.concatenate([lines[:, o, 0:GRID], lines[:, o, GRID:]], axis=0)
        spectral[...] = dot3((zi0[...], zi1[...]), split(modes), NN)
        read = readout[core * HALF + o]
        for t in range(8):
            rows = slice(32 * t, 32 * t + 32)
            value, derivative = gelu_both(spectral[rows, :] + local[o, rows, :])
            slope[o, rows, :] = read * derivative
            if o == 0:
                total[rows, :] = read * value
            else:
                total[rows, :] += read * value
    padded[0:8, :] = jnp.zeros((8, GRID), F32)
    padded[256:264, :] = jnp.zeros((8, GRID), F32)
    padded[4:260, :] = total[...].T
    keep = jnp.where(core == 0, 1.0, 0.0).astype(F32)
    blank = jnp.zeros((1, GRID), F32)
    row = lax.broadcasted_iota(jnp.int32, (24, GRID), 0)
    for c in range(COLS):
        before = plane[16 * c - 1 : 16 * c, :] * keep if c > 0 else blank
        after = plane[16 * c + 16 : 16 * c + 17, :] * keep if c < COLS - 1 else blank
        block = padded[16 * c : 16 * c + 24, :]
        block = jnp.where(row == 1, before, jnp.where(row == 22, after, block))
        out[c, 0:24, :] = block[:, 0:128]
        out[c, 24:48, :] = block[:, 128:256]


def gather_spectra(received, xt0, xt1, sign):
    spectra = []
    for k in range(2):
        lines = jnp.concatenate(
            [received[(2 * q + k) * 32 : (2 * q + k) * 32 + 32, :] for q in range(PLANES)], axis=0
        )
        product = dot3(split(lines.T), (xt0[...], xt1[...]), NN)
        spectra.append(product[:64] + sign * swapped(product[64:]))
    return spectra


def mix_kernel(received, weight, xt0, xt1, out, spectra_out, real, imag):
    low = lane_index((64, 128)) < MODES
    sign = jnp.where(low, -1.0, 1.0).astype(F32)
    for k, spectra in enumerate(gather_spectra(received, xt0, xt1, sign)):
        spectra_out[k] = spectra
        other = swapped(spectra)
        real[k] = jnp.where(low, spectra, other)
        imag[k] = jnp.where(low, other, spectra)
    parts = [[], []]
    for group in range(8):
        a, j = group // 4, group % 4
        first = jnp.zeros((WIDTH, 128), F32)
        second = jnp.zeros((WIDTH, 128), F32)
        for i in range(WIDTH):
            k, row = i // HALF, group * HALF + i % HALF
            tile = weight[a, j, i].astype(F32)
            first = first + tile * real[k, row : row + 1, :]
            second = second + tile * imag[k, row : row + 1, :]
        mixed = first + sign[:WIDTH] * swapped(second)
        parts[0].append(mixed[:HALF])
        parts[1].append(mixed[HALF:])
    for k in range(2):
        mixed = jnp.concatenate(parts[k], axis=0)
        both = jnp.concatenate([mixed, -sign * swapped(mixed)], axis=0)
        result = dot3((xt0[...], xt1[...]), split(both), NT)
        for q in range(PLANES):
            out[(2 * q + k) * 32 : (2 * q + k) * 32 + 32, :] = result[q * 32 : q * 32 + 32]


def outer_kernel(place, received, spectra_in, xt0, xt1, out, real, imag):
    low = lane_index((64, 128)) < MODES
    sign = jnp.where(low, -1.0, 1.0).astype(F32)
    row = lax.broadcasted_iota(jnp.int32, (64, 128), 0)
    zero_mode = jnp.logical_and((row // HALF) % 4 == 0, place[2] == 0)
    doubling = jnp.where(zero_mode, 1.0, 2.0).astype(F32)
    grads = [doubling * g for g in gather_spectra(received, xt0, xt1, sign)]
    turned = [-sign * swapped(g) for g in grads]
    for k in range(2):
        spectra = spectra_in[k]
        other = swapped(spectra)
        real[k] = jnp.where(low, spectra, other)
        imag[k] = jnp.where(low, other, spectra)
    for group in range(8):
        a, j = group // 4, group % 4
        rows = slice(group * HALF, group * HALF + HALF)
        straight = jnp.concatenate([grads[0][rows], grads[1][rows]], axis=0)
        crossed = jnp.concatenate([turned[0][rows], turned[1][rows]], axis=0)
        for i in range(WIDTH):
            k, line = i // HALF, group * HALF + i % HALF
            value = straight * real[k, line : line + 1, :] + crossed * imag[k, line : line + 1, :]
            out[a, j, i] = value.astype(BF16)


def edge_kernel(received, field, planes, lower, upper):
    for q in range(PLANES):
        planes[q] = received[2 * q] + received[2 * q + 1]
    for ref, first, own in ((lower, 0, 0), (upper, PLANES - 2, PLANES - 1)):
        ref[0:48, :] = planes[first]
        ref[48:96, :] = planes[first + 1]
        ref[96:112, :] = field[own, :, 0:128]
        ref[112:128, :] = field[own, :, 128:256]


def stencil_kernel(place, planes, before, after, field, residual, adjoint, wide, sources):
    row_place, col_place = place[1], place[2]
    for q in range(PLANES):
        wide[q + 2, :, 0:128] = planes[q, 0:24, :]
        wide[q + 2, :, 128:256] = planes[q, 24:48, :]
    for p in range(2):
        for base, ref in ((0, before), (PLANES + 2, after)):
            wide[base + p, :, 0:128] = ref[48 * p : 48 * p + 24, :]
            wide[base + p, :, 128:256] = ref[48 * p + 24 : 48 * p + 48, :]
    row = lax.broadcasted_iota(jnp.int32, (24, GRID), 0)
    lane = lane_index((24, GRID))
    sources[...] = jnp.zeros(sources.shape, F32)
    for q in range(PLANES):
        sources[q + 1, 4:20, :] = field[q]
        sources[q + 1, 3:4, :] = wide[q + 2, 1:2, :]
        sources[q + 1, 20:21, :] = wide[q + 2, 22:23, :]
    for base, ref in ((0, before), (PLANES + 1, after)):
        sources[base, 4:20, 0:128] = ref[96:112, :]
        sources[base, 4:20, 128:256] = ref[112:128, :]
    first_row = jnp.where(col_place == 0, 4, 3)
    last_row = jnp.where(col_place == COLS - 1, 19, 20)
    inside = jnp.logical_and(row >= first_row, row <= last_row)

    def cross(get, index):
        centre = get(index)
        beside = get(index - 1) + get(index + 1)
        beside = beside + pltpu.roll(centre, 1, 0) + pltpu.roll(centre, 23, 0)
        left = jnp.where(lane == 0, 0.0, pltpu.roll(centre, 1, 1))
        right = jnp.where(lane == GRID - 1, 0.0, pltpu.roll(centre, GRID - 1, 1))
        return 6.0 * centre - (beside + left + right)

    rest = []
    for p in range(PLANES + 2):
        value = cross(lambda n: wide[n], p + 1) - sources[p]
        keep = inside
        if p == 0:
            keep = jnp.logical_and(inside, row_place > 0)
        if p == PLANES + 1:
            keep = jnp.logical_and(inside, row_place < ROWS - 1)
        value = jnp.where(keep, value, 0.0)
        rest.append(value)
        if 1 <= p <= PLANES:
            residual[p - 1] = value[4:20]
    for q in range(PLANES):
        value = cross(lambda n: rest[n], q + 1)[4:20]
        adjoint[2 * q] = value
        adjoint[2 * q + 1] = value


def call(kernel, operands, scalars, outputs, scratch, flops=0):
    many = isinstance(outputs, list)
    vmem = pl.BlockSpec(memory_space=pltpu.VMEM)
    smem = pl.BlockSpec(memory_space=pltpu.SMEM)
    cost = pl.CostEstimate(flops=flops, bytes_accessed=4 << 20, transcendentals=flops // 16)
    return pl.pallas_call(
        kernel,
        in_specs=[smem] * len(scalars) + [vmem] * len(operands),
        out_specs=[vmem] * len(outputs) if many else vmem,
        out_shape=outputs,
        scratch_shapes=scratch,
        compiler_params=pltpu.CompilerParams(vmem_limit_bytes=VMEM_LIMIT),
        cost_estimate=cost if flops else None,
    )(*scalars, *operands)


def exchange(value, axes):
    return lax.all_to_all(value, axes, split_axis=0, concat_axis=0, tiled=True)


def shape(*sizes):
    return jax.ShapeDtypeStruct(sizes, F32)


def shards(right_side, lift_scale, lift_shift, spectral_weight, local_weight, local_bias, readout):
    zf, zi, yt, xt = tables()
    core = lax.axis_index("core")
    row_place = lax.axis_index(ROW)
    col_place = lax.axis_index(COL)
    place = jnp.stack([core, row_place, col_place]).astype(jnp.int32)
    everywhere = COL + ROW
    field = right_side[0]

    plane = exchange(jnp.repeat(field, 2, axis=0), COL).reshape(GRID, GRID)
    line_scratch = pltpu.VMEM((MODES, HALF, 2 * GRID), F32)
    plane_scratch = [
        pltpu.VMEM((GRID, GRID), F32),
        pltpu.VMEM((GRID, GRID), BF16),
        pltpu.VMEM((GRID, GRID), BF16),
        line_scratch,
    ]
    lifted = call(
        lift_kernel, (plane, *zf, *yt), (place, lift_scale, lift_shift), shape(512, 128), plane_scratch
    )
    lifted = exchange(lifted, everywhere)
    local = call(
        local_kernel,
        (plane,),
        (place, lift_scale, lift_shift, local_weight, local_bias),
        shape(HALF, GRID, GRID),
        [pltpu.VMEM((GRID, GRID), F32)],
        flops=1 << 27,
    )
    pair = pltpu.VMEM((2, 64, 128), F32)
    mixed, spectra = call(
        mix_kernel, (lifted, spectral_weight, *xt), (), [shape(512, 128), shape(2, 64, 128)], [pair, pair]
    )
    mixed = exchange(mixed, everywhere)
    message, slope = call(
        inverse_kernel,
        (mixed, local, plane, *zi, *yt),
        (place, readout),
        [shape(COLS, 48, 128), shape(HALF, GRID, GRID)],
        [
            pltpu.VMEM((128, 512), F32),
            line_scratch,
            pltpu.VMEM((GRID, GRID), F32),
            pltpu.VMEM((GRID, GRID), F32),
            pltpu.VMEM((GRID + 8, GRID), F32),
        ],
    )
    message = exchange(message, COL)
    planes, lower, upper = call(
        edge_kernel, (message, field), (), [shape(PLANES, 48, 128), shape(128, 128), shape(128, 128)], []
    )
    forward = [(i, i + 1) for i in range(ROWS - 1)]
    backward = [(target, source) for source, target in forward]
    before = lax.ppermute(upper, ROW, forward)
    after = lax.ppermute(lower, ROW, backward)
    residual, adjoint = call(
        stencil_kernel,
        (planes, before, after, field),
        (place,),
        [shape(PLANES, COLS, GRID), shape(2 * PLANES, COLS, GRID)],
        [pltpu.VMEM((PLANES + 4, 24, GRID), F32), pltpu.VMEM((PLANES + 2, 24, GRID), F32)],
    )
    adjoint = exchange(adjoint, COL).reshape(GRID, GRID)
    grads = call(grad_kernel, (adjoint, slope, *zf, *yt), (), shape(512, 128), plane_scratch)
    grads = exchange(grads, everywhere)
    spectral_grad = call(
        outer_kernel,
        (grads, spectra, *xt),
        (place,),
        jax.ShapeDtypeStruct(spectral_weight.shape, BF16),
        [pair, pair],
    )
    return residual[None], spectral_grad


def solution(mesh):
    fine = Mesh(mesh.devices.reshape(8, 4, 2, 4, 2), ROW + COL)
    in_specs = (P(None, ROW, COL, None), P(), P(), P(ROW, COL, None, None, None), P(), P(), P())
    out_specs = (P(None, ROW, COL, None), P(ROW, COL, None, None, None))
    return jax.shard_map(shards, mesh=fine, in_specs=in_specs, out_specs=out_specs, check_vma=False)
```

profile of v0, /device:TPU:1, one launch (start us, length us, event | category | flops | bytes accessed | tf_op | source)
XLA Modules:
  0.0 160.2 jit_solution(18311402888604631968)
XLA Ops:
  0.7 1.7 %broadcast_in_dim.6 = f32[8,2,16,256]{3,2,1,0:T(8,128)} broadcast(f32[8,16,256]{2,1,0:T(8,128)} %bitcast.23), dimensions={0,2,3} | broadcast | bytes 393216 | tf_op jit(solution)/shard_map/broadcast_in_dim | solution.py:365
  2.4 10.2 %all-to-all-start = ((f32[16,16,256]{2,1,0:T(8,128)}), f32[16,16,256]{2,1,0:T(8,128)S(1)}, u32[]{:S(2)}, u32[]{:S(2)}) async-start(f32[16,16,256]{2,1,0:T(8,128)} %bitcast.4), calls=%async_computation | async-start | bytes 524288 | tf_op jit(solution)/shard_map/all_to_all | solution.py:349
  12.7 7.2 %all-to-all-done = f32[16,16,256]{2,1,0:T(8,128)S(1)} async-done(((f32[16,16,256]{2,1,0:T(8,128)}), f32[16,16,256]{2,1,0:T(8,128)S(1)}, u32[]{:S(2)}, u32[]{:S(2)}) %all-to-all-start) | async-done | bytes 262176 | tf_op jit(solution)/shard_map/all_to_all | solution.py:349
  19.9 0.9 copy-done
  20.8 0.9 copy-done.2
  21.7 0.8 copy-done.8
  22.5 0.8 copy-done.10
  23.3 0.7 copy-done.14
  24.7 3.7 %shard_map.158 = f32[512,128]{1,0:T(8,128)S(1)} custom-call(s32[3]{0:T(128)S(1)} %pad_add_fusion.place, f32[16]{0:T(128)S(1)} %copy-done.14, f32[16]{0:T(128)S(1)} %copy-done.16, f32[256,256]{1,0:T(8,128)S(1)} %bitcast.20, bf16[128,256]{1,0:T(8,128)(2,1)S(1)} %copy-done.10, bf16[128,256]{1,0:T(8,128)(2,1)S(1)} %copy-done.8, bf16[128,512]{1,0:T(8,128)(2,1)S(1)} %copy-done.2, ...), custom_call_target="tpu_custom_call" | custom-call | tf_op jit(solution)/shard_map/pallas_call | solution.py:337
  28.4 33.2 %all_to_all.48 = f32[512,1,128]{2,1,0:T(1,128)S(1)} all-to-all(f32[512,1,128]{2,1,0:T(1,128)S(1)} %bitcast.30), channel_id=1, replica_groups=mesh['y'=8,'zh'=4,'zl'=2,'x'=4,'core'=2] {'zl','x','core','y','zh'}, dimensions={0} | all-to-all | bytes 524288 | tf_op jit(solution)/shard_map/all_to_all | solution.py:349
  61.6 1.6 %shard_map.159 = (f32[512,128]{1,0:T(8,128)}, f32[2,64,128]{2,1,0:T(8,128)S(1)}) custom-call(f32[512,128]{1,0:T(8,128)S(1)} %bitcast.29, bf16[2,4,16,16,128]{4,3,2,1,0:T(8,128)(2,1)S(1)} %copy-done.5, bf16[256,128]{1,0:T(8,128)(2,1)S(1)} %copy-done.7, bf16[256,128]{1,0:T(8,128)(2,1)S(1)} %copy-done.6), custom_call_target="tpu_custom_call" | custom-call | tf_op jit(solution)/shard_map/pallas_call | solution.py:337
  63.2 8.5 %all-to-all-start.2 = ((f32[512,1,128]{2,1,0:T(1,128)}), f32[512,1,128]{2,1,0:T(1,128)S(1)}, u32[]{:S(2)}, u32[]{:S(2)}) async-start(f32[512,1,128]{2,1,0:T(1,128)} %bitcast.10), calls=%async_computation.2 | async-start | bytes 524288 | tf_op jit(solution)/shard_map/all_to_all | solution.py:349
  71.9 7.9 %shard_map.160.local = f32[8,256,256]{2,1,0:T(8,128)S(1)} custom-call(s32[3]{0:T(128)S(1)} %pad_add_fusion.place, f32[16]{0:T(128)S(1)} %copy-done.15, f32[16]{0:T(128)S(1)} %copy-done.17, f32[16,16]{1,0:T(8,128)S(1)} %copy-done.19, f32[16]{0:T(128)S(1)} %copy-done.20, f32[256,256]{1,0:T(8,128)S(1)} %bitcast.21), custom_call_target="tpu_custom_call" | custom-call | flops 134217728 | bytes 4194304 | tf_op jit(solution)/shard_map/pallas_call | solution.py:337
  79.8 8.9 %all-to-all-done.2 = f32[512,1,128]{2,1,0:T(1,128)S(1)} async-done(((f32[512,1,128]{2,1,0:T(1,128)}), f32[512,1,128]{2,1,0:T(1,128)S(1)}, u32[]{:S(2)}, u32[]{:S(2)}) %all-to-all-start.2) | async-done | bytes 262176 | tf_op jit(solution)/shard_map/all_to_all | solution.py:349
  88.8 3.5 %shard_map.161 = (f32[16,48,128]{2,1,0:T(8,128)S(1)}, f32[8,256,256]{2,1,0:T(8,128)S(1)}) custom-call(s32[3]{0:T(128)S(1)} %pad_add_fusion.place, f32[16]{0:T(128)S(1)} %copy-done.18, f32[512,128]{1,0:T(8,128)S(1)} %bitcast.31, f32[8,256,256]{2,1,0:T(8,128)S(1)} %shard_map.160.local, f32[256,256]{1,0:T(8,128)S(1)} %bitcast.22, ...), custom_call_target="tpu_custom_call" | custom-call | tf_op jit(solution)/shard_map/pallas_call | solution.py:337
  92.3 11.7 %all_to_all.49.received = f32[16,48,128]{2,1,0:T(8,128)S(1)} all-to-all(f32[16,48,128]{2,1,0:T(8,128)S(1)} %get-tuple-element.12), channel_id=1, replica_groups=mesh['y'=8,'zh'=4,'zl'=2,'x'=4,'core'=2] {'zl','x','core'}, dimensions={0} | all-to-all | bytes 786432 | tf_op jit(solution)/shard_map/all_to_all | solution.py:349
  104.0 3.3 %collective-permute-start = (f32[128,128]{1,0:T(8,128)S(1)}, f32[128,128]{1,0:T(8,128)S(1)}, u32[]{:S(2)}, u32[]{:S(2)}) collective-permute-start(f32[128,128]{1,0:T(8,128)S(1)} %get-tuple-element.14), channel_id=1, source_target_pairs={{0,16},{16,32},{32,48},{48,64},{64,80},{80,96},{96,112},{112,128},... | collective-permute-start | bytes 196616 | tf_op jit(solution)/shard_map/ppermute | solution.py:409
  107.3 1.3 collective-permute-start.1
  108.6 5.2 %collective-permute-done.1.after = f32[128,128]{1,0:T(8,128)S(1)} collective-permute-done((f32[128,128]{1,0:T(8,128)S(1)}, f32[128,128]{1,0:T(8,128)S(1)}, u32[]{:S(2)}, u32[]{:S(2)}) %collective-permute-start.1) | collective-permute-done | bytes 65568 | tf_op jit(solution)/shard_map/ppermute | solution.py:410
  113.8 1.4 shard_map.163
  115.2 13.3 %all_to_all.50 = f32[16,16,256]{2,1,0:T(8,128)S(1)} all-to-all(f32[16,16,256]{2,1,0:T(8,128)S(1)} %get-tuple-element.17), channel_id=1, replica_groups=mesh['y'=8,'zh'=4,'zl'=2,'x'=4,'core'=2] {'zl','x','core'}, dimensions={0} | all-to-all | bytes 524288 | tf_op jit(solution)/shard_map/all_to_all | solution.py:349
  128.5 1.9 %shard_map.164 = f32[512,128]{1,0:T(8,128)S(1)} custom-call(f32[256,256]{1,0:T(8,128)S(1)} %bitcast.26, f32[8,256,256]{2,1,0:T(8,128)S(1)} %get-tuple-element.18.slope, bf16[128,256]{1,0:T(8,128)(2,1)S(1)} %copy-done.11, bf16[128,256]{1,0:T(8,128)(2,1)S(1)} %copy-done.9, bf16[128,512]{1,0:T(8,128)(2,1)S(1)} %copy-done.3, bf16[128,512]{1,0:T(8,128)(2,1)S(1)} %copy-done.1), custom_call_target="tpu_custom_call" | custom-call | tf_op jit(solution)/shard_map/pallas_call | solution.py:337
  130.4 27.9 %all_to_all.51 = f32[512,1,128]{2,1,0:T(1,128)S(1)} all-to-all(f32[512,1,128]{2,1,0:T(1,128)S(1)} %bitcast.27), channel_id=1, replica_groups=mesh['y'=8,'zh'=4,'zl'=2,'x'=4,'core'=2] {'zl','x','core','y','zh'}, dimensions={0} | all-to-all | bytes 524288 | tf_op jit(solution)/shard_map/all_to_all | solution.py:349
  158.3 1.9 %shard_map.165 = bf16[2,4,16,16,128]{4,3,2,1,0:T(8,128)(2,1)} custom-call(s32[3]{0:T(128)S(1)} %pad_add_fusion.place, f32[512,128]{1,0:T(8,128)S(1)} %bitcast.28, f32[2,64,128]{2,1,0:T(8,128)S(1)} %get-tuple-element.19.spectra_in, bf16[256,128]{1,0:T(8,128)(2,1)S(1)} %copy-done.7, bf16[256,128]{1,0:T(8,128)(2,1)S(1)} %copy-done.6), custom_call_target="tpu_custom_call" | custom-call | tf_op jit(solution)/shard_map/pallas_call | solution.py:337
  (40 shorter events, 0.9 us)
Async XLA Ops:
  0.6 61.0 %copy-start.6 = (bf16[256,128]{1,0:T(8,128)(2,1)S(1)}, bf16[256,128]{1,0:T(8,128)(2,1)}, u32[]{:S(2)}) copy-start(bf16[256,128]{1,0:T(8,128)(2,1)} %constant.47.clone.xt1) | copy-start | bytes 196612
  0.6 61.0 %copy-start.7 = (bf16[256,128]{1,0:T(8,128)(2,1)S(1)}, bf16[256,128]{1,0:T(8,128)(2,1)}, u32[]{:S(2)}) copy-start(bf16[256,128]{1,0:T(8,128)(2,1)} %constant.46.clone.xt0) | copy-start | bytes 196612
  0.7 71.1 %copy-start.17 = (f32[16]{0:T(128)S(1)}, f32[16]{0:T(128)}, u32[]{:S(2)}) copy-start(f32[16]{0:T(128)} %shift.3) | copy-start | bytes 196
  0.7 71.1 %copy-start.15 = (f32[16]{0:T(128)S(1)}, f32[16]{0:T(128)}, u32[]{:S(2)}) copy-start(f32[16]{0:T(128)} %scale.3) | copy-start | bytes 196
  0.7 60.9 %copy-start.5 = (bf16[2,4,16,16,128]{4,3,2,1,0:T(8,128)(2,1)S(1)}, bf16[2,4,16,16,128]{4,3,2,1,0:T(8,128)(2,1)}, u32[]{:S(2)}) copy-start(bf16[2,4,16,16,128]{4,3,2,1,0:T(8,128)(2,1)} %weight.2) | copy-start | bytes 1572868
  0.7 71.1 %copy-start.20 = (f32[16]{0:T(128)S(1)}, f32[16]{0:T(128)}, u32[]{:S(2)}) copy-start(f32[16]{0:T(128)} %bias.1) | copy-start | bytes 196
  0.7 71.1 %copy-start.19 = (f32[16,16]{1,0:T(8,128)S(1)}, f32[16,16]{1,0:T(8,128)}, u32[]{:S(2)}) copy-start(f32[16,16]{1,0:T(8,128)} %weight.3) | copy-start | bytes 3076
  2.4 17.4 %all-to-all-start = ((f32[16,16,256]{2,1,0:T(8,128)}), f32[16,16,256]{2,1,0:T(8,128)S(1)}, u32[]{:S(2)}, u32[]{:S(2)}) async-start(f32[16,16,256]{2,1,0:T(8,128)} %bitcast.4), calls=%async_computation | async-start | bytes 524288 | tf_op jit(solution)/shard_map/all_to_all | solution.py:349
  19.8 0.9 copy-start
  20.8 0.9 copy-start.2
  21.7 0.8 copy-start.8
  22.5 0.8 copy-start.10
  23.3 0.7 copy-start.14
  63.2 25.5 %all-to-all-start.2 = ((f32[512,1,128]{2,1,0:T(1,128)}), f32[512,1,128]{2,1,0:T(1,128)S(1)}, u32[]{:S(2)}, u32[]{:S(2)}) async-start(f32[512,1,128]{2,1,0:T(1,128)} %bitcast.10), calls=%async_computation.2 | async-start | bytes 524288 | tf_op jit(solution)/shard_map/all_to_all | solution.py:349
  71.8 16.9 %copy-start.1 = (bf16[128,512]{1,0:T(8,128)(2,1)S(1)}, bf16[128,512]{1,0:T(8,128)(2,1)}, u32[]{:S(2)}) copy-start(bf16[128,512]{1,0:T(8,128)(2,1)} %constant.45.clone.yt1) | copy-start | bytes 393220
  71.8 16.9 %copy-start.3 = (bf16[128,512]{1,0:T(8,128)(2,1)S(1)}, bf16[128,512]{1,0:T(8,128)(2,1)}, u32[]{:S(2)}) copy-start(bf16[128,512]{1,0:T(8,128)(2,1)} %constant.44.clone.yt0) | copy-start | bytes 393220
  71.8 16.9 %copy-start.12 = (bf16[256,128]{1,0:T(8,128)(2,1)S(1)}, bf16[256,128]{1,0:T(8,128)(2,1)}, u32[]{:S(2)}) copy-start(bf16[256,128]{1,0:T(8,128)(2,1)} %constant.49.clone.zi1) | copy-start | bytes 196612
  71.9 16.9 %copy-start.13 = (bf16[256,128]{1,0:T(8,128)(2,1)S(1)}, bf16[256,128]{1,0:T(8,128)(2,1)}, u32[]{:S(2)}) copy-start(bf16[256,128]{1,0:T(8,128)(2,1)} %constant.48.clone.zi0) | copy-start | bytes 196612
  71.9 16.9 %copy-start.18 = (f32[16]{0:T(128)S(1)}, f32[16]{0:T(128)}, u32[]{:S(2)}) copy-start(f32[16]{0:T(128)} %readout.1) | copy-start | bytes 196
  79.8 24.1 %copy-start.4 = (f32[1,8,16,256]{3,2,1,0:T(8,128)S(1)}, f32[1,8,16,256]{3,2,1,0:T(8,128)}, u32[]{:S(2)}) copy-start(f32[1,8,16,256]{3,2,1,0:T(8,128)} %param.15) | copy-start | bytes 393220
  88.7 39.8 %copy-start.9 = (bf16[128,256]{1,0:T(8,128)(2,1)S(1)}, bf16[128,256]{1,0:T(8,128)(2,1)}, u32[]{:S(2)}) copy-start(bf16[128,256]{1,0:T(8,128)(2,1)} %constant.43.clone.zf1) | copy-start | bytes 196612
  88.8 39.8 %copy-start.11 = (bf16[128,256]{1,0:T(8,128)(2,1)S(1)}, bf16[128,256]{1,0:T(8,128)(2,1)}, u32[]{:S(2)}) copy-start(bf16[128,256]{1,0:T(8,128)(2,1)} %constant.42.clone.zf0) | copy-start | bytes 196612
  104.0 4.6 %collective-permute-start = (f32[128,128]{1,0:T(8,128)S(1)}, f32[128,128]{1,0:T(8,128)S(1)}, u32[]{:S(2)}, u32[]{:S(2)}) collective-permute-start(f32[128,128]{1,0:T(8,128)S(1)} %get-tuple-element.14), channel_id=1, source_target_pairs={{0,16},{16,32},{32,48},{48,64},{64,80},{80,96},{96,112},{112,128},... | collective-permute-start | bytes 196616 | tf_op jit(solution)/shard_map/ppermute | solution.py:409
  107.3 6.5 %collective-permute-start.1 = (f32[128,128]{1,0:T(8,128)S(1)}, f32[128,128]{1,0:T(8,128)S(1)}, u32[]{:S(2)}, u32[]{:S(2)}) collective-permute-start(f32[128,128]{1,0:T(8,128)S(1)} %get-tuple-element.15), channel_id=1, source_target_pairs={{16,0},{32,16},{48,32},{64,48},{80,64},{96,80},{112,96},{128,112},... | collective-permute-start | bytes 196616 | tf_op jit(solution)/shard_map/ppermute | solution.py:410
  (1 other events, 0.7 us)
where the time goes:
time: 161 us; the launch traced here: 160 us
  blocking collectives  86 us (53%)
  starting transfers between devices  23.3 us (14%)
  Pallas kernels  22.1 us (14%)
  waiting for transfers between devices  21.3 us (13%)
  local copies, waits for them, and re-layouts  6.59 us (4%)
    all_to_all x4, blocking collectives, exchange(): return lax.all_to_all(value, axes, split_axis=0, concat_axis=0, tiled=True)  86 us
    pallas_call x8, Pallas kernels, call(): pl.pallas_call(kernel, in_specs=[smem] * len(scalars) + [vmem] * len(oper...  22.1 us
    all_to_all x2, starting transfers between devices, exchange(): return lax.all_to_all(value, axes, split_axis=0, concat_axis=0, tiled=True)  18.7 us
    all_to_all x2, waiting for transfers between devices, exchange(): return lax.all_to_all(value, axes, split_axis=0, concat_axis=0, tiled=True)  16.1 us
    ppermute x1, waiting for transfers between devices, shards(): after = lax.ppermute(lower, ROW, backward)  5.21 us
    unnamed x42, local copies, waits for them, and re-layouts  4.89 us
    ppermute x1, starting transfers between devices, shards(): before = lax.ppermute(upper, ROW, forward)  3.29 us
  transfers between devices with their start and end apart: 4, of which 3 were waited for; matrix products, arithmetic and copies ran while one was open for 0% of the time, Pallas kernels for 5%

commit v1 on v0

v1 whole, which is shorter than its diff:
```python
import math

import jax
import jax.numpy as jnp
import numpy as np
from jax import lax
from jax.experimental import pallas as pl
from jax.experimental.pallas import tpu as pltpu
from jax.sharding import Mesh
from jax.sharding import PartitionSpec as P

MODES = 64
GRID = 256
WIDTH = 16
HALF = 8
ROWS = 32
PLANES = 8
COLS = 16
ROW = ("y", "zh")
COL = ("zl", "x", "core")
F32 = jnp.float32
BF16 = jnp.bfloat16
VMEM_LIMIT = 40 * 1024 * 1024


def halves(table):
    high = table.astype(jnp.bfloat16)
    low = (table - high.astype(np.float64)).astype(jnp.bfloat16)
    return high, low


def wave(frequencies, points):
    phase = (np.outer(frequencies, points) % GRID) * (2.0 * math.pi / GRID)
    return np.cos(phase) / 16.0, np.sin(phase) / 16.0


def tables():
    points = np.arange(GRID)
    cos_z, sin_z = wave(np.arange(MODES), points)
    z_forward = np.concatenate(halves(np.concatenate([cos_z, -sin_z], axis=0)), axis=0)
    weight = np.where(np.arange(MODES) == 0, 1.0, 2.0)[:, None]
    high, low = halves(np.concatenate([cos_z * weight, -sin_z * weight], axis=0).T)
    z_inverse = np.block([[high, high], [low, np.zeros_like(low)]])
    ky = np.array([2 * r + a - MODES // 2 for a in range(2) for r in range(ROWS)])
    cos_y, sin_y = wave(ky, points)
    y_table = np.concatenate(
        [np.concatenate([cos_y, sin_y], axis=1), np.concatenate([-sin_y, cos_y], axis=1)], axis=0
    )
    y_table = np.concatenate(halves(y_table), axis=0)
    places = np.array([8 * r + q for q in range(PLANES) for r in range(ROWS)])
    cos_x, sin_x = wave(np.arange(MODES) - MODES // 2, places)
    x_table = np.concatenate(halves(np.concatenate([cos_x.T, -sin_x.T], axis=1)), axis=1)
    return z_forward, z_inverse, y_table, x_table


def split(value):
    high = value.astype(BF16)
    return high, (value - high.astype(F32)).astype(BF16)


def dot(left, right, dims):
    return lax.dot_general(left, right, (dims, ((), ())), preferred_element_type=F32)


NN = ((1,), (0,))
NT = ((1,), (1,))


ROOT = math.sqrt(2.0 / math.pi)
CUBE = 0.044715


def gelu(value):
    inner = value * (ROOT + (ROOT * CUBE) * (value * value))
    half = 0.5 * value
    return half + half * jnp.tanh(inner)


def gelu_both(value):
    square = value * value
    inner = value * (ROOT + (ROOT * CUBE) * square)
    bent = jnp.tanh(inner)
    cdf = 0.5 + 0.5 * bent
    slope = ROOT + (3.0 * ROOT * CUBE) * square
    return value * cdf, cdf + (0.5 * value) * ((1.0 - bent * bent) * slope)


def lift(field, scale, shift):
    scaled = scale * field
    return gelu(shift + scaled) - gelu(shift - scaled)


def lane_index(shape):
    return lax.broadcasted_iota(jnp.int32, shape, len(shape) - 1)


def swapped(value):
    return pltpu.roll(value, MODES, 1)


def plane_forward(fill, z_table, y_table, stage_high, stage_low, lines, out):
    for channel in range(HALF):
        fill(channel, stage_high, stage_low)
        z = dot(z_table[...], stage_high[...], NN)
        z = z[:128] + z[128:] + dot(z_table[0:128, :], stage_low[...], NN)
        lines[:, channel, 0:GRID] = z[:MODES]
        lines[:, channel, GRID:] = z[MODES:]
    high, low = split(lines[...].reshape(MODES * HALF, 2 * GRID))
    spectrum = dot(y_table[...], high, NT)
    spectrum = spectrum[:128] + spectrum[128:] + dot(y_table[0:128, :], low, NT)
    lane = lane_index((ROWS, 128)) // 32
    for tile in range(4):
        parts = [spectrum[b * 32 : b * 32 + 32, tile * 128 : tile * 128 + 128] for b in range(4)]
        for e in range(4):
            total = None
            for b in range(4):
                turn = ((b - e) % 4) * 32
                moved = pltpu.roll(parts[b], turn, 1) if turn else parts[b]
                total = moved if total is None else jnp.where(lane == b, moved, total)
            column = 4 * tile + e
            out[column * 32 : column * 32 + 32, :] = total


def lift_kernel(place, params, plane, z_far, y_far, out, turned, high, low, lines, z_table, y_table, sems):
    z_copy = pltpu.make_async_copy(z_far, z_table, sems.at[0])
    y_copy = pltpu.make_async_copy(y_far, y_table, sems.at[1])
    z_copy.start()
    y_copy.start()
    core = place[0]
    turned[...] = plane[...].T
    z_copy.wait()
    y_copy.wait()

    def fill(channel, stage_high, stage_low):
        gain, offset = params[0, core * HALF + channel], params[1, core * HALF + channel]
        for t in range(8):
            rows = slice(32 * t, 32 * t + 32)
            stage_high[rows, :], stage_low[rows, :] = split(lift(turned[rows, :], gain, offset))

    plane_forward(fill, z_table, y_table, high, low, lines, out)


def grad_kernel(adjoint, slope, z_table, y_table, out, turned, high, low, lines):
    turned[...] = adjoint[...].T

    def fill(channel, stage_high, stage_low):
        for t in range(8):
            rows = slice(32 * t, 32 * t + 32)
            stage_high[rows, :], stage_low[rows, :] = split(turned[rows, :] * slope[channel, rows, :])

    plane_forward(fill, z_table, y_table, high, low, lines, out)


def spread_kernel(field, out, sems):
    copies = [pltpu.make_async_copy(field, out.at[:, k], sems.at[k]) for k in range(2)]
    for copy in copies:
        copy.start()
    for copy in copies:
        copy.wait()


def local_kernel(place, params, plane, out, turned):
    first = place[0] * HALF
    turned[...] = plane[...].T

    def step(t, carry):
        rows = pl.ds(pl.multiple_of(t * 8, 8), 8)
        field = turned[rows, :]
        sums = [jnp.full((8, GRID), params[2, first + o], F32) for o in range(HALF)]
        for i in range(WIDTH):
            lifted = lift(field, params[0, i], params[1, i])
            sums = [sums[o] + params[4 + i, first + o] * lifted for o in range(HALF)]
        for o in range(HALF):
            out[o, rows, :] = sums[o]
        return carry

    lax.fori_loop(0, GRID // 8, step, 0)


def inverse_kernel(
    place, params, received, local, plane, z_table, y_table, out, slope, grid, lines, spectral, total, padded
):
    core = place[0]
    lane = lane_index((ROWS, 128)) // 32
    for tile in range(4):
        parts = [received[(4 * tile + e) * 32 : (4 * tile + e) * 32 + 32, :] for e in range(4)]
        for b in range(4):
            whole = None
            for e in range(4):
                turn = ((e - b) % 4) * 32
                moved = pltpu.roll(parts[e], turn, 1) if turn else parts[e]
                whole = moved if whole is None else jnp.where(lane == e, moved, whole)
            grid[b * 32 : b * 32 + 32, tile * 128 : tile * 128 + 128] = whole
    high, low = split(grid[...].T)
    modes = dot(jnp.concatenate([high, high], axis=1), y_table[...], NN) + dot(low, y_table[0:128, :], NN)
    lines[...] = modes.reshape(MODES, HALF, 2 * GRID)
    for o in range(HALF):
        modes = jnp.concatenate([lines[:, o, 0:GRID], lines[:, o, GRID:]], axis=0)
        product = dot(z_table[...], jnp.concatenate(split(modes), axis=0), NN)
        spectral[...] = product[:GRID] + product[GRID:]
        read = params[3, core * HALF + o]
        for t in range(8):
            rows = slice(32 * t, 32 * t + 32)
            value, derivative = gelu_both(spectral[rows, :] + local[o, rows, :])
            slope[o, rows, :] = read * derivative
            if o == 0:
                total[rows, :] = read * value
            else:
                total[rows, :] += read * value
    padded[0:8, :] = jnp.zeros((8, GRID), F32)
    padded[256:264, :] = jnp.zeros((8, GRID), F32)
    padded[4:260, :] = total[...].T
    keep = jnp.where(core == 0, 1.0, 0.0).astype(F32)
    blank = jnp.zeros((1, GRID), F32)
    row = lax.broadcasted_iota(jnp.int32, (24, GRID), 0)
    for c in range(COLS):
        before = plane[16 * c - 1 : 16 * c, :] * keep if c > 0 else blank
        after = plane[16 * c + 16 : 16 * c + 17, :] * keep if c < COLS - 1 else blank
        block = padded[16 * c : 16 * c + 24, :]
        block = jnp.where(row == 1, before, jnp.where(row == 22, after, block))
        out[c, 0:24, :] = block[:, 0:128]
        out[c, 24:48, :] = block[:, 128:256]


def gather_spectra(received, x_table, sign):
    lines = []
    for k in range(2):
        parts = [received[(2 * q + k) * 32 : (2 * q + k) * 32 + 32, :] for q in range(PLANES)]
        lines.append(jnp.concatenate(parts, axis=0).T)
    product = dot(jnp.concatenate(split(jnp.concatenate(lines, axis=0)), axis=0), x_table[...], NN)
    product = product[:, :128] + product[:, 128:]
    product = product[:256] + product[256:]
    first = [product[128 * k : 128 * k + 64] for k in range(2)]
    second = [product[128 * k + 64 : 128 * k + 128] for k in range(2)]
    return [first[k] + sign * swapped(second[k]) for k in range(2)]


def mix_kernel(received, weight, x_table, out, spectra_out, real, imag):
    low = lane_index((64, 128)) < MODES
    sign = jnp.where(low, -1.0, 1.0).astype(F32)
    for k, spectra in enumerate(gather_spectra(received, x_table, sign)):
        spectra_out[k] = spectra
        other = swapped(spectra)
        real[k] = jnp.where(low, spectra, other)
        imag[k] = jnp.where(low, other, spectra)
    parts = [[], []]
    for group in range(8):
        a, j = group // 4, group % 4
        first = jnp.zeros((WIDTH, 128), F32)
        second = jnp.zeros((WIDTH, 128), F32)
        for i in range(WIDTH):
            k, row = i // HALF, group * HALF + i % HALF
            tile = weight[a, j, i].astype(F32)
            first = first + tile * real[k, row : row + 1, :]
            second = second + tile * imag[k, row : row + 1, :]
        mixed = first + sign[:WIDTH] * swapped(second)
        parts[0].append(mixed[:HALF])
        parts[1].append(mixed[HALF:])
    both = []
    for k in range(2):
        mixed = jnp.concatenate(parts[k], axis=0)
        both += [mixed, -sign * swapped(mixed)]
    high, low = split(jnp.concatenate(both, axis=0))
    result = dot(x_table[...], jnp.concatenate([high, high], axis=1), NT) + dot(x_table[:, 0:128], low, NT)
    for q in range(PLANES):
        for k in range(2):
            place = (2 * q + k) * 32
            out[place : place + 32, :] = result[q * 32 : q * 32 + 32, k * 128 : k * 128 + 128]


def outer_kernel(place, received, spectra_in, x_table, out, real, imag):
    low = lane_index((64, 128)) < MODES
    sign = jnp.where(low, -1.0, 1.0).astype(F32)
    row = lax.broadcasted_iota(jnp.int32, (64, 128), 0)
    zero_mode = jnp.logical_and((row // HALF) % 4 == 0, place[2] == 0)
    doubling = jnp.where(zero_mode, 1.0, 2.0).astype(F32)
    grads = [doubling * g for g in gather_spectra(received, x_table, sign)]
    turned = [-sign * swapped(g) for g in grads]
    for k in range(2):
        spectra = spectra_in[k]
        other = swapped(spectra)
        real[k] = jnp.where(low, spectra, other)
        imag[k] = jnp.where(low, other, spectra)
    for group in range(8):
        a, j = group // 4, group % 4
        rows = slice(group * HALF, group * HALF + HALF)
        straight = jnp.concatenate([grads[0][rows], grads[1][rows]], axis=0)
        crossed = jnp.concatenate([turned[0][rows], turned[1][rows]], axis=0)
        for i in range(WIDTH):
            k, line = i // HALF, group * HALF + i % HALF
            value = straight * real[k, line : line + 1, :] + crossed * imag[k, line : line + 1, :]
            out[a, j, i] = value.astype(BF16)


def beside_z(value, lane):
    left = jnp.where(lane == 0, 0.0, pltpu.roll(value, 1, 1))
    return left + jnp.where(lane == GRID - 1, 0.0, pltpu.roll(value, GRID - 1, 1))


def beside_y(value):
    return pltpu.roll(value, 1, 0) + pltpu.roll(value, 23, 0)


def edge_kernel(received, field, wide, lower, upper):
    lane = lane_index((24, GRID))
    for q in range(PLANES):
        for h in range(2):
            rows, lanes = slice(24 * h, 24 * h + 24), slice(128 * h, 128 * h + 128)
            wide[q, :, lanes] = received[2 * q, rows, :] + received[2 * q + 1, rows, :]
    for ref, edge, inner in ((lower, 0, 1), (upper, PLANES - 1, PLANES - 2)):
        value = wide[edge]
        rest = 6.0 * value - (wide[inner] + beside_y(value) + beside_z(value, lane))
        rest = rest[4:20] - field[edge]
        ref[0:24, :] = value[:, 0:128]
        ref[24:48, :] = value[:, 128:256]
        ref[48:64, :] = rest[:, 0:128]
        ref[64:80, :] = rest[:, 128:256]


def stencil_kernel(place, wide, before, after, field, residual, adjoint, sources):
    row_place, col_place = place[1], place[2]
    row = lax.broadcasted_iota(jnp.int32, (24, GRID), 0)
    lane = lane_index((24, GRID))
    first_row = jnp.where(col_place == 0, 4, 3)
    last_row = jnp.where(col_place == COLS - 1, 19, 20)
    inside = jnp.logical_and(row >= first_row, row <= last_row)
    beyond = [jnp.concatenate([ref[0:24, :], ref[24:48, :]], axis=1) for ref in (before, after)]
    values = [beyond[0]] + [wide[q] for q in range(PLANES)] + [beyond[1]]
    rest = []
    for q in range(PLANES):
        sources[q] = jnp.zeros((24, GRID), F32)
        sources[q, 4:20, :] = field[q]
        sources[q, 3:4, :] = wide[q, 1:2, :]
        sources[q, 20:21, :] = wide[q, 22:23, :]
        centre = values[q + 1]
        near = values[q] + values[q + 2] + beside_y(centre) + beside_z(centre, lane)
        value = jnp.where(inside, 6.0 * centre - near - sources[q], 0.0)
        rest.append(value)
        residual[q] = value[4:20]
    outer = []
    for ref, edge, some in ((before, 0, row_place > 0), (after, PLANES - 1, row_place < ROWS - 1)):
        part = jnp.concatenate([ref[48:64, :], ref[64:80, :]], axis=1) - wide[edge, 4:20, :]
        outer.append(jnp.where(some, part, 0.0))
    for q in range(PLANES):
        low = outer[0] if q == 0 else rest[q - 1][4:20]
        high = outer[1] if q == PLANES - 1 else rest[q + 1][4:20]
        near = (beside_y(rest[q]) + beside_z(rest[q], lane))[4:20]
        value = 6.0 * rest[q][4:20] - (low + high + near)
        adjoint[2 * q] = value
        adjoint[2 * q + 1] = value


def call(kernel, operands, scalars, outputs, scratch, flops=0, far=0):
    many = isinstance(outputs, list)
    vmem = pl.BlockSpec(memory_space=pltpu.VMEM)
    smem = pl.BlockSpec(memory_space=pltpu.SMEM)
    hbm = pl.BlockSpec(memory_space=pltpu.HBM)
    cost = pl.CostEstimate(flops=flops, bytes_accessed=4 << 20, transcendentals=flops // 16)
    return pl.pallas_call(
        kernel,
        in_specs=[smem] * len(scalars) + [vmem] * (len(operands) - far) + [hbm] * far,
        out_specs=[vmem] * len(outputs) if many else vmem,
        out_shape=outputs,
        scratch_shapes=scratch,
        compiler_params=pltpu.CompilerParams(vmem_limit_bytes=VMEM_LIMIT),
        cost_estimate=cost if flops else None,
    )(*scalars, *operands)


def exchange(value, axes):
    return lax.all_to_all(value, axes, split_axis=0, concat_axis=0, tiled=True)


def shape(*sizes):
    return jax.ShapeDtypeStruct(sizes, F32)


def shards(right_side, lift_scale, lift_shift, spectral_weight, local_weight, local_bias, readout):
    z_forward, z_inverse, y_table, x_table = tables()
    place = jnp.stack([lax.axis_index("core"), lax.axis_index(ROW), lax.axis_index(COL)]).astype(jnp.int32)
    params = jnp.concatenate([jnp.stack([lift_scale, lift_shift, local_bias, readout]), local_weight], axis=0)
    everywhere = COL + ROW
    field = right_side[0]
    copies = pltpu.SemaphoreType.DMA((2,))

    spread = call(spread_kernel, (field,), (), shape(PLANES, 2, COLS, GRID), [copies], far=1)
    plane = exchange(spread.reshape(COLS, COLS, GRID), COL).reshape(GRID, GRID)
    line_scratch = pltpu.VMEM((MODES, HALF, 2 * GRID), F32)
    plane_scratch = [
        pltpu.VMEM((GRID, GRID), F32),
        pltpu.VMEM((GRID, GRID), BF16),
        pltpu.VMEM((GRID, GRID), BF16),
        line_scratch,
    ]
    lifted = call(
        lift_kernel,
        (plane, z_forward, y_table),
        (place, params),
        shape(512, 128),
        plane_scratch + [pltpu.VMEM(z_forward.shape, BF16), pltpu.VMEM(y_table.shape, BF16), copies],
        far=2,
    )
    lifted = exchange(lifted, everywhere)
    local = call(
        local_kernel,
        (plane,),
        (place, params),
        shape(HALF, GRID, GRID),
        [pltpu.VMEM((GRID, GRID), F32)],
        flops=1 << 27,
    )
    pair = pltpu.VMEM((2, 64, 128), F32)
    mixed, spectra = call(
        mix_kernel, (lifted, spectral_weight, x_table), (), [shape(512, 128), shape(2, 64, 128)], [pair, pair]
    )
    mixed = exchange(mixed, everywhere)
    message, slope = call(
        inverse_kernel,
        (mixed, local, plane, z_inverse, y_table),
        (place, params),
        [shape(COLS, 48, 128), shape(HALF, GRID, GRID)],
        [
            pltpu.VMEM((128, 512), F32),
            line_scratch,
            pltpu.VMEM((GRID, GRID), F32),
            pltpu.VMEM((GRID, GRID), F32),
            pltpu.VMEM((GRID + 8, GRID), F32),
        ],
    )
    message = exchange(message, COL)
    wide, lower, upper = call(
        edge_kernel, (message, field), (), [shape(PLANES, 24, GRID), shape(80, 128), shape(80, 128)], []
    )
    forward = [(i, i + 1) for i in range(ROWS - 1)]
    backward = [(target, source) for source, target in forward]
    before = lax.ppermute(upper, ROW, forward)
    after = lax.ppermute(lower, ROW, backward)
    residual, adjoint = call(
        stencil_kernel,
        (wide, before, after, field),
        (place,),
        [shape(PLANES, COLS, GRID), shape(2 * PLANES, COLS, GRID)],
        [pltpu.VMEM((PLANES, 24, GRID), F32)],
    )
    adjoint = exchange(adjoint, COL).reshape(GRID, GRID)
    grads = call(grad_kernel, (adjoint, slope, z_forward, y_table), (), shape(512, 128), plane_scratch)
    grads = exchange(grads, everywhere)
    spectral_grad = call(
        outer_kernel,
        (grads, spectra, x_table),
        (place,),
        jax.ShapeDtypeStruct(spectral_weight.shape, BF16),
        [pair, pair],
    )
    return residual[None], spectral_grad


def solution(mesh):
    fine = Mesh(mesh.devices.reshape(8, 4, 2, 4, 2), ROW + COL)
    in_specs = (P(None, ROW, COL, None), P(), P(), P(ROW, COL, None, None, None), P(), P(), P())
    out_specs = (P(None, ROW, COL, None), P(ROW, COL, None, None, None))
    return jax.shard_map(shards, mesh=fine, in_specs=in_specs, out_specs=out_specs, check_vma=False)
```

time: 161 us -> 157 us (0.975)
  waiting for transfers between devices: 21.3 us -> 18.8 us
  local copies, waits for them, and re-layouts: 6.59 us -> 4.28 us
    unnamed x42 -> x18, local copies, waits for them, and re-layouts: 4.89 us -> 2.78 us
    broadcast_in_dim x1 -> x0, local copies, waits for them, and re-layouts: 1.7 us -> none  [shards(): plane = exchange(jnp.repeat(field, 2, axis=0), COL).reshape(GRID, GRID)]
    pallas_call x8 -> x9, Pallas kernels: 22.1 us -> 22.9 us  [call(): pl.pallas_call(kernel, in_specs=[smem] * len(scalars) + [vmem] * (len(ope...]
  transfers between devices with their start and end apart: 4 -> 4, of which waited for: 3 -> 3; matrix products, arithmetic and copies ran while one was open for 0% -> 1% of each run, Pallas kernels for 5% -> 5%
where the time goes in v1:
time: 157 us; the launch traced here: 156 us
  blocking collectives  86.4 us (55%)
  starting transfers between devices  23.1 us (15%)
  Pallas kernels  22.9 us (15%)
  waiting for transfers between devices  18.8 us (12%)
  local copies, waits for them, and re-layouts  4.28 us (3%)
    all_to_all x4, blocking collectives, exchange(): return lax.all_to_all(value, axes, split_axis=0, concat_axis=0, tiled=True)  86.4 us
    pallas_call x9, Pallas kernels, call(): pl.pallas_call(kernel, in_specs=[smem] * len(scalars) + [vmem] * (len(ope...  22.9 us
    all_to_all x2, starting transfers between devices, exchange(): return lax.all_to_all(value, axes, split_axis=0, concat_axis=0, tiled=True)  18.6 us
    all_to_all x2, waiting for transfers between devices, exchange(): return lax.all_to_all(value, axes, split_axis=0, concat_axis=0, tiled=True)  14.5 us
    ppermute x1, waiting for transfers between devices, shards(): after = lax.ppermute(lower, ROW, backward)  4.33 us
    ppermute x1, starting transfers between devices, shards(): before = lax.ppermute(upper, ROW, forward)  3.28 us
  transfers between devices with their start and end apart: 4, of which 3 were waited for; matrix products, arithmetic and copies ran while one was open for 1% of the time, Pallas kernels for 5%

profile of v1, /device:TPU:1, one launch (start us, length us, event | category | flops | bytes accessed | tf_op | source)
XLA Modules:
  0.0 156.3 jit_solution(7855088510088656266)
XLA Ops:
  0.6 0.9 copy-done.2
  1.5 0.8 shard_map.122
  2.3 10.2 %all-to-all-start = ((f32[16,16,256]{2,1,0:T(8,128)}), f32[16,16,256]{2,1,0:T(8,128)S(1)}, u32[]{:S(2)}, u32[]{:S(2)}) async-start(f32[16,16,256]{2,1,0:T(8,128)} %bitcast.8), calls=%async_computation | async-start | bytes 524288 | tf_op jit(solution)/shard_map/all_to_all | solution.py:371
  12.5 1.5 concatenate.3.params
  14.1 5.7 %all-to-all-done = f32[16,16,256]{2,1,0:T(8,128)S(1)} async-done(((f32[16,16,256]{2,1,0:T(8,128)}), f32[16,16,256]{2,1,0:T(8,128)S(1)}, u32[]{:S(2)}, u32[]{:S(2)}) %all-to-all-start) | async-done | bytes 262176 | tf_op jit(solution)/shard_map/all_to_all | solution.py:371
  19.8 0.9 copy-done
  20.7 0.9 copy-done.5
  21.6 3.9 %shard_map.123 = f32[512,128]{1,0:T(8,128)S(1)} custom-call(s32[3]{0:T(128)S(1)} %pad_add_fusion.place, f32[20,16]{1,0:T(8,128)S(1)} %concatenate.3.params, f32[256,256]{1,0:T(8,128)S(1)} %bitcast.24, bf16[256,256]{1,0:T(8,128)(2,1)S(1)} %copy-done.5, bf16[256,512]{1,0:T(8,128)(2,1)S(1)} %copy-done), custom_call_target="tpu_custom_call" | custom-call | tf_op jit(solution)/shard_map/pallas_call | solution.py:359
  25.5 33.2 %all_to_all.48 = f32[512,1,128]{2,1,0:T(1,128)S(1)} all-to-all(f32[512,1,128]{2,1,0:T(1,128)S(1)} %bitcast.34), channel_id=1, replica_groups=mesh['y'=8,'zh'=4,'zl'=2,'x'=4,'core'=2] {'zl','x','core','y','zh'}, dimensions={0} | all-to-all | bytes 524288 | tf_op jit(solution)/shard_map/all_to_all | solution.py:371
  58.7 1.7 %shard_map.124 = (f32[512,128]{1,0:T(8,128)}, f32[2,64,128]{2,1,0:T(8,128)S(1)}) custom-call(f32[512,128]{1,0:T(8,128)S(1)} %bitcast.33, bf16[2,4,16,16,128]{4,3,2,1,0:T(8,128)(2,1)S(1)} %copy-done.7, bf16[256,256]{1,0:T(8,128)(2,1)S(1)} %copy-done.4), custom_call_target="tpu_custom_call" | custom-call | tf_op jit(solution)/shard_map/pallas_call | solution.py:359
  60.4 8.3 %all-to-all-start.2 = ((f32[512,1,128]{2,1,0:T(1,128)}), f32[512,1,128]{2,1,0:T(1,128)S(1)}, u32[]{:S(2)}, u32[]{:S(2)}) async-start(f32[512,1,128]{2,1,0:T(1,128)} %bitcast.14), calls=%async_computation.2 | async-start | bytes 524288 | tf_op jit(solution)/shard_map/all_to_all | solution.py:371
  68.8 8.3 %shard_map.125.local = f32[8,256,256]{2,1,0:T(8,128)S(1)} custom-call(s32[3]{0:T(128)S(1)} %pad_add_fusion.place, f32[20,16]{1,0:T(8,128)S(1)} %concatenate.3.params, f32[256,256]{1,0:T(8,128)S(1)} %bitcast.25), custom_call_target="tpu_custom_call" | custom-call | flops 134217728 | bytes 4194304 | tf_op jit(solution)/shard_map/pallas_call | solution.py:359
  77.0 8.8 %all-to-all-done.2 = f32[512,1,128]{2,1,0:T(1,128)S(1)} async-done(((f32[512,1,128]{2,1,0:T(1,128)}), f32[512,1,128]{2,1,0:T(1,128)S(1)}, u32[]{:S(2)}, u32[]{:S(2)}) %all-to-all-start.2) | async-done | bytes 262176 | tf_op jit(solution)/shard_map/all_to_all | solution.py:371
  85.8 3.4 %shard_map.126 = (f32[16,48,128]{2,1,0:T(8,128)S(1)}, f32[8,256,256]{2,1,0:T(8,128)S(1)}) custom-call(s32[3]{0:T(128)S(1)} %pad_add_fusion.place, f32[20,16]{1,0:T(8,128)S(1)} %concatenate.3.params, f32[512,128]{1,0:T(8,128)S(1)} %bitcast.35, f32[8,256,256]{2,1,0:T(8,128)S(1)} %shard_map.125.local, f32[256,256]{1,0:T(8,128)S(1)} %bitcast.26, ...), custom_call_target="tpu_custom_call" | custom-call | tf_op jit(solution)/shard_map/pallas_call | solution.py:359
  89.2 11.7 %all_to_all.49.received = f32[16,48,128]{2,1,0:T(8,128)S(1)} all-to-all(f32[16,48,128]{2,1,0:T(8,128)S(1)} %get-tuple-element.12), channel_id=1, replica_groups=mesh['y'=8,'zh'=4,'zl'=2,'x'=4,'core'=2] {'zl','x','core'}, dimensions={0} | all-to-all | bytes 786432 | tf_op jit(solution)/shard_map/all_to_all | solution.py:371
  100.9 0.1 shard_map.127
  101.0 3.3 %collective-permute-start = (f32[80,128]{1,0:T(8,128)S(1)}, f32[80,128]{1,0:T(8,128)S(1)}, u32[]{:S(2)}, u32[]{:S(2)}) collective-permute-start(f32[80,128]{1,0:T(8,128)S(1)} %get-tuple-element.14), channel_id=1, source_target_pairs={{0,16},{16,32},{32,48},{48,64},{64,80},{80,96},{96,112},{112,128},... | collective-permute-start | bytes 122888 | tf_op jit(solution)/shard_map/ppermute | solution.py:436
  104.3 1.3 collective-permute-start.1
  105.6 4.3 %collective-permute-done.1.after = f32[80,128]{1,0:T(8,128)S(1)} collective-permute-done((f32[80,128]{1,0:T(8,128)S(1)}, f32[80,128]{1,0:T(8,128)S(1)}, u32[]{:S(2)}, u32[]{:S(2)}) %collective-permute-start.1) | collective-permute-done | bytes 40992 | tf_op jit(solution)/shard_map/ppermute | solution.py:437
  109.9 1.4 shard_map.128
  111.3 12.7 %all_to_all.50 = f32[16,16,256]{2,1,0:T(8,128)S(1)} all-to-all(f32[16,16,256]{2,1,0:T(8,128)S(1)} %get-tuple-element.17), channel_id=1, replica_groups=mesh['y'=8,'zh'=4,'zl'=2,'x'=4,'core'=2] {'zl','x','core'}, dimensions={0} | all-to-all | bytes 524288 | tf_op jit(solution)/shard_map/all_to_all | solution.py:371
  124.0 1.6 %shard_map.129 = f32[512,128]{1,0:T(8,128)S(1)} custom-call(f32[256,256]{1,0:T(8,128)S(1)} %bitcast.30, f32[8,256,256]{2,1,0:T(8,128)S(1)} %get-tuple-element.18.slope, bf16[256,256]{1,0:T(8,128)(2,1)S(1)} %copy-done.6, bf16[256,512]{1,0:T(8,128)(2,1)S(1)} %copy-done.1), custom_call_target="tpu_custom_call" | custom-call | tf_op jit(solution)/shard_map/pallas_call | solution.py:359
  125.6 28.8 %all_to_all.51 = f32[512,1,128]{2,1,0:T(1,128)S(1)} all-to-all(f32[512,1,128]{2,1,0:T(1,128)S(1)} %bitcast.32), channel_id=1, replica_groups=mesh['y'=8,'zh'=4,'zl'=2,'x'=4,'core'=2] {'zl','x','core','y','zh'}, dimensions={0} | all-to-all | bytes 524288 | tf_op jit(solution)/shard_map/all_to_all | solution.py:371
  154.4 1.9 %shard_map.130 = bf16[2,4,16,16,128]{4,3,2,1,0:T(8,128)(2,1)} custom-call(s32[3]{0:T(128)S(1)} %pad_add_fusion.place, f32[512,128]{1,0:T(8,128)S(1)} %bitcast.31, f32[2,64,128]{2,1,0:T(8,128)S(1)} %get-tuple-element.19.spectra_in, bf16[256,256]{1,0:T(8,128)(2,1)S(1)} %copy-done.4), custom_call_target="tpu_custom_call" | custom-call | tf_op jit(solution)/shard_map/pallas_call | solution.py:359
  (17 shorter events, 0.1 us)
Async XLA Ops:
  0.6 0.9 copy-start.2
  1.5 57.2 %copy-start.4 = (bf16[256,256]{1,0:T(8,128)(2,1)S(1)}, bf16[256,256]{1,0:T(8,128)(2,1)}, u32[]{:S(2)}) copy-start(bf16[256,256]{1,0:T(8,128)(2,1)} %constant.36.clone.x_table) | copy-start | bytes 393220
  1.5 57.2 %copy-start.7 = (bf16[2,4,16,16,128]{4,3,2,1,0:T(8,128)(2,1)S(1)}, bf16[2,4,16,16,128]{4,3,2,1,0:T(8,128)(2,1)}, u32[]{:S(2)}) copy-start(bf16[2,4,16,16,128]{4,3,2,1,0:T(8,128)(2,1)} %weight.1) | copy-start | bytes 1572868
  2.3 17.5 %all-to-all-start = ((f32[16,16,256]{2,1,0:T(8,128)}), f32[16,16,256]{2,1,0:T(8,128)S(1)}, u32[]{:S(2)}, u32[]{:S(2)}) async-start(f32[16,16,256]{2,1,0:T(8,128)} %bitcast.8), calls=%async_computation | async-start | bytes 524288 | tf_op jit(solution)/shard_map/all_to_all | solution.py:371
  19.8 1.0 copy-start
  20.7 0.9 copy-start.5
  60.4 25.5 %all-to-all-start.2 = ((f32[512,1,128]{2,1,0:T(1,128)}), f32[512,1,128]{2,1,0:T(1,128)S(1)}, u32[]{:S(2)}, u32[]{:S(2)}) async-start(f32[512,1,128]{2,1,0:T(1,128)} %bitcast.14), calls=%async_computation.2 | async-start | bytes 524288 | tf_op jit(solution)/shard_map/all_to_all | solution.py:371
  68.7 17.1 %copy-start.1 = (bf16[256,512]{1,0:T(8,128)(2,1)S(1)}, bf16[256,512]{1,0:T(8,128)(2,1)}, u32[]{:S(2)}) copy-start(bf16[256,512]{1,0:T(8,128)(2,1)} %constant.35.clone.y_far.y_table) | copy-start | bytes 786436
  68.7 17.1 %copy-start.8 = (bf16[512,256]{1,0:T(8,128)(2,1)S(1)}, bf16[512,256]{1,0:T(8,128)(2,1)}, u32[]{:S(2)}) copy-start(bf16[512,256]{1,0:T(8,128)(2,1)} %constant.37.clone.z_table) | copy-start | bytes 786436
  77.0 23.9 %copy-start.3 = (f32[1,8,16,256]{3,2,1,0:T(8,128)S(1)}, f32[1,8,16,256]{3,2,1,0:T(8,128)}, u32[]{:S(2)}) copy-start(f32[1,8,16,256]{3,2,1,0:T(8,128)} %param.11) | copy-start | bytes 393220
  85.8 38.2 %copy-start.6 = (bf16[256,256]{1,0:T(8,128)(2,1)S(1)}, bf16[256,256]{1,0:T(8,128)(2,1)}, u32[]{:S(2)}) copy-start(bf16[256,256]{1,0:T(8,128)(2,1)} %constant.34.clone.z_far.z_table) | copy-start | bytes 393220
  101.0 4.6 %collective-permute-start = (f32[80,128]{1,0:T(8,128)S(1)}, f32[80,128]{1,0:T(8,128)S(1)}, u32[]{:S(2)}, u32[]{:S(2)}) collective-permute-start(f32[80,128]{1,0:T(8,128)S(1)} %get-tuple-element.14), channel_id=1, source_target_pairs={{0,16},{16,32},{32,48},{48,64},{64,80},{80,96},{96,112},{112,128},... | collective-permute-start | bytes 122888 | tf_op jit(solution)/shard_map/ppermute | solution.py:436
  104.3 5.6 %collective-permute-start.1 = (f32[80,128]{1,0:T(8,128)S(1)}, f32[80,128]{1,0:T(8,128)S(1)}, u32[]{:S(2)}, u32[]{:S(2)}) collective-permute-start(f32[80,128]{1,0:T(8,128)S(1)} %get-tuple-element.15), channel_id=1, source_target_pairs={{16,0},{32,16},{48,32},{64,48},{80,64},{96,80},{112,96},{128,112},... | collective-permute-start | bytes 122888 | tf_op jit(solution)/shard_map/ppermute | solution.py:437

commit v2 on v1

--- a/solution.py
+++ b/solution.py
@@ -76,18 +76,20 @@
     return half + half * jnp.tanh(inner)
 
 
-def gelu_both(value):
+def gelu_slope(value):
     square = value * value
-    inner = value * (ROOT + (ROOT * CUBE) * square)
-    bent = jnp.tanh(inner)
-    cdf = 0.5 + 0.5 * bent
+    bent = jnp.tanh(value * (ROOT + (ROOT * CUBE) * square))
     slope = ROOT + (3.0 * ROOT * CUBE) * square
-    return value * cdf, cdf + (0.5 * value) * ((1.0 - bent * bent) * slope)
-
-
-def lift(field, scale, shift):
-    scaled = scale * field
-    return gelu(shift + scaled) - gelu(shift - scaled)
+    return 0.5 + 0.5 * bent + (0.5 * value) * ((1.0 - bent * bent) * slope)
+
+
+def bent_half(half):
+    return half * jnp.tanh(half * (2.0 * ROOT + (8.0 * ROOT * CUBE) * (half * half)))
+
+
+def lift(field, half_scale, half_shift):
+    scaled = half_scale * field
+    return (scaled + scaled) + (bent_half(half_shift + scaled) - bent_half(half_shift - scaled))
 
 
 def lane_index(shape):
@@ -98,13 +100,16 @@
     return pltpu.roll(value, MODES, 1)
 
 
-def plane_forward(fill, z_table, y_table, stage_high, stage_low, lines, out):
+def plane_forward(fill, z_table, y_table, stage_high, stage_low, lines, out, ready=lambda n: None):
     for channel in range(HALF):
         fill(channel, stage_high, stage_low)
+        if channel == 0:
+            ready(0)
         z = dot(z_table[...], stage_high[...], NN)
         z = z[:128] + z[128:] + dot(z_table[0:128, :], stage_low[...], NN)
         lines[:, channel, 0:GRID] = z[:MODES]
         lines[:, channel, GRID:] = z[MODES:]
+    ready(1)
     high, low = split(lines[...].reshape(MODES * HALF, 2 * GRID))
     spectrum = dot(y_table[...], high, NT)
     spectrum = spectrum[:128] + spectrum[128:] + dot(y_table[0:128, :], low, NT)
@@ -128,16 +133,14 @@
     y_copy.start()
     core = place[0]
     turned[...] = plane[...].T
-    z_copy.wait()
-    y_copy.wait()
 
     def fill(channel, stage_high, stage_low):
-        gain, offset = params[0, core * HALF + channel], params[1, core * HALF + channel]
+        gain, offset = 0.5 * params[0, core * HALF + channel], 0.5 * params[1, core * HALF + channel]
         for t in range(8):
             rows = slice(32 * t, 32 * t + 32)
             stage_high[rows, :], stage_low[rows, :] = split(lift(turned[rows, :], gain, offset))
 
-    plane_forward(fill, z_table, y_table, high, low, lines, out)
+    plane_forward(fill, z_table, y_table, high, low, lines, out, lambda n: (z_copy, y_copy)[n].wait())
 
 
 def grad_kernel(adjoint, slope, z_table, y_table, out, turned, high, low, lines):
@@ -168,7 +171,7 @@
         field = turned[rows, :]
         sums = [jnp.full((8, GRID), params[2, first + o], F32) for o in range(HALF)]
         for i in range(WIDTH):
-            lifted = lift(field, params[0, i], params[1, i])
+            lifted = lift(field, 0.5 * params[0, i], 0.5 * params[1, i])
             sums = [sums[o] + params[4 + i, first + o] * lifted for o in range(HALF)]
         for o in range(HALF):
             out[o, rows, :] = sums[o]
@@ -178,7 +181,7 @@
 
 
 def inverse_kernel(
-    place, params, received, local, plane, z_table, y_table, out, slope, grid, lines, spectral, total, padded
+    place, params, received, local, plane, z_table, y_table, out, preact, grid, lines, spectral, total, padded
 ):
     core = place[0]
     lane = lane_index((ROWS, 128)) // 32
@@ -201,12 +204,12 @@
         read = params[3, core * HALF + o]
         for t in range(8):
             rows = slice(32 * t, 32 * t + 32)
-            value, derivative = gelu_both(spectral[rows, :] + local[o, rows, :])
-            slope[o, rows, :] = read * derivative
+            value = spectral[rows, :] + local[o, rows, :]
+            preact[o, rows, :] = value
             if o == 0:
-                total[rows, :] = read * value
+                total[rows, :] = read * gelu(value)
             else:
-                total[rows, :] += read * value
+                total[rows, :] += read * gelu(value)
     padded[0:8, :] = jnp.zeros((8, GRID), F32)
     padded[256:264, :] = jnp.zeros((8, GRID), F32)
     padded[4:260, :] = total[...].T
@@ -220,6 +223,14 @@
         block = jnp.where(row == 1, before, jnp.where(row == 22, after, block))
         out[c, 0:24, :] = block[:, 0:128]
         out[c, 24:48, :] = block[:, 128:256]
+
+
+def slope_kernel(place, params, preact, out):
+    for o in range(HALF):
+        read = params[3, place[0] * HALF + o]
+        for t in range(8):
+            rows = slice(32 * t, 32 * t + 32)
+            out[o, rows, :] = read * gelu_slope(preact[o, rows, :])
 
 
 def gather_spectra(received, x_table, sign):
@@ -268,7 +279,7 @@
             out[place : place + 32, :] = result[q * 32 : q * 32 + 32, k * 128 : k * 128 + 128]
 
 
-def outer_kernel(place, received, spectra_in, x_table, out, real, imag):
+def outer_kernel(place, received, spectra_in, x_table, out, real, imag, stage, sems):
     low = lane_index((64, 128)) < MODES
     sign = jnp.where(low, -1.0, 1.0).astype(F32)
     row = lax.broadcasted_iota(jnp.int32, (64, 128), 0)
@@ -281,6 +292,7 @@
         other = swapped(spectra)
         real[k] = jnp.where(low, spectra, other)
         imag[k] = jnp.where(low, other, spectra)
+    copies = []
     for group in range(8):
         a, j = group // 4, group % 4
         rows = slice(group * HALF, group * HALF + HALF)
@@ -289,7 +301,11 @@
         for i in range(WIDTH):
             k, line = i // HALF, group * HALF + i % HALF
             value = straight * real[k, line : line + 1, :] + crossed * imag[k, line : line + 1, :]
-            out[a, j, i] = value.astype(BF16)
+            stage[a, j, i] = value.astype(BF16)
+        copies.append(pltpu.make_async_copy(stage.at[a, j], out.at[a, j], sems.at[group]))
+        copies[-1].start()
+    for copy in copies:
+        copy.wait()
 
 
 def beside_z(value, lane):
@@ -317,49 +333,70 @@
         ref[64:80, :] = rest[:, 128:256]
 
 
-def stencil_kernel(place, wide, before, after, field, residual, adjoint, sources):
-    row_place, col_place = place[1], place[2]
+def inside_rows(col_place):
     row = lax.broadcasted_iota(jnp.int32, (24, GRID), 0)
-    lane = lane_index((24, GRID))
     first_row = jnp.where(col_place == 0, 4, 3)
     last_row = jnp.where(col_place == COLS - 1, 19, 20)
-    inside = jnp.logical_and(row >= first_row, row <= last_row)
-    beyond = [jnp.concatenate([ref[0:24, :], ref[24:48, :]], axis=1) for ref in (before, after)]
-    values = [beyond[0]] + [wide[q] for q in range(PLANES)] + [beyond[1]]
-    rest = []
+    return jnp.logical_and(row >= first_row, row <= last_row)
+
+
+def inner_kernel(place, wide, field, rest, sources):
+    lane = lane_index((24, GRID))
+    inside = inside_rows(place[2])
     for q in range(PLANES):
         sources[q] = jnp.zeros((24, GRID), F32)
         sources[q, 4:20, :] = field[q]
         sources[q, 3:4, :] = wide[q, 1:2, :]
         sources[q, 20:21, :] = wide[q, 22:23, :]
-        centre = values[q + 1]
-        near = values[q] + values[q + 2] + beside_y(centre) + beside_z(centre, lane)
-        value = jnp.where(inside, 6.0 * centre - near - sources[q], 0.0)
-        rest.append(value)
-        residual[q] = value[4:20]
+        centre = wide[q]
+        near = beside_y(centre) + beside_z(centre, lane) + sources[q]
+        if q > 0:
+            near = near + wide[q - 1]
+        if q < PLANES - 1:
+            near = near + wide[q + 1]
+        rest[q] = jnp.where(inside, 6.0 * centre - near, 0.0)
+
+
+def stencil_kernel(place, rest, wide, before, after, ends, adjoint):
+    row_place = place[1]
+    lane = lane_index((24, GRID))
+    inside = inside_rows(place[2])
+    values = [rest[q] for q in range(PLANES)]
     outer = []
-    for ref, edge, some in ((before, 0, row_place > 0), (after, PLANES - 1, row_place < ROWS - 1)):
+    for n, ref, edge, some in ((0, before, 0, row_place > 0), (1, after, PLANES - 1, row_place < ROWS - 1)):
+        beyond = jnp.concatenate([ref[0:24, :], ref[24:48, :]], axis=1)
+        values[edge] = values[edge] - jnp.where(inside, beyond, 0.0)
+        ends[n] = values[edge][4:20]
         part = jnp.concatenate([ref[48:64, :], ref[64:80, :]], axis=1) - wide[edge, 4:20, :]
         outer.append(jnp.where(some, part, 0.0))
     for q in range(PLANES):
-        low = outer[0] if q == 0 else rest[q - 1][4:20]
-        high = outer[1] if q == PLANES - 1 else rest[q + 1][4:20]
-        near = (beside_y(rest[q]) + beside_z(rest[q], lane))[4:20]
-        value = 6.0 * rest[q][4:20] - (low + high + near)
+        low = outer[0] if q == 0 else values[q - 1][4:20]
+        high = outer[1] if q == PLANES - 1 else values[q + 1][4:20]
+        near = (beside_y(values[q]) + beside_z(values[q], lane))[4:20]
+        value = 6.0 * values[q][4:20] - (low + high + near)
         adjoint[2 * q] = value
         adjoint[2 * q + 1] = value
 
 
-def call(kernel, operands, scalars, outputs, scratch, flops=0, far=0):
+def residual_kernel(rest, ends, out):
+    for q in range(PLANES):
+        out[q] = ends[0] if q == 0 else ends[1] if q == PLANES - 1 else rest[q, 4:20, :]
+
+
+def call(kernel, operands, scalars, outputs, scratch, flops=0, far=0, far_out=False):
     many = isinstance(outputs, list)
     vmem = pl.BlockSpec(memory_space=pltpu.VMEM)
     smem = pl.BlockSpec(memory_space=pltpu.SMEM)
     hbm = pl.BlockSpec(memory_space=pltpu.HBM)
+    place_out = hbm if far_out else vmem
+    operands = list(operands)
+    for n in range(len(operands) - far, len(operands)):
+        operands[n] = pltpu.with_memory_space_constraint(operands[n], pltpu.HBM)
     cost = pl.CostEstimate(flops=flops, bytes_accessed=4 << 20, transcendentals=flops // 16)
     return pl.pallas_call(
         kernel,
         in_specs=[smem] * len(scalars) + [vmem] * (len(operands) - far) + [hbm] * far,
-        out_specs=[vmem] * len(outputs) if many else vmem,
+        out_specs=[place_out] * len(outputs) if many else place_out,
         out_shape=outputs,
         scratch_shapes=scratch,
         compiler_params=pltpu.CompilerParams(vmem_limit_bytes=VMEM_LIMIT),
@@ -414,7 +451,7 @@
         mix_kernel, (lifted, spectral_weight, x_table), (), [shape(512, 128), shape(2, 64, 128)], [pair, pair]
     )
     mixed = exchange(mixed, everywhere)
-    message, slope = call(
+    message, preact = call(
         inverse_kernel,
         (mixed, local, plane, z_inverse, y_table),
         (place, params),
@@ -428,6 +465,9 @@
         ],
     )
     message = exchange(message, COL)
+    slope = call(
+        slope_kernel, (preact,), (place, params), shape(HALF, GRID, GRID), [], flops=1 << 25
+    )
     wide, lower, upper = call(
         edge_kernel, (message, field), (), [shape(PLANES, 24, GRID), shape(80, 128), shape(80, 128)], []
     )
@@ -435,13 +475,22 @@
     backward = [(target, source) for source, target in forward]
     before = lax.ppermute(upper, ROW, forward)
     after = lax.ppermute(lower, ROW, backward)
-    residual, adjoint = call(
+    rest = call(
+        inner_kernel,
+        (wide, field),
+        (place,),
+        shape(PLANES, 24, GRID),
+        [pltpu.VMEM((PLANES, 24, GRID), F32)],
+        flops=1 << 22,
+    )
+    ends, adjoint = call(
         stencil_kernel,
-        (wide, before, after, field),
+        (rest, wide, before, after),
         (place,),
-        [shape(PLANES, COLS, GRID), shape(2 * PLANES, COLS, GRID)],
-        [pltpu.VMEM((PLANES, 24, GRID), F32)],
-    )
+        [shape(2, COLS, GRID), shape(2 * PLANES, COLS, GRID)],
+        [],
+    )
+    residual = call(residual_kernel, (rest, ends), (), shape(PLANES, COLS, GRID), [], flops=1 << 22)
     adjoint = exchange(adjoint, COL).reshape(GRID, GRID)
     grads = call(grad_kernel, (adjoint, slope, z_forward, y_table), (), shape(512, 128), plane_scratch)
     grads = exchange(grads, everywhere)
@@ -450,7 +499,8 @@
         (grads, spectra, x_table),
         (place,),
         jax.ShapeDtypeStruct(spectral_weight.shape, BF16),
-        [pair, pair],
+        [pair, pair, pltpu.VMEM(spectral_weight.shape, BF16), pltpu.SemaphoreType.DMA((8,))],
+        far_out=True,
     )
     return residual[None], spectral_grad
 

time: 157 us -> 160 us (1.019)
  blocking collectives: 86.4 us -> 44.9 us
  waiting for transfers between devices: 18.8 us -> 37.6 us
  starting transfers between devices: 23.1 us -> 41.4 us
  Pallas kernels: 22.9 us -> 27.1 us
  local copies, waits for them, and re-layouts: 4.28 us -> 7.35 us
    all_to_all x4 -> x2, blocking collectives: 86.4 us -> 44.9 us  [exchange(): return lax.all_to_all(value, axes, split_axis=0, concat_axis=0, tiled=True)]
    all_to_all x2 -> x4, waiting for transfers between devices: 14.5 us -> 34 us  [exchange(): return lax.all_to_all(value, axes, split_axis=0, concat_axis=0, tiled=True)]
    all_to_all x2 -> x4, starting transfers between devices: 18.6 us -> 36.9 us  [exchange(): return lax.all_to_all(value, axes, split_axis=0, concat_axis=0, tiled=True)]
    pallas_call x9 -> x12, Pallas kernels: 22.9 us -> 27.1 us  [call(): pl.pallas_call(kernel, in_specs=[smem] * len(scalars) + [vmem] * (len(ope...]
    unnamed x18 -> x20, local copies, waits for them, and re-layouts: 2.78 us -> 5.85 us
  transfers between devices with their start and end apart: 4 -> 6, of which waited for: 3 -> 5; matrix products, arithmetic and copies ran while one was open for 1% -> 1% of each run, Pallas kernels for 5% -> 7%
where the time goes in v2:
time: 160 us; the launch traced here: 159 us
  blocking collectives  44.9 us (28%)
  starting transfers between devices  41.4 us (26%)
  waiting for transfers between devices  37.6 us (24%)
  Pallas kernels  27.1 us (17%)
  local copies, waits for them, and re-layouts  7.35 us (5%)
    all_to_all x2, blocking collectives, exchange(): return lax.all_to_all(value, axes, split_axis=0, concat_axis=0, tiled=True)  44.9 us
    all_to_all x4, starting transfers between devices, exchange(): return lax.all_to_all(value, axes, split_axis=0, concat_axis=0, tiled=True)  36.9 us
    all_to_all x4, waiting for transfers between devices, exchange(): return lax.all_to_all(value, axes, split_axis=0, concat_axis=0, tiled=True)  34 us
    pallas_call x12, Pallas kernels, call(): pl.pallas_call(kernel, in_specs=[smem] * len(scalars) + [vmem] * (len(ope...  27.1 us
    unnamed x20, local copies, waits for them, and re-layouts  5.85 us
    ppermute x1, waiting for transfers between devices, shards(): after = lax.ppermute(lower, ROW, backward)  3.61 us
    ppermute x1, starting transfers between devices, shards(): before = lax.ppermute(upper, ROW, forward)  3.28 us
  transfers between devices with their start and end apart: 6, of which 5 were waited for; matrix products, arithmetic and copies ran while one was open for 1% of the time, Pallas kernels for 7%

profile of v2, /device:TPU:1, one launch (start us, length us, event | category | flops | bytes accessed | tf_op | source)
XLA Modules:
  0.0 159.4 jit_solution(14511434821959821889)
XLA Ops:
  0.7 1.8 %shard_map.122 = f32[8,2,16,256]{3,2,1,0:T(8,128)} custom-call(f32[8,16,256]{2,1,0:T(8,128)} %bitcast.27), custom_call_target="tpu_custom_call" | custom-call | tf_op jit(solution)/shard_map/pallas_call | solution.py:396
  2.4 10.2 %all-to-all-start = ((f32[16,16,256]{2,1,0:T(8,128)}), f32[16,16,256]{2,1,0:T(8,128)S(1)}, u32[]{:S(2)}, u32[]{:S(2)}) async-start(f32[16,16,256]{2,1,0:T(8,128)} %bitcast.8), calls=%async_computation | async-start | bytes 524288 | tf_op jit(solution)/shard_map/all_to_all | solution.py:408
  12.6 1.5 concatenate.3.params
  14.2 5.7 %all-to-all-done = f32[16,16,256]{2,1,0:T(8,128)S(1)} async-done(((f32[16,16,256]{2,1,0:T(8,128)}), f32[16,16,256]{2,1,0:T(8,128)S(1)}, u32[]{:S(2)}, u32[]{:S(2)}) %all-to-all-start) | async-done | bytes 262176 | tf_op jit(solution)/shard_map/all_to_all | solution.py:408
  19.9 4.1 %shard_map.123 = f32[512,128]{1,0:T(8,128)S(1)} custom-call(s32[3]{0:T(128)S(1)} %pad_add_fusion.place, f32[20,16]{1,0:T(8,128)S(1)} %concatenate.3.params, f32[256,256]{1,0:T(8,128)S(1)} %bitcast.24, bf16[256,256]{1,0:T(8,128)(2,1)} %constant.34.clone.z_far.z_table, bf16[256,512]{1,0:T(8,128)(2,1)} %constant.35.clone.y_far.y_table), custom_call_target="tpu_custom_call" | custom-call | tf_op jit(solution)/shard_map/pallas_call | solution.py:396
  24.0 33.2 %all_to_all.48 = f32[512,1,128]{2,1,0:T(1,128)S(1)} all-to-all(f32[512,1,128]{2,1,0:T(1,128)S(1)} %bitcast.33), channel_id=1, replica_groups=mesh['y'=8,'zh'=4,'zl'=2,'x'=4,'core'=2] {'zl','x','core','y','zh'}, dimensions={0} | all-to-all | bytes 524288 | tf_op jit(solution)/shard_map/all_to_all | solution.py:408
  57.2 1.7 %shard_map.124 = (f32[512,128]{1,0:T(8,128)}, f32[2,64,128]{2,1,0:T(8,128)S(1)}) custom-call(f32[512,128]{1,0:T(8,128)S(1)} %bitcast.32, bf16[2,4,16,16,128]{4,3,2,1,0:T(8,128)(2,1)S(1)} %copy-done.8, bf16[256,256]{1,0:T(8,128)(2,1)S(1)} %copy-done.6), custom_call_target="tpu_custom_call" | custom-call | tf_op jit(solution)/shard_map/pallas_call | solution.py:396
  58.9 8.3 %all-to-all-start.2 = ((f32[512,1,128]{2,1,0:T(1,128)}), f32[512,1,128]{2,1,0:T(1,128)S(1)}, u32[]{:S(2)}, u32[]{:S(2)}) async-start(f32[512,1,128]{2,1,0:T(1,128)} %bitcast.14), calls=%async_computation.2 | async-start | bytes 524288 | tf_op jit(solution)/shard_map/all_to_all | solution.py:408
  67.2 7.8 %shard_map.125.local = f32[8,256,256]{2,1,0:T(8,128)S(1)} custom-call(s32[3]{0:T(128)S(1)} %pad_add_fusion.place, f32[20,16]{1,0:T(8,128)S(1)} %concatenate.3.params, f32[256,256]{1,0:T(8,128)S(1)} %bitcast.25), custom_call_target="tpu_custom_call" | custom-call | flops 134217728 | bytes 4194304 | tf_op jit(solution)/shard_map/pallas_call | solution.py:396
  76.4 7.9 %all-to-all-done.2 = f32[512,1,128]{2,1,0:T(1,128)S(1)} async-done(((f32[512,1,128]{2,1,0:T(1,128)}), f32[512,1,128]{2,1,0:T(1,128)S(1)}, u32[]{:S(2)}, u32[]{:S(2)}) %all-to-all-start.2) | async-done | bytes 262176 | tf_op jit(solution)/shard_map/all_to_all | solution.py:408
  84.3 1.6 copy-done.4
  85.9 2.8 %shard_map.126 = (f32[16,48,128]{2,1,0:T(8,128)S(1)}, f32[8,256,256]{2,1,0:T(8,128)S(1)}) custom-call(s32[3]{0:T(128)S(1)} %pad_add_fusion.place, f32[20,16]{1,0:T(8,128)S(1)} %concatenate.3.params, f32[512,128]{1,0:T(8,128)S(1)} %bitcast.34, f32[8,256,256]{2,1,0:T(8,128)S(1)} %copy-done.4, f32[256,256]{1,0:T(8,128)S(1)} %bitcast.26, ...), custom_call_target="tpu_custom_call" | custom-call | tf_op jit(solution)/shard_map/pallas_call | solution.py:396
  90.1 11.7 %all_to_all.49.received = f32[16,48,128]{2,1,0:T(8,128)S(1)} all-to-all(f32[16,48,128]{2,1,0:T(8,128)S(1)} %get-tuple-element.12), channel_id=1, replica_groups=mesh['y'=8,'zh'=4,'zl'=2,'x'=4,'core'=2] {'zl','x','core'}, dimensions={0} | all-to-all | bytes 786432 | tf_op jit(solution)/shard_map/all_to_all | solution.py:408
  101.8 3.3 %collective-permute-start = (f32[80,128]{1,0:T(8,128)S(1)}, f32[80,128]{1,0:T(8,128)S(1)}, u32[]{:S(2)}, u32[]{:S(2)}) collective-permute-start(f32[80,128]{1,0:T(8,128)S(1)} %get-tuple-element.14), channel_id=1, source_target_pairs={{0,16},{16,32},{32,48},{48,64},{64,80},{80,96},{96,112},{112,128},... | collective-permute-start | bytes 122888 | tf_op jit(solution)/shard_map/ppermute | solution.py:476
  107.2 3.6 %collective-permute-done.1.after = f32[80,128]{1,0:T(8,128)S(1)} collective-permute-done((f32[80,128]{1,0:T(8,128)S(1)}, f32[80,128]{1,0:T(8,128)S(1)}, u32[]{:S(2)}, u32[]{:S(2)}) %collective-permute-start.1) | collective-permute-done | bytes 40992 | tf_op jit(solution)/shard_map/ppermute | solution.py:477
  110.8 1.4 shard_map.129
  112.2 6.4 %all-to-all-start.4 = ((f32[16,16,256]{2,1,0:T(8,128)}), f32[16,16,256]{2,1,0:T(8,128)S(1)}, u32[]{:S(2)}, u32[]{:S(2)}) async-start(f32[16,16,256]{2,1,0:T(8,128)} %get-tuple-element.17), calls=%async_computation.4 | async-start | bytes 524288 | tf_op jit(solution)/shard_map/all_to_all | solution.py:408
  118.6 1.6 copy-done.2
  120.1 1.8 %shard_map.131.slope = f32[8,256,256]{2,1,0:T(8,128)S(1)} custom-call(s32[3]{0:T(128)S(1)} %pad_add_fusion.place, f32[20,16]{1,0:T(8,128)S(1)} %concatenate.3.params, f32[8,256,256]{2,1,0:T(8,128)S(1)} %copy-done.2), custom_call_target="tpu_custom_call" | custom-call | flops 33554432 | bytes 4194304 | tf_op jit(solution)/shard_map/pallas_call | solution.py:396
  122.0 3.8 %all-to-all-done.4 = f32[16,16,256]{2,1,0:T(8,128)S(1)} async-done(((f32[16,16,256]{2,1,0:T(8,128)}), f32[16,16,256]{2,1,0:T(8,128)S(1)}, u32[]{:S(2)}, u32[]{:S(2)}) %all-to-all-start.4) | async-done | bytes 262176 | tf_op jit(solution)/shard_map/all_to_all | solution.py:408
  125.8 2.3 %shard_map.132 = f32[512,128]{1,0:T(8,128)} custom-call(f32[256,256]{1,0:T(8,128)S(1)} %bitcast.31, f32[8,256,256]{2,1,0:T(8,128)S(1)} %shard_map.131.slope, bf16[256,256]{1,0:T(8,128)(2,1)S(1)} %copy-done.7, bf16[256,512]{1,0:T(8,128)(2,1)S(1)} %copy-done), custom_call_target="tpu_custom_call" | custom-call | tf_op jit(solution)/shard_map/pallas_call | solution.py:396
  128.1 12.0 %all-to-all-start.5 = ((f32[512,1,128]{2,1,0:T(1,128)}), f32[512,1,128]{2,1,0:T(1,128)S(1)}, u32[]{:S(2)}, u32[]{:S(2)}) async-start(f32[512,1,128]{2,1,0:T(1,128)} %bitcast.19), calls=%async_computation.5 | async-start | bytes 524288 | tf_op jit(solution)/shard_map/all_to_all | solution.py:408
  140.7 16.6 %all-to-all-done.5 = f32[512,1,128]{2,1,0:T(1,128)S(1)} async-done(((f32[512,1,128]{2,1,0:T(1,128)}), f32[512,1,128]{2,1,0:T(1,128)S(1)}, u32[]{:S(2)}, u32[]{:S(2)}) %all-to-all-start.5) | async-done | bytes 262176 | tf_op jit(solution)/shard_map/all_to_all | solution.py:408
  157.3 1.9 %shard_map.133 = bf16[2,4,16,16,128]{4,3,2,1,0:T(8,128)(2,1)} custom-call(s32[3]{0:T(128)S(1)} %pad_add_fusion.place, f32[512,128]{1,0:T(8,128)S(1)} %bitcast.30, f32[2,64,128]{2,1,0:T(8,128)S(1)} %get-tuple-element.19.spectra_in, bf16[256,256]{1,0:T(8,128)(2,1)S(1)} %copy-done.6), custom_call_target="tpu_custom_call" | custom-call | tf_op jit(solution)/shard_map/pallas_call | solution.py:396
  (24 shorter events, 5.5 us)
Async XLA Ops:
  0.6 56.5 %copy-start.6 = (bf16[256,256]{1,0:T(8,128)(2,1)S(1)}, bf16[256,256]{1,0:T(8,128)(2,1)}, u32[]{:S(2)}) copy-start(bf16[256,256]{1,0:T(8,128)(2,1)} %constant.36.clone.x_table) | copy-start | bytes 393220
  0.6 56.5 %copy-start.8 = (bf16[2,4,16,16,128]{4,3,2,1,0:T(8,128)(2,1)S(1)}, bf16[2,4,16,16,128]{4,3,2,1,0:T(8,128)(2,1)}, u32[]{:S(2)}) copy-start(bf16[2,4,16,16,128]{4,3,2,1,0:T(8,128)(2,1)} %weight.1) | copy-start | bytes 1572868
  2.4 17.5 %all-to-all-start = ((f32[16,16,256]{2,1,0:T(8,128)}), f32[16,16,256]{2,1,0:T(8,128)S(1)}, u32[]{:S(2)}, u32[]{:S(2)}) async-start(f32[16,16,256]{2,1,0:T(8,128)} %bitcast.8), calls=%async_computation | async-start | bytes 524288 | tf_op jit(solution)/shard_map/all_to_all | solution.py:408
  58.9 25.5 %all-to-all-start.2 = ((f32[512,1,128]{2,1,0:T(1,128)}), f32[512,1,128]{2,1,0:T(1,128)S(1)}, u32[]{:S(2)}, u32[]{:S(2)}) async-start(f32[512,1,128]{2,1,0:T(1,128)} %bitcast.14), calls=%async_computation.2 | async-start | bytes 524288 | tf_op jit(solution)/shard_map/all_to_all | solution.py:408
  67.2 17.1 %copy-start = (bf16[256,512]{1,0:T(8,128)(2,1)S(1)}, bf16[256,512]{1,0:T(8,128)(2,1)}, u32[]{:S(2)}) copy-start(bf16[256,512]{1,0:T(8,128)(2,1)} %constant.35.clone.y_far.y_table) | copy-start | bytes 786436
  67.2 17.1 %copy-start.9 = (bf16[512,256]{1,0:T(8,128)(2,1)S(1)}, bf16[512,256]{1,0:T(8,128)(2,1)}, u32[]{:S(2)}) copy-start(bf16[512,256]{1,0:T(8,128)(2,1)} %constant.37.clone.z_table) | copy-start | bytes 786436
  67.2 34.5 %copy-start.5 = (f32[1,8,16,256]{3,2,1,0:T(8,128)S(1)}, f32[1,8,16,256]{3,2,1,0:T(8,128)}, u32[]{:S(2)}) copy-start(f32[1,8,16,256]{3,2,1,0:T(8,128)} %param.11) | copy-start | bytes 393220
  75.1 1.3 copy-start.3
  84.3 1.6 copy-start.4
  88.7 1.3 copy-start.1
  101.8 5.3 %collective-permute-start = (f32[80,128]{1,0:T(8,128)S(1)}, f32[80,128]{1,0:T(8,128)S(1)}, u32[]{:S(2)}, u32[]{:S(2)}) collective-permute-start(f32[80,128]{1,0:T(8,128)S(1)} %get-tuple-element.14), channel_id=1, source_target_pairs={{0,16},{16,32},{32,48},{48,64},{64,80},{80,96},{96,112},{112,128},... | collective-permute-start | bytes 122888 | tf_op jit(solution)/shard_map/ppermute | solution.py:476
  105.1 5.6 %collective-permute-start.1 = (f32[80,128]{1,0:T(8,128)S(1)}, f32[80,128]{1,0:T(8,128)S(1)}, u32[]{:S(2)}, u32[]{:S(2)}) collective-permute-start(f32[80,128]{1,0:T(8,128)S(1)} %get-tuple-element.15), channel_id=1, source_target_pairs={{16,0},{32,16},{48,32},{64,48},{80,64},{96,80},{112,96},{128,112},... | collective-permute-start | bytes 122888 | tf_op jit(solution)/shard_map/ppermute | solution.py:477
  112.2 13.6 %all-to-all-start.4 = ((f32[16,16,256]{2,1,0:T(8,128)}), f32[16,16,256]{2,1,0:T(8,128)S(1)}, u32[]{:S(2)}, u32[]{:S(2)}) async-start(f32[16,16,256]{2,1,0:T(8,128)} %get-tuple-element.17), calls=%async_computation.4 | async-start | bytes 524288 | tf_op jit(solution)/shard_map/all_to_all | solution.py:408
  118.6 1.6 copy-start.2
  120.1 5.7 %copy-start.7 = (bf16[256,256]{1,0:T(8,128)(2,1)S(1)}, bf16[256,256]{1,0:T(8,128)(2,1)}, u32[]{:S(2)}) copy-start(bf16[256,256]{1,0:T(8,128)(2,1)} %constant.34.clone.z_far.z_table) | copy-start | bytes 393220
  128.1 29.2 %all-to-all-start.5 = ((f32[512,1,128]{2,1,0:T(1,128)}), f32[512,1,128]{2,1,0:T(1,128)S(1)}, u32[]{:S(2)}, u32[]{:S(2)}) async-start(f32[512,1,128]{2,1,0:T(1,128)} %bitcast.19), calls=%async_computation.5 | async-start | bytes 524288 | tf_op jit(solution)/shard_map/all_to_all | solution.py:408

commit v3 on v2

--- a/solution.py
+++ b/solution.py
@@ -76,11 +76,12 @@
     return half + half * jnp.tanh(inner)
 
 
-def gelu_slope(value):
+def gelu_both(value):
     square = value * value
     bent = jnp.tanh(value * (ROOT + (ROOT * CUBE) * square))
     slope = ROOT + (3.0 * ROOT * CUBE) * square
-    return 0.5 + 0.5 * bent + (0.5 * value) * ((1.0 - bent * bent) * slope)
+    cdf = 0.5 + 0.5 * bent
+    return value * cdf, cdf + (0.5 * value) * ((1.0 - bent * bent) * slope)
 
 
 def bent_half(half):
@@ -100,16 +101,13 @@
     return pltpu.roll(value, MODES, 1)
 
 
-def plane_forward(fill, z_table, y_table, stage_high, stage_low, lines, out, ready=lambda n: None):
+def plane_forward(fill, z_table, y_table, stage_high, stage_low, lines, out):
     for channel in range(HALF):
         fill(channel, stage_high, stage_low)
-        if channel == 0:
-            ready(0)
         z = dot(z_table[...], stage_high[...], NN)
         z = z[:128] + z[128:] + dot(z_table[0:128, :], stage_low[...], NN)
         lines[:, channel, 0:GRID] = z[:MODES]
         lines[:, channel, GRID:] = z[MODES:]
-    ready(1)
     high, low = split(lines[...].reshape(MODES * HALF, 2 * GRID))
     spectrum = dot(y_table[...], high, NT)
     spectrum = spectrum[:128] + spectrum[128:] + dot(y_table[0:128, :], low, NT)
@@ -126,11 +124,7 @@
             out[column * 32 : column * 32 + 32, :] = total
 
 
-def lift_kernel(place, params, plane, z_far, y_far, out, turned, high, low, lines, z_table, y_table, sems):
-    z_copy = pltpu.make_async_copy(z_far, z_table, sems.at[0])
-    y_copy = pltpu.make_async_copy(y_far, y_table, sems.at[1])
-    z_copy.start()
-    y_copy.start()
+def lift_kernel(place, params, plane, z_table, y_table, out, turned, high, low, lines):
     core = place[0]
     turned[...] = plane[...].T
 
@@ -140,18 +134,28 @@
             rows = slice(32 * t, 32 * t + 32)
             stage_high[rows, :], stage_low[rows, :] = split(lift(turned[rows, :], gain, offset))
 
-    plane_forward(fill, z_table, y_table, high, low, lines, out, lambda n: (z_copy, y_copy)[n].wait())
-
-
-def grad_kernel(adjoint, slope, z_table, y_table, out, turned, high, low, lines):
+    plane_forward(fill, z_table, y_table, high, low, lines, out)
+
+
+def grad_kernel(adjoint, z_table, y_table, *refs):
+    slope = refs[:HALF]
+    out, turned, high, low, lines = refs[HALF:]
     turned[...] = adjoint[...].T
 
     def fill(channel, stage_high, stage_low):
         for t in range(8):
             rows = slice(32 * t, 32 * t + 32)
-            stage_high[rows, :], stage_low[rows, :] = split(turned[rows, :] * slope[channel, rows, :])
+            stage_high[rows, :], stage_low[rows, :] = split(turned[rows, :] * slope[channel][rows, :])
 
     plane_forward(fill, z_table, y_table, high, low, lines, out)
+
+
+def ready_kernel(z_far, y_far, z_table, y_table, sems):
+    copies = [pltpu.make_async_copy(z_far, z_table, sems.at[0]), pltpu.make_async_copy(y_far, y_table, sems.at[1])]
+    for copy in copies:
+        copy.start()
+    for copy in copies:
+        copy.wait()
 
 
 def spread_kernel(field, out, sems):
@@ -162,27 +166,33 @@
         copy.wait()
 
 
-def local_kernel(place, params, plane, out, turned):
+def local_kernel(place, params, plane, margin, *refs):
+    out, turned = refs[:HALF], refs[HALF]
     first = place[0] * HALF
+    keep = jnp.where(place[0] == 0, 1.0, 0.0).astype(F32)
     turned[...] = plane[...].T
+    margin[...] = jnp.zeros(margin.shape, F32)
+    for c in range(1, COLS):
+        margin[c : c + 1, :] = plane[16 * c - 1 : 16 * c, :] * keep
+        margin[COLS + c - 1 : COLS + c, :] = plane[16 * c : 16 * c + 1, :] * keep
 
     def step(t, carry):
-        rows = pl.ds(pl.multiple_of(t * 8, 8), 8)
+        rows = pl.ds(pl.multiple_of(t * 16, 16), 16)
         field = turned[rows, :]
-        sums = [jnp.full((8, GRID), params[2, first + o], F32) for o in range(HALF)]
+        sums = [jnp.full((16, GRID), params[2, first + o], F32) for o in range(HALF)]
         for i in range(WIDTH):
             lifted = lift(field, 0.5 * params[0, i], 0.5 * params[1, i])
             sums = [sums[o] + params[4 + i, first + o] * lifted for o in range(HALF)]
         for o in range(HALF):
-            out[o, rows, :] = sums[o]
+            out[o][rows, :] = sums[o]
         return carry
 
-    lax.fori_loop(0, GRID // 8, step, 0)
-
-
-def inverse_kernel(
-    place, params, received, local, plane, z_table, y_table, out, preact, grid, lines, spectral, total, padded
-):
+    lax.fori_loop(0, GRID // 16, step, 0)
+
+
+def inverse_kernel(place, params, received, margin, z_table, y_table, *refs):
+    local, out, slope = refs[:HALF], refs[HALF], refs[HALF + 1 : 2 * HALF + 1]
+    grid, lines, spectral, total, padded = refs[2 * HALF + 1 :]
     core = place[0]
     lane = lane_index((ROWS, 128)) // 32
     for tile in range(4):
@@ -204,33 +214,23 @@
         read = params[3, core * HALF + o]
         for t in range(8):
             rows = slice(32 * t, 32 * t + 32)
-            value = spectral[rows, :] + local[o, rows, :]
-            preact[o, rows, :] = value
+            value = spectral[rows, :] + local[o][rows, :]
+            value, derivative = gelu_both(value)
+            slope[o][rows, :] = read * derivative
             if o == 0:
-                total[rows, :] = read * gelu(value)
+                total[rows, :] = read * value
             else:
-                total[rows, :] += read * gelu(value)
+                total[rows, :] += read * value
     padded[0:8, :] = jnp.zeros((8, GRID), F32)
     padded[256:264, :] = jnp.zeros((8, GRID), F32)
     padded[4:260, :] = total[...].T
-    keep = jnp.where(core == 0, 1.0, 0.0).astype(F32)
-    blank = jnp.zeros((1, GRID), F32)
     row = lax.broadcasted_iota(jnp.int32, (24, GRID), 0)
     for c in range(COLS):
-        before = plane[16 * c - 1 : 16 * c, :] * keep if c > 0 else blank
-        after = plane[16 * c + 16 : 16 * c + 17, :] * keep if c < COLS - 1 else blank
+        before, after = margin[c : c + 1, :], margin[COLS + c : COLS + c + 1, :]
         block = padded[16 * c : 16 * c + 24, :]
         block = jnp.where(row == 1, before, jnp.where(row == 22, after, block))
         out[c, 0:24, :] = block[:, 0:128]
         out[c, 24:48, :] = block[:, 128:256]
-
-
-def slope_kernel(place, params, preact, out):
-    for o in range(HALF):
-        read = params[3, place[0] * HALF + o]
-        for t in range(8):
-            rows = slice(32 * t, 32 * t + 32)
-            out[o, rows, :] = read * gelu_slope(preact[o, rows, :])
 
 
 def gather_spectra(received, x_table, sign):
@@ -383,12 +383,12 @@
         out[q] = ends[0] if q == 0 else ends[1] if q == PLANES - 1 else rest[q, 4:20, :]
 
 
-def call(kernel, operands, scalars, outputs, scratch, flops=0, far=0, far_out=False):
+def call(kernel, operands, scalars, outputs, scratch, flops=0, far=0, far_out=()):
     many = isinstance(outputs, list)
     vmem = pl.BlockSpec(memory_space=pltpu.VMEM)
     smem = pl.BlockSpec(memory_space=pltpu.SMEM)
     hbm = pl.BlockSpec(memory_space=pltpu.HBM)
-    place_out = hbm if far_out else vmem
+    out_specs = [hbm if n in far_out else vmem for n in range(len(outputs) if many else 1)]
     operands = list(operands)
     for n in range(len(operands) - far, len(operands)):
         operands[n] = pltpu.with_memory_space_constraint(operands[n], pltpu.HBM)
@@ -396,7 +396,7 @@
     return pl.pallas_call(
         kernel,
         in_specs=[smem] * len(scalars) + [vmem] * (len(operands) - far) + [hbm] * far,
-        out_specs=[place_out] * len(outputs) if many else place_out,
+        out_specs=out_specs if many else out_specs[0],
         out_shape=outputs,
         scratch_shapes=scratch,
         compiler_params=pltpu.CompilerParams(vmem_limit_bytes=VMEM_LIMIT),
@@ -419,9 +419,21 @@
     everywhere = COL + ROW
     field = right_side[0]
     copies = pltpu.SemaphoreType.DMA((2,))
+    fields = [shape(GRID, GRID)] * HALF
 
     spread = call(spread_kernel, (field,), (), shape(PLANES, 2, COLS, GRID), [copies], far=1)
-    plane = exchange(spread.reshape(COLS, COLS, GRID), COL).reshape(GRID, GRID)
+    plane = exchange(spread.reshape(COLS, COLS, GRID), COL)
+    near = call(
+        ready_kernel,
+        (z_forward, y_table),
+        (),
+        [jax.ShapeDtypeStruct(z_forward.shape, BF16), jax.ShapeDtypeStruct(y_table.shape, BF16)],
+        [copies],
+        flops=1 << 24,
+        far=2,
+    )
+    plane, near = lax.optimization_barrier((plane, near))
+    plane = plane.reshape(GRID, GRID)
     line_scratch = pltpu.VMEM((MODES, HALF, 2 * GRID), F32)
     plane_scratch = [
         pltpu.VMEM((GRID, GRID), F32),
@@ -429,20 +441,13 @@
         pltpu.VMEM((GRID, GRID), BF16),
         line_scratch,
     ]
-    lifted = call(
-        lift_kernel,
-        (plane, z_forward, y_table),
-        (place, params),
-        shape(512, 128),
-        plane_scratch + [pltpu.VMEM(z_forward.shape, BF16), pltpu.VMEM(y_table.shape, BF16), copies],
-        far=2,
-    )
+    lifted = call(lift_kernel, (plane, *near), (place, params), shape(512, 128), plane_scratch)
     lifted = exchange(lifted, everywhere)
-    local = call(
+    margin, *local = call(
         local_kernel,
         (plane,),
         (place, params),
-        shape(HALF, GRID, GRID),
+        [shape(2 * COLS, GRID)] + fields,
         [pltpu.VMEM((GRID, GRID), F32)],
         flops=1 << 27,
     )
@@ -451,11 +456,11 @@
         mix_kernel, (lifted, spectral_weight, x_table), (), [shape(512, 128), shape(2, 64, 128)], [pair, pair]
     )
     mixed = exchange(mixed, everywhere)
-    message, preact = call(
+    message, *slope = call(
         inverse_kernel,
-        (mixed, local, plane, z_inverse, y_table),
+        (mixed, margin, z_inverse, y_table, *local),
         (place, params),
-        [shape(COLS, 48, 128), shape(HALF, GRID, GRID)],
+        [shape(COLS, 48, 128)] + fields,
         [
             pltpu.VMEM((128, 512), F32),
             line_scratch,
@@ -465,9 +470,6 @@
         ],
     )
     message = exchange(message, COL)
-    slope = call(
-        slope_kernel, (preact,), (place, params), shape(HALF, GRID, GRID), [], flops=1 << 25
-    )
     wide, lower, upper = call(
         edge_kernel, (message, field), (), [shape(PLANES, 24, GRID), shape(80, 128), shape(80, 128)], []
     )
@@ -492,7 +494,7 @@
     )
     residual = call(residual_kernel, (rest, ends), (), shape(PLANES, COLS, GRID), [], flops=1 << 22)
     adjoint = exchange(adjoint, COL).reshape(GRID, GRID)
-    grads = call(grad_kernel, (adjoint, slope, z_forward, y_table), (), shape(512, 128), plane_scratch)
+    grads = call(grad_kernel, (adjoint, z_forward, y_table, *slope), (), shape(512, 128), plane_scratch)
     grads = exchange(grads, everywhere)
     spectral_grad = call(
         outer_kernel,
@@ -500,7 +502,7 @@
         (place,),
         jax.ShapeDtypeStruct(spectral_weight.shape, BF16),
         [pair, pair, pltpu.VMEM(spectral_weight.shape, BF16), pltpu.SemaphoreType.DMA((8,))],
-        far_out=True,
+        far_out=(0,),
     )
     return residual[None], spectral_grad
 

time: 160 us -> 155 us (0.969)
  blocking collectives: 44.9 us -> 57.8 us
  starting transfers between devices: 41.4 us -> 34.8 us
  local copies, waits for them, and re-layouts: 7.35 us -> 0.85 us
  Pallas kernels: 27.1 us -> 23.7 us
    all_to_all x2 -> x3, blocking collectives: 44.9 us -> 57.8 us  [exchange(): return lax.all_to_all(value, axes, split_axis=0, concat_axis=0, tiled=True)]
    all_to_all x4 -> x3, starting transfers between devices: 36.9 us -> 30.2 us  [exchange(): return lax.all_to_all(value, axes, split_axis=0, concat_axis=0, tiled=True)]
    unnamed x20 -> x22, local copies, waits for them, and re-layouts: 5.85 us -> 0.71 us
    pallas_call x12, Pallas kernels: 27.1 us -> 23.7 us  [call(): pl.pallas_call(kernel, in_specs=[smem] * len(scalars) + [vmem] * (len(ope...]
    all_to_all x4 -> x3, waiting for transfers between devices: 34 us -> 32.8 us  [exchange(): return lax.all_to_all(value, axes, split_axis=0, concat_axis=0, tiled=True)]
  transfers between devices with their start and end apart: 6 -> 5, of which waited for: 5 -> 4; matrix products, arithmetic and copies ran while one was open for 1% -> 0% of each run, Pallas kernels for 7% -> 5%
where the time goes in v3:
time: 155 us
  blocking collectives  57.8 us (37%)
  waiting for transfers between devices  36.4 us (23%)
  starting transfers between devices  34.8 us (22%)
  Pallas kernels  23.7 us (15%)
    all_to_all x3, blocking collectives, exchange(): return lax.all_to_all(value, axes, split_axis=0, concat_axis=0, tiled=True)  57.8 us
    all_to_all x3, waiting for transfers between devices, exchange(): return lax.all_to_all(value, axes, split_axis=0, concat_axis=0, tiled=True)  32.8 us
    all_to_all x3, starting transfers between devices, exchange(): return lax.all_to_all(value, axes, split_axis=0, concat_axis=0, tiled=True)  30.2 us
    pallas_call x12, Pallas kernels, call(): pl.pallas_call(kernel, in_specs=[smem] * len(scalars) + [vmem] * (len(ope...  23.7 us
    ppermute x1, waiting for transfers between devices, shards(): after = lax.ppermute(lower, ROW, backward)  3.61 us
    ppermute x1, starting transfers between devices, shards(): before = lax.ppermute(upper, ROW, forward)  3.28 us
  transfers between devices with their start and end apart: 5, of which 4 were waited for; matrix products, arithmetic and copies ran while one was open for 0% of the time, Pallas kernels for 5%

profile of v3, /device:TPU:1, one launch (start us, length us, event | category | flops | bytes accessed | tf_op | source)
XLA Modules:
  0.0 154.7 jit_solution(2367314622205388504)
XLA Ops:
  0.6 1.7 %shard_map.122 = f32[8,2,16,256]{3,2,1,0:T(8,128)} custom-call(f32[8,16,256]{2,1,0:T(8,128)} %bitcast.24), custom_call_target="tpu_custom_call" | custom-call | tf_op jit(solution)/shard_map/pallas_call | solution.py:396
  2.3 10.2 %all-to-all-start = ((f32[16,16,256]{2,1,0:T(8,128)}), f32[16,16,256]{2,1,0:T(8,128)S(1)}, u32[]{:S(2)}, u32[]{:S(2)}) async-start(f32[16,16,256]{2,1,0:T(8,128)} %bitcast.8), calls=%async_computation | async-start | bytes 524288 | tf_op jit(solution)/shard_map/all_to_all | solution.py:408
  12.6 0.6 copy-done.6
  13.4 1.0 shard_map.123
  14.5 5.2 %all-to-all-done = f32[16,16,256]{2,1,0:T(8,128)S(1)} async-done(((f32[16,16,256]{2,1,0:T(8,128)}), f32[16,16,256]{2,1,0:T(8,128)S(1)}, u32[]{:S(2)}, u32[]{:S(2)}) %all-to-all-start) | async-done | bytes 262176 | tf_op jit(solution)/shard_map/all_to_all | solution.py:408
  19.8 3.4 %shard_map.124 = f32[512,128]{1,0:T(8,128)S(1)} custom-call(s32[3]{0:T(128)S(1)} %pad_add_fusion.place, f32[20,16]{1,0:T(8,128)S(1)} %concatenate.3.params, f32[256,256]{1,0:T(8,128)S(1)} %bitcast.27, bf16[256,256]{1,0:T(8,128)(2,1)S(1)} %get-tuple-element.35.z_table, bf16[256,512]{1,0:T(8,128)(2,1)S(1)} %get-tuple-element.36.y_table), custom_call_target="tpu_custom_call" | custom-call | tf_op jit(solution)/shard_map/pallas_call | solution.py:396
  23.2 33.2 %all_to_all.48 = f32[512,1,128]{2,1,0:T(1,128)S(1)} all-to-all(f32[512,1,128]{2,1,0:T(1,128)S(1)} %bitcast.33), channel_id=1, replica_groups=mesh['y'=8,'zh'=4,'zl'=2,'x'=4,'core'=2] {'zl','x','core','y','zh'}, dimensions={0} | all-to-all | bytes 524288 | tf_op jit(solution)/shard_map/all_to_all | solution.py:408
  56.4 1.7 %shard_map.125 = (f32[512,128]{1,0:T(8,128)}, f32[2,64,128]{2,1,0:T(8,128)S(1)}) custom-call(f32[512,128]{1,0:T(8,128)S(1)} %bitcast.32, bf16[2,4,16,16,128]{4,3,2,1,0:T(8,128)(2,1)S(1)} %copy-done.3, bf16[256,256]{1,0:T(8,128)(2,1)S(1)} %copy-done.2), custom_call_target="tpu_custom_call" | custom-call | tf_op jit(solution)/shard_map/pallas_call | solution.py:396
  58.1 8.3 %all-to-all-start.2 = ((f32[512,1,128]{2,1,0:T(1,128)}), f32[512,1,128]{2,1,0:T(1,128)S(1)}, u32[]{:S(2)}, u32[]{:S(2)}) async-start(f32[512,1,128]{2,1,0:T(1,128)} %bitcast.14), calls=%async_computation.2 | async-start | bytes 524288 | tf_op jit(solution)/shard_map/all_to_all | solution.py:408
  66.5 6.1 %shard_map.126 = (f32[32,256]{1,0:T(8,128)S(1)}, f32[256,256]{1,0:T(8,128)S(1)}, f32[256,256]{1,0:T(8,128)S(1)}, f32[256,256]{1,0:T(8,128)S(1)}, f32[256,256]{1,...) custom-call(s32[3]{0:T(128)S(1)} %pad_add_fusion.place, ...), custom_call_target="tpu_custom_call" | custom-call | flops 134217728 | bytes 4194304 | tf_op jit(solution)/shard_map/pallas_call | solution.py:396
  72.6 11.0 %all-to-all-done.2 = f32[512,1,128]{2,1,0:T(1,128)S(1)} async-done(((f32[512,1,128]{2,1,0:T(1,128)}), f32[512,1,128]{2,1,0:T(1,128)S(1)}, u32[]{:S(2)}, u32[]{:S(2)}) %all-to-all-start.2) | async-done | bytes 262176 | tf_op jit(solution)/shard_map/all_to_all | solution.py:408
  83.6 3.4 %shard_map.127 = (f32[16,48,128]{2,1,0:T(8,128)S(1)}, f32[256,256]{1,0:T(8,128)S(1)}, f32[256,256]{1,0:T(8,128)S(1)}, f32[256,256]{1,0:T(8,128)S(1)}, f32[256,25...) custom-call(s32[3]{0:T(128)S(1)} %pad_add_fusion.place, ...), custom_call_target="tpu_custom_call" | custom-call | tf_op jit(solution)/shard_map/pallas_call | solution.py:396
  87.0 11.8 %all_to_all.49.received = f32[16,48,128]{2,1,0:T(8,128)S(1)} all-to-all(f32[16,48,128]{2,1,0:T(8,128)S(1)} %get-tuple-element.47), channel_id=1, replica_groups=mesh['y'=8,'zh'=4,'zl'=2,'x'=4,'core'=2] {'zl','x','core'}, dimensions={0} | all-to-all | bytes 786432 | tf_op jit(solution)/shard_map/all_to_all | solution.py:408
  98.9 3.3 %collective-permute-start = (f32[80,128]{1,0:T(8,128)S(1)}, f32[80,128]{1,0:T(8,128)S(1)}, u32[]{:S(2)}, u32[]{:S(2)}) collective-permute-start(f32[80,128]{1,0:T(8,128)S(1)} %get-tuple-element.49), channel_id=1, source_target_pairs={{0,16},{16,32},{32,48},{48,64},{64,80},{80,96},{96,112},{112,128},... | collective-permute-start | bytes 122888 | tf_op jit(solution)/shard_map/ppermute | solution.py:478
  102.2 1.3 collective-permute-start.1
  103.5 0.7 shard_map.129.rest
  104.2 3.6 %collective-permute-done.1.after = f32[80,128]{1,0:T(8,128)S(1)} collective-permute-done((f32[80,128]{1,0:T(8,128)S(1)}, f32[80,128]{1,0:T(8,128)S(1)}, u32[]{:S(2)}, u32[]{:S(2)}) %collective-permute-start.1) | collective-permute-done | bytes 40992 | tf_op jit(solution)/shard_map/ppermute | solution.py:479
  107.8 0.7 shard_map.130
  108.6 12.8 %all_to_all.50 = f32[16,16,256]{2,1,0:T(8,128)S(1)} all-to-all(f32[16,16,256]{2,1,0:T(8,128)S(1)} %get-tuple-element.52), channel_id=1, replica_groups=mesh['y'=8,'zh'=4,'zl'=2,'x'=4,'core'=2] {'zl','x','core'}, dimensions={0} | all-to-all | bytes 524288 | tf_op jit(solution)/shard_map/all_to_all | solution.py:408
  121.4 2.3 %shard_map.132 = f32[512,128]{1,0:T(8,128)} custom-call(f32[256,256]{1,0:T(8,128)S(1)} %bitcast.31, bf16[256,256]{1,0:T(8,128)(2,1)S(1)} %copy-done.5, bf16[256,512]{1,0:T(8,128)(2,1)S(1)} %copy-done.1, f32[256,256]{1,0:T(8,128)S(1)} %get-tuple-element.53.refs_0_, f32[256,256]{1,0:T(8,128)S(1)} %get-tuple-element.54.refs_1_, ...), custom_call_target="tpu_custom_call" | custom-call | tf_op jit(solution)/shard_map/pallas_call | solution.py:396
  123.7 11.7 %all-to-all-start.5 = ((f32[512,1,128]{2,1,0:T(1,128)}), f32[512,1,128]{2,1,0:T(1,128)S(1)}, u32[]{:S(2)}, u32[]{:S(2)}) async-start(f32[512,1,128]{2,1,0:T(1,128)} %bitcast.19), calls=%async_computation.5 | async-start | bytes 524288 | tf_op jit(solution)/shard_map/all_to_all | solution.py:408
  135.3 0.7 shard_map.131
  136.0 16.6 %all-to-all-done.5 = f32[512,1,128]{2,1,0:T(1,128)S(1)} async-done(((f32[512,1,128]{2,1,0:T(1,128)}), f32[512,1,128]{2,1,0:T(1,128)S(1)}, u32[]{:S(2)}, u32[]{:S(2)}) %all-to-all-start.5) | async-done | bytes 262176 | tf_op jit(solution)/shard_map/all_to_all | solution.py:408
  152.6 1.9 %shard_map.133 = bf16[2,4,16,16,128]{4,3,2,1,0:T(8,128)(2,1)} custom-call(s32[3]{0:T(128)S(1)} %pad_add_fusion.place, f32[512,128]{1,0:T(8,128)S(1)} %bitcast.30, f32[2,64,128]{2,1,0:T(8,128)S(1)} %get-tuple-element.61.spectra_in, bf16[256,256]{1,0:T(8,128)(2,1)S(1)} %copy-done.2), custom_call_target="tpu_custom_call" | custom-call | tf_op jit(solution)/shard_map/pallas_call | solution.py:396
  (25 shorter events, 0.4 us)
Async XLA Ops:
  2.3 17.5 %all-to-all-start = ((f32[16,16,256]{2,1,0:T(8,128)}), f32[16,16,256]{2,1,0:T(8,128)S(1)}, u32[]{:S(2)}, u32[]{:S(2)}) async-start(f32[16,16,256]{2,1,0:T(8,128)} %bitcast.8), calls=%async_computation | async-start | bytes 524288 | tf_op jit(solution)/shard_map/all_to_all | solution.py:408
  12.5 0.7 copy-start.6
  12.6 0.7 copy-start.10
  12.6 0.7 copy-start.7
  12.6 0.7 copy-start.8
  12.6 0.7 copy-start.9
  19.8 36.6 %copy-start.3 = (bf16[2,4,16,16,128]{4,3,2,1,0:T(8,128)(2,1)S(1)}, bf16[2,4,16,16,128]{4,3,2,1,0:T(8,128)(2,1)}, u32[]{:S(2)}) copy-start(bf16[2,4,16,16,128]{4,3,2,1,0:T(8,128)(2,1)} %weight.1) | copy-start | bytes 1572868
  23.2 33.2 %copy-start.2 = (bf16[256,256]{1,0:T(8,128)(2,1)S(1)}, bf16[256,256]{1,0:T(8,128)(2,1)}, u32[]{:S(2)}) copy-start(bf16[256,256]{1,0:T(8,128)(2,1)} %constant.36.clone.x_table) | copy-start | bytes 393220
  58.1 25.5 %all-to-all-start.2 = ((f32[512,1,128]{2,1,0:T(1,128)}), f32[512,1,128]{2,1,0:T(1,128)S(1)}, u32[]{:S(2)}, u32[]{:S(2)}) async-start(f32[512,1,128]{2,1,0:T(1,128)} %bitcast.14), calls=%async_computation.2 | async-start | bytes 524288 | tf_op jit(solution)/shard_map/all_to_all | solution.py:408
  66.4 17.1 %copy-start.1 = (bf16[256,512]{1,0:T(8,128)(2,1)S(1)}, bf16[256,512]{1,0:T(8,128)(2,1)}, u32[]{:S(2)}) copy-start(bf16[256,512]{1,0:T(8,128)(2,1)} %constant.35.clone.y_far.y_table) | copy-start | bytes 786436
  66.5 17.1 %copy-start.4 = (bf16[512,256]{1,0:T(8,128)(2,1)S(1)}, bf16[512,256]{1,0:T(8,128)(2,1)}, u32[]{:S(2)}) copy-start(bf16[512,256]{1,0:T(8,128)(2,1)} %constant.37.clone.z_table) | copy-start | bytes 786436
  87.0 11.8 %copy-start = (f32[1,8,16,256]{3,2,1,0:T(8,128)S(1)}, f32[1,8,16,256]{3,2,1,0:T(8,128)}, u32[]{:S(2)}) copy-start(f32[1,8,16,256]{3,2,1,0:T(8,128)} %param.11) | copy-start | bytes 393220
  98.9 5.3 %collective-permute-start = (f32[80,128]{1,0:T(8,128)S(1)}, f32[80,128]{1,0:T(8,128)S(1)}, u32[]{:S(2)}, u32[]{:S(2)}) collective-permute-start(f32[80,128]{1,0:T(8,128)S(1)} %get-tuple-element.49), channel_id=1, source_target_pairs={{0,16},{16,32},{32,48},{48,64},{64,80},{80,96},{96,112},{112,128},... | collective-permute-start | bytes 122888 | tf_op jit(solution)/shard_map/ppermute | solution.py:478
  102.2 5.6 %collective-permute-start.1 = (f32[80,128]{1,0:T(8,128)S(1)}, f32[80,128]{1,0:T(8,128)S(1)}, u32[]{:S(2)}, u32[]{:S(2)}) collective-permute-start(f32[80,128]{1,0:T(8,128)S(1)} %get-tuple-element.50), channel_id=1, source_target_pairs={{16,0},{32,16},{48,32},{64,48},{80,64},{96,80},{112,96},{128,112},... | collective-permute-start | bytes 122888 | tf_op jit(solution)/shard_map/ppermute | solution.py:479
  108.6 12.8 %copy-start.5 = (bf16[256,256]{1,0:T(8,128)(2,1)S(1)}, bf16[256,256]{1,0:T(8,128)(2,1)}, u32[]{:S(2)}) copy-start(bf16[256,256]{1,0:T(8,128)(2,1)} %constant.34.clone.z_far.z_table) | copy-start | bytes 393220
  123.7 28.9 %all-to-all-start.5 = ((f32[512,1,128]{2,1,0:T(1,128)}), f32[512,1,128]{2,1,0:T(1,128)S(1)}, u32[]{:S(2)}, u32[]{:S(2)}) async-start(f32[512,1,128]{2,1,0:T(1,128)} %bitcast.19), calls=%async_computation.5 | async-start | bytes 524288 | tf_op jit(solution)/shard_map/all_to_all | solution.py:408

commit v4 on v3

--- a/solution.py
+++ b/solution.py
@@ -124,12 +124,11 @@
             out[column * 32 : column * 32 + 32, :] = total
 
 
-def lift_kernel(place, params, plane, z_table, y_table, out, turned, high, low, lines):
-    core = place[0]
+def lift_kernel(plane, z_table, y_table, scalars, out, turned, high, low, lines):
     turned[...] = plane[...].T
 
     def fill(channel, stage_high, stage_low):
-        gain, offset = 0.5 * params[0, core * HALF + channel], 0.5 * params[1, core * HALF + channel]
+        gain, offset = scalars[channel : channel + 1, :], scalars[HALF + channel : HALF + channel + 1, :]
         for t in range(8):
             rows = slice(32 * t, 32 * t + 32)
             stage_high[rows, :], stage_low[rows, :] = split(lift(turned[rows, :], gain, offset))
@@ -137,9 +136,11 @@
     plane_forward(fill, z_table, y_table, high, low, lines, out)
 
 
-def grad_kernel(adjoint, z_table, y_table, *refs):
+def grad_kernel(adjoint, rest, z_table, y_table, *refs):
     slope = refs[:HALF]
-    out, turned, high, low, lines = refs[HALF:]
+    out, residual, turned, high, low, lines, sem = refs[HALF:]
+    copy = pltpu.make_async_copy(rest, residual, sem)
+    copy.start()
     turned[...] = adjoint[...].T
 
     def fill(channel, stage_high, stage_low):
@@ -148,12 +149,27 @@
             stage_high[rows, :], stage_low[rows, :] = split(turned[rows, :] * slope[channel][rows, :])
 
     plane_forward(fill, z_table, y_table, high, low, lines, out)
-
-
-def ready_kernel(z_far, y_far, z_table, y_table, sems):
+    copy.wait()
+
+
+def ready_kernel(place, scale, shift, readout, z_far, y_far, z_table, y_table, scalars, ring, doubling, sems):
     copies = [pltpu.make_async_copy(z_far, z_table, sems.at[0]), pltpu.make_async_copy(y_far, y_table, sems.at[1])]
     for copy in copies:
         copy.start()
+    first = place[0] * HALF
+    for n in range(HALF):
+        for m, value in enumerate((0.5 * scale[first + n], 0.5 * shift[first + n], readout[first + n])):
+            scalars[HALF * m + n : HALF * m + n + 1, :] = jnp.full((1, GRID), value, F32)
+    row = lax.broadcasted_iota(jnp.int32, (24, GRID), 0)
+    first_row = jnp.where(place[2] == 0, 4, 3)
+    last_row = jnp.where(place[2] == COLS - 1, 19, 20)
+    ring[0:24, :] = jnp.where(jnp.logical_and(row >= first_row, row <= last_row), 1.0, 0.0).astype(F32)
+    row = lax.broadcasted_iota(jnp.int32, (8, GRID), 0)
+    before, after = jnp.where(place[1] > 0, 1.0, 0.0), jnp.where(place[1] < ROWS - 1, 1.0, 0.0)
+    ring[24:32, :] = jnp.where(row == 0, before, after).astype(F32)
+    row = lax.broadcasted_iota(jnp.int32, (64, 128), 0)
+    zero_mode = jnp.logical_and((row // HALF) % 4 == 0, place[2] == 0)
+    doubling[...] = jnp.where(zero_mode, 1.0, 2.0).astype(F32)
     for copy in copies:
         copy.wait()
 
@@ -166,7 +182,7 @@
         copy.wait()
 
 
-def local_kernel(place, params, plane, margin, *refs):
+def local_kernel(place, scale, shift, bias, weight, plane, margin, *refs):
     out, turned = refs[:HALF], refs[HALF]
     first = place[0] * HALF
     keep = jnp.where(place[0] == 0, 1.0, 0.0).astype(F32)
@@ -179,10 +195,10 @@
     def step(t, carry):
         rows = pl.ds(pl.multiple_of(t * 16, 16), 16)
         field = turned[rows, :]
-        sums = [jnp.full((16, GRID), params[2, first + o], F32) for o in range(HALF)]
+        sums = [jnp.full((16, GRID), bias[first + o], F32) for o in range(HALF)]
         for i in range(WIDTH):
-            lifted = lift(field, 0.5 * params[0, i], 0.5 * params[1, i])
-            sums = [sums[o] + params[4 + i, first + o] * lifted for o in range(HALF)]
+            lifted = lift(field, 0.5 * scale[i], 0.5 * shift[i])
+            sums = [sums[o] + weight[i, first + o] * lifted for o in range(HALF)]
         for o in range(HALF):
             out[o][rows, :] = sums[o]
         return carry
@@ -190,10 +206,9 @@
     lax.fori_loop(0, GRID // 16, step, 0)
 
 
-def inverse_kernel(place, params, received, margin, z_table, y_table, *refs):
+def inverse_kernel(received, margin, z_table, y_table, scalars, *refs):
     local, out, slope = refs[:HALF], refs[HALF], refs[HALF + 1 : 2 * HALF + 1]
     grid, lines, spectral, total, padded = refs[2 * HALF + 1 :]
-    core = place[0]
     lane = lane_index((ROWS, 128)) // 32
     for tile in range(4):
         parts = [received[(4 * tile + e) * 32 : (4 * tile + e) * 32 + 32, :] for e in range(4)]
@@ -211,7 +226,7 @@
         modes = jnp.concatenate([lines[:, o, 0:GRID], lines[:, o, GRID:]], axis=0)
         product = dot(z_table[...], jnp.concatenate(split(modes), axis=0), NN)
         spectral[...] = product[:GRID] + product[GRID:]
-        read = params[3, core * HALF + o]
+        read = scalars[2 * HALF + o : 2 * HALF + o + 1, :]
         for t in range(8):
             rows = slice(32 * t, 32 * t + 32)
             value = spectral[rows, :] + local[o][rows, :]
@@ -279,13 +294,10 @@
             out[place : place + 32, :] = result[q * 32 : q * 32 + 32, k * 128 : k * 128 + 128]
 
 
-def outer_kernel(place, received, spectra_in, x_table, out, real, imag, stage, sems):
+def outer_kernel(received, spectra_in, x_table, doubling, out, real, imag, stage, sems):
     low = lane_index((64, 128)) < MODES
     sign = jnp.where(low, -1.0, 1.0).astype(F32)
-    row = lax.broadcasted_iota(jnp.int32, (64, 128), 0)
-    zero_mode = jnp.logical_and((row // HALF) % 4 == 0, place[2] == 0)
-    doubling = jnp.where(zero_mode, 1.0, 2.0).astype(F32)
-    grads = [doubling * g for g in gather_spectra(received, x_table, sign)]
+    grads = [doubling[...] * g for g in gather_spectra(received, x_table, sign)]
     turned = [-sign * swapped(g) for g in grads]
     for k in range(2):
         spectra = spectra_in[k]
@@ -333,16 +345,9 @@
         ref[64:80, :] = rest[:, 128:256]
 
 
-def inside_rows(col_place):
-    row = lax.broadcasted_iota(jnp.int32, (24, GRID), 0)
-    first_row = jnp.where(col_place == 0, 4, 3)
-    last_row = jnp.where(col_place == COLS - 1, 19, 20)
-    return jnp.logical_and(row >= first_row, row <= last_row)
-
-
-def inner_kernel(place, wide, field, rest, sources):
+def inner_kernel(wide, field, ring, rest, sources):
     lane = lane_index((24, GRID))
-    inside = inside_rows(place[2])
+    inside = ring[0:24, :]
     for q in range(PLANES):
         sources[q] = jnp.zeros((24, GRID), F32)
         sources[q, 4:20, :] = field[q]
@@ -354,33 +359,27 @@
             near = near + wide[q - 1]
         if q < PLANES - 1:
             near = near + wide[q + 1]
-        rest[q] = jnp.where(inside, 6.0 * centre - near, 0.0)
-
-
-def stencil_kernel(place, rest, wide, before, after, ends, adjoint):
-    row_place = place[1]
+        rest[q] = inside * (6.0 * centre - near)
+
+
+def stencil_kernel(rest, wide, before, after, ring, residual, adjoint):
     lane = lane_index((24, GRID))
-    inside = inside_rows(place[2])
+    inside = ring[0:24, :]
     values = [rest[q] for q in range(PLANES)]
     outer = []
-    for n, ref, edge, some in ((0, before, 0, row_place > 0), (1, after, PLANES - 1, row_place < ROWS - 1)):
+    for n, ref, edge in ((0, before, 0), (1, after, PLANES - 1)):
         beyond = jnp.concatenate([ref[0:24, :], ref[24:48, :]], axis=1)
-        values[edge] = values[edge] - jnp.where(inside, beyond, 0.0)
-        ends[n] = values[edge][4:20]
+        values[edge] = values[edge] - inside * beyond
         part = jnp.concatenate([ref[48:64, :], ref[64:80, :]], axis=1) - wide[edge, 4:20, :]
-        outer.append(jnp.where(some, part, 0.0))
+        outer.append(ring[24 + n : 25 + n, :] * part)
     for q in range(PLANES):
         low = outer[0] if q == 0 else values[q - 1][4:20]
         high = outer[1] if q == PLANES - 1 else values[q + 1][4:20]
+        residual[q] = values[q][4:20]
         near = (beside_y(values[q]) + beside_z(values[q], lane))[4:20]
         value = 6.0 * values[q][4:20] - (low + high + near)
         adjoint[2 * q] = value
         adjoint[2 * q + 1] = value
-
-
-def residual_kernel(rest, ends, out):
-    for q in range(PLANES):
-        out[q] = ends[0] if q == 0 else ends[1] if q == PLANES - 1 else rest[q, 4:20, :]
 
 
 def call(kernel, operands, scalars, outputs, scratch, flops=0, far=0, far_out=()):
@@ -415,7 +414,6 @@
 def shards(right_side, lift_scale, lift_shift, spectral_weight, local_weight, local_bias, readout):
     z_forward, z_inverse, y_table, x_table = tables()
     place = jnp.stack([lax.axis_index("core"), lax.axis_index(ROW), lax.axis_index(COL)]).astype(jnp.int32)
-    params = jnp.concatenate([jnp.stack([lift_scale, lift_shift, local_bias, readout]), local_weight], axis=0)
     everywhere = COL + ROW
     field = right_side[0]
     copies = pltpu.SemaphoreType.DMA((2,))
@@ -426,13 +424,20 @@
     near = call(
         ready_kernel,
         (z_forward, y_table),
-        (),
-        [jax.ShapeDtypeStruct(z_forward.shape, BF16), jax.ShapeDtypeStruct(y_table.shape, BF16)],
+        (place, lift_scale, lift_shift, readout),
+        [
+            jax.ShapeDtypeStruct(z_forward.shape, BF16),
+            jax.ShapeDtypeStruct(y_table.shape, BF16),
+            shape(24, GRID),
+            shape(32, GRID),
+            shape(64, 128),
+        ],
         [copies],
         flops=1 << 24,
         far=2,
     )
     plane, near = lax.optimization_barrier((plane, near))
+    z_near, y_near, scalars, ring, doubling = near
     plane = plane.reshape(GRID, GRID)
     line_scratch = pltpu.VMEM((MODES, HALF, 2 * GRID), F32)
     plane_scratch = [
@@ -441,12 +446,12 @@
         pltpu.VMEM((GRID, GRID), BF16),
         line_scratch,
     ]
-    lifted = call(lift_kernel, (plane, *near), (place, params), shape(512, 128), plane_scratch)
+    lifted = call(lift_kernel, (plane, z_near, y_near, scalars), (), shape(512, 128), plane_scratch)
     lifted = exchange(lifted, everywhere)
     margin, *local = call(
         local_kernel,
         (plane,),
-        (place, params),
+        (place, lift_scale, lift_shift, local_bias, local_weight),
         [shape(2 * COLS, GRID)] + fields,
         [pltpu.VMEM((GRID, GRID), F32)],
         flops=1 << 27,
@@ -458,8 +463,8 @@
     mixed = exchange(mixed, everywhere)
     message, *slope = call(
         inverse_kernel,
-        (mixed, margin, z_inverse, y_table, *local),
-        (place, params),
+        (mixed, margin, z_inverse, y_table, scalars, *local),
+        (),
         [shape(COLS, 48, 128)] + fields,
         [
             pltpu.VMEM((128, 512), F32),
@@ -479,27 +484,33 @@
     after = lax.ppermute(lower, ROW, backward)
     rest = call(
         inner_kernel,
-        (wide, field),
-        (place,),
+        (wide, field, ring),
+        (),
         shape(PLANES, 24, GRID),
         [pltpu.VMEM((PLANES, 24, GRID), F32)],
         flops=1 << 22,
     )
-    ends, adjoint = call(
+    rest, adjoint = call(
         stencil_kernel,
-        (rest, wide, before, after),
-        (place,),
-        [shape(2, COLS, GRID), shape(2 * PLANES, COLS, GRID)],
+        (rest, wide, before, after, ring),
+        (),
+        [shape(PLANES, COLS, GRID), shape(2 * PLANES, COLS, GRID)],
         [],
     )
-    residual = call(residual_kernel, (rest, ends), (), shape(PLANES, COLS, GRID), [], flops=1 << 22)
     adjoint = exchange(adjoint, COL).reshape(GRID, GRID)
-    grads = call(grad_kernel, (adjoint, z_forward, y_table, *slope), (), shape(512, 128), plane_scratch)
+    grads, residual = call(
+        grad_kernel,
+        (adjoint, rest, z_forward, y_table, *slope),
+        (),
+        [shape(512, 128), shape(PLANES, COLS, GRID)],
+        plane_scratch + [pltpu.SemaphoreType.DMA],
+        far_out=(1,),
+    )
     grads = exchange(grads, everywhere)
     spectral_grad = call(
         outer_kernel,
-        (grads, spectra, x_table),
-        (place,),
+        (grads, spectra, x_table, doubling),
+        (),
         jax.ShapeDtypeStruct(spectral_weight.shape, BF16),
         [pair, pair, pltpu.VMEM(spectral_weight.shape, BF16), pltpu.SemaphoreType.DMA((8,))],
         far_out=(0,),

time: 155 us -> 152 us (0.981)
  blocking collectives: 57.8 us -> 86.6 us
  waiting for transfers between devices: 36.4 us -> 20.2 us
  starting transfers between devices: 34.8 us -> 23.4 us
  Pallas kernels: 23.7 us -> 19.7 us
    all_to_all x3 -> x4, blocking collectives: 57.8 us -> 86.6 us  [exchange(): return lax.all_to_all(value, axes, split_axis=0, concat_axis=0, tiled=True)]
    all_to_all x3 -> x2, waiting for transfers between devices: 32.8 us -> 16 us  [exchange(): return lax.all_to_all(value, axes, split_axis=0, concat_axis=0, tiled=True)]
    all_to_all x3 -> x2, starting transfers between devices: 30.2 us -> 18.7 us  [exchange(): return lax.all_to_all(value, axes, split_axis=0, concat_axis=0, tiled=True)]
    pallas_call x12 -> x11, Pallas kernels: 23.7 us -> 19.7 us  [call(): pl.pallas_call(kernel, in_specs=[smem] * len(scalars) + [vmem] * (len(ope...]
  transfers between devices with their start and end apart: 5 -> 4, of which waited for: 4 -> 3; matrix products, arithmetic and copies ran while one was open for 0% -> 0% of each run, Pallas kernels for 5% -> 5%
where the time goes in v4:
time: 152 us
  blocking collectives  86.6 us (57%)
  starting transfers between devices  23.4 us (15%)
  waiting for transfers between devices  20.2 us (13%)
  Pallas kernels  19.7 us (13%)
    all_to_all x4, blocking collectives, exchange(): return lax.all_to_all(value, axes, split_axis=0, concat_axis=0, tiled=True)  86.6 us
    pallas_call x11, Pallas kernels, call(): pl.pallas_call(kernel, in_specs=[smem] * len(scalars) + [vmem] * (len(ope...  19.7 us
    all_to_all x2, starting transfers between devices, exchange(): return lax.all_to_all(value, axes, split_axis=0, concat_axis=0, tiled=True)  18.7 us
    all_to_all x2, waiting for transfers between devices, exchange(): return lax.all_to_all(value, axes, split_axis=0, concat_axis=0, tiled=True)  16 us
    ppermute x1, waiting for transfers between devices, shards(): after = lax.ppermute(lower, ROW, backward)  4.15 us
    ppermute x1, starting transfers between devices, shards(): before = lax.ppermute(upper, ROW, forward)  3.28 us
  transfers between devices with their start and end apart: 4, of which 3 were waited for; matrix products, arithmetic and copies ran while one was open for 0% of the time, Pallas kernels for 5%

profile of v4, /device:TPU:1, one launch (start us, length us, event | category | flops | bytes accessed | tf_op | source)
XLA Modules:
  0.0 151.7 jit_solution(10074345220949672215)
XLA Ops:
  0.6 1.7 %shard_map.122 = f32[8,2,16,256]{3,2,1,0:T(8,128)} custom-call(f32[8,16,256]{2,1,0:T(8,128)} %bitcast.20), custom_call_target="tpu_custom_call" | custom-call | tf_op jit(solution)/shard_map/pallas_call | solution.py:395
  2.3 10.2 %all-to-all-start = ((f32[16,16,256]{2,1,0:T(8,128)}), f32[16,16,256]{2,1,0:T(8,128)S(1)}, u32[]{:S(2)}, u32[]{:S(2)}) async-start(f32[16,16,256]{2,1,0:T(8,128)} %bitcast.1), calls=%async_computation | async-start | bytes 524288 | tf_op jit(solution)/shard_map/all_to_all | solution.py:407
  12.6 0.1 pad_add_fusion.place
  12.7 0.5 copy-done.7
  13.2 1.6 %shard_map.123 = (bf16[256,256]{1,0:T(8,128)(2,1)S(1)}, bf16[256,512]{1,0:T(8,128)(2,1)S(1)}, f32[24,256]{1,0:T(8,128)S(1)}, f32[32,256]{1,0:T(8,128)S(1)}, f32[64,128]{1,0:T(8,128)S(1)}) custom-call(s32[3]{0:T(128)S(1)} %pad_add_fusion.place, f32[16]{0:T(128)S(1)} %copy-done.8, f32[16]{0:T(128)S(1)} %copy-done.9, f32[16]{0:T(128)S(1)} %copy-done.7, ...), custom_call_target="tpu_custom_call" | custom-call | flops 16777216 | bytes 4194304 | tf_op jit(solution)/shard_map/pallas_call | solution.py:395
  14.8 4.9 %all-to-all-done = f32[16,16,256]{2,1,0:T(8,128)S(1)} async-done(((f32[16,16,256]{2,1,0:T(8,128)}), f32[16,16,256]{2,1,0:T(8,128)S(1)}, u32[]{:S(2)}, u32[]{:S(2)}) %all-to-all-start) | async-done | bytes 262176 | tf_op jit(solution)/shard_map/all_to_all | solution.py:407
  19.8 2.7 %shard_map.124 = f32[512,128]{1,0:T(8,128)S(1)} custom-call(f32[256,256]{1,0:T(8,128)S(1)} %bitcast.23, bf16[256,256]{1,0:T(8,128)(2,1)S(1)} %get-tuple-element.46.z_table, bf16[256,512]{1,0:T(8,128)(2,1)S(1)} %get-tuple-element.47.y_table, f32[24,256]{1,0:T(8,128)S(1)} %get-tuple-element.48.scalars), custom_call_target="tpu_custom_call" | custom-call | tf_op jit(solution)/shard_map/pallas_call | solution.py:395
  22.5 33.2 %all_to_all.48 = f32[512,1,128]{2,1,0:T(1,128)S(1)} all-to-all(f32[512,1,128]{2,1,0:T(1,128)S(1)} %bitcast.27), channel_id=1, replica_groups=mesh['y'=8,'zh'=4,'zl'=2,'x'=4,'core'=2] {'zl','x','core','y','zh'}, dimensions={0} | all-to-all | bytes 524288 | tf_op jit(solution)/shard_map/all_to_all | solution.py:407
  55.7 1.7 %shard_map.125 = (f32[512,128]{1,0:T(8,128)}, f32[2,64,128]{2,1,0:T(8,128)S(1)}) custom-call(f32[512,128]{1,0:T(8,128)S(1)} %bitcast.26, bf16[2,4,16,16,128]{4,3,2,1,0:T(8,128)(2,1)S(1)} %copy-done.2, bf16[256,256]{1,0:T(8,128)(2,1)S(1)} %copy-done.3), custom_call_target="tpu_custom_call" | custom-call | tf_op jit(solution)/shard_map/pallas_call | solution.py:395
  57.4 8.5 %all-to-all-start.2 = ((f32[512,1,128]{2,1,0:T(1,128)}), f32[512,1,128]{2,1,0:T(1,128)S(1)}, u32[]{:S(2)}, u32[]{:S(2)}) async-start(f32[512,1,128]{2,1,0:T(1,128)} %bitcast.10), calls=%async_computation.2 | async-start | bytes 524288 | tf_op jit(solution)/shard_map/all_to_all | solution.py:407
  65.9 6.0 %shard_map.126 = (f32[32,256]{1,0:T(8,128)S(1)}, f32[256,256]{1,0:T(8,128)S(1)}, f32[256,256]{1,0:T(8,128)S(1)}, f32[256,256]{1,0:T(8,128)S(1)}, f32[256,256]{1,...) custom-call(s32[3]{0:T(128)S(1)} %pad_add_fusion.place, ...), custom_call_target="tpu_custom_call" | custom-call | flops 134217728 | bytes 4194304 | tf_op jit(solution)/shard_map/pallas_call | solution.py:395
  71.9 11.1 %all-to-all-done.2 = f32[512,1,128]{2,1,0:T(1,128)S(1)} async-done(((f32[512,1,128]{2,1,0:T(1,128)}), f32[512,1,128]{2,1,0:T(1,128)S(1)}, u32[]{:S(2)}, u32[]{:S(2)}) %all-to-all-start.2) | async-done | bytes 262176 | tf_op jit(solution)/shard_map/all_to_all | solution.py:407
  83.0 2.7 %shard_map.127 = (f32[16,48,128]{2,1,0:T(8,128)S(1)}, f32[256,256]{1,0:T(8,128)S(1)}, f32[256,256]{1,0:T(8,128)S(1)}, f32[256,256]{1,0:T(8,128)S(1)}, f32[256,25...) custom-call(f32[512,128]{1,0:T(8,128)S(1)} %bitcast.25, ...), custom_call_target="tpu_custom_call" | custom-call | tf_op jit(solution)/shard_map/pallas_call | solution.py:395
  85.6 11.8 %all_to_all.49.received = f32[16,48,128]{2,1,0:T(8,128)S(1)} all-to-all(f32[16,48,128]{2,1,0:T(8,128)S(1)} %get-tuple-element.59), channel_id=1, replica_groups=mesh['y'=8,'zh'=4,'zl'=2,'x'=4,'core'=2] {'zl','x','core'}, dimensions={0} | all-to-all | bytes 786432 | tf_op jit(solution)/shard_map/all_to_all | solution.py:407
  97.5 0.1 shard_map.128
  97.6 3.3 %collective-permute-start = (f32[80,128]{1,0:T(8,128)S(1)}, f32[80,128]{1,0:T(8,128)S(1)}, u32[]{:S(2)}, u32[]{:S(2)}) collective-permute-start(f32[80,128]{1,0:T(8,128)S(1)} %get-tuple-element.62), channel_id=1, source_target_pairs={{0,16},{16,32},{32,48},{48,64},{64,80},{80,96},{96,112},{112,128},... | collective-permute-start | bytes 122888 | tf_op jit(solution)/shard_map/ppermute | solution.py:483
  100.8 1.5 collective-permute-start.1
  102.3 0.2 shard_map.129.rest
  102.5 4.2 %collective-permute-done.1.after = f32[80,128]{1,0:T(8,128)S(1)} collective-permute-done((f32[80,128]{1,0:T(8,128)S(1)}, f32[80,128]{1,0:T(8,128)S(1)}, u32[]{:S(2)}, u32[]{:S(2)}) %collective-permute-start.1) | collective-permute-done | bytes 40992 | tf_op jit(solution)/shard_map/ppermute | solution.py:484
  106.7 0.2 shard_map.130
  106.9 12.8 %all_to_all.50 = f32[16,16,256]{2,1,0:T(8,128)S(1)} all-to-all(f32[16,16,256]{2,1,0:T(8,128)S(1)} %get-tuple-element.64), channel_id=1, replica_groups=mesh['y'=8,'zh'=4,'zl'=2,'x'=4,'core'=2] {'zl','x','core'}, dimensions={0} | all-to-all | bytes 524288 | tf_op jit(solution)/shard_map/all_to_all | solution.py:407
  119.7 1.6 %shard_map.131 = (f32[512,128]{1,0:T(8,128)S(1)}, f32[8,16,256]{2,1,0:T(8,128)}) custom-call(f32[256,256]{1,0:T(8,128)S(1)} %bitcast.29, f32[8,16,256]{2,1,0:T(8,128)S(1)} %get-tuple-element.65.rest, bf16[256,256]{1,0:T(8,128)(2,1)S(1)} %copy-done.5, bf16[256,512]{1,0:T(8,128)(2,1)S(1)} %copy-done.1, f32[256,256]{1,0:T(8,128)S(1)} %get-tuple-element.66.refs_0_, ...), custom_call_target="tpu_custom_call" | custom-call | tf_op jit(solution)/shard_map/pallas_call | solution.py:395
  121.3 28.8 %all_to_all.51 = f32[512,1,128]{2,1,0:T(1,128)S(1)} all-to-all(f32[512,1,128]{2,1,0:T(1,128)S(1)} %bitcast.30), channel_id=1, replica_groups=mesh['y'=8,'zh'=4,'zl'=2,'x'=4,'core'=2] {'zl','x','core','y','zh'}, dimensions={0} | all-to-all | bytes 524288 | tf_op jit(solution)/shard_map/all_to_all | solution.py:407
  150.2 1.3 shard_map.132
  (22 shorter events, 0.1 us)
Async XLA Ops:
  2.3 17.5 %all-to-all-start = ((f32[16,16,256]{2,1,0:T(8,128)}), f32[16,16,256]{2,1,0:T(8,128)S(1)}, u32[]{:S(2)}, u32[]{:S(2)}) async-start(f32[16,16,256]{2,1,0:T(8,128)} %bitcast.1), calls=%async_computation | async-start | bytes 524288 | tf_op jit(solution)/shard_map/all_to_all | solution.py:407
  12.5 0.7 copy-start.7
  12.6 0.7 copy-start.8
  12.6 0.7 copy-start.9
  19.8 35.9 %copy-start.2 = (bf16[2,4,16,16,128]{4,3,2,1,0:T(8,128)(2,1)S(1)}, bf16[2,4,16,16,128]{4,3,2,1,0:T(8,128)(2,1)}, u32[]{:S(2)}) copy-start(bf16[2,4,16,16,128]{4,3,2,1,0:T(8,128)(2,1)} %weight.2) | copy-start | bytes 1572868
  22.5 33.2 %copy-start.3 = (bf16[256,256]{1,0:T(8,128)(2,1)S(1)}, bf16[256,256]{1,0:T(8,128)(2,1)}, u32[]{:S(2)}) copy-start(bf16[256,256]{1,0:T(8,128)(2,1)} %constant.36.clone.x_table) | copy-start | bytes 393220
  57.4 8.5 %copy-start.6 = (f32[16,16]{1,0:T(8,128)S(1)}, f32[16,16]{1,0:T(8,128)}, u32[]{:S(2)}) copy-start(f32[16,16]{1,0:T(8,128)} %weight.3) | copy-start | bytes 3076
  57.4 8.5 %copy-start.10 = (f32[16]{0:T(128)S(1)}, f32[16]{0:T(128)}, u32[]{:S(2)}) copy-start(f32[16]{0:T(128)} %bias.1) | copy-start | bytes 196
  57.4 25.6 %all-to-all-start.2 = ((f32[512,1,128]{2,1,0:T(1,128)}), f32[512,1,128]{2,1,0:T(1,128)S(1)}, u32[]{:S(2)}, u32[]{:S(2)}) async-start(f32[512,1,128]{2,1,0:T(1,128)} %bitcast.10), calls=%async_computation.2 | async-start | bytes 524288 | tf_op jit(solution)/shard_map/all_to_all | solution.py:407
  65.9 17.1 %copy-start.1 = (bf16[256,512]{1,0:T(8,128)(2,1)S(1)}, bf16[256,512]{1,0:T(8,128)(2,1)}, u32[]{:S(2)}) copy-start(bf16[256,512]{1,0:T(8,128)(2,1)} %constant.35.clone.y_far.y_table) | copy-start | bytes 786436
  65.9 17.1 %copy-start.4 = (bf16[512,256]{1,0:T(8,128)(2,1)S(1)}, bf16[512,256]{1,0:T(8,128)(2,1)}, u32[]{:S(2)}) copy-start(bf16[512,256]{1,0:T(8,128)(2,1)} %constant.37.clone.z_table) | copy-start | bytes 786436
  85.6 11.8 %copy-start = (f32[1,8,16,256]{3,2,1,0:T(8,128)S(1)}, f32[1,8,16,256]{3,2,1,0:T(8,128)}, u32[]{:S(2)}) copy-start(f32[1,8,16,256]{3,2,1,0:T(8,128)} %param.11) | copy-start | bytes 393220
  97.6 4.9 %collective-permute-start = (f32[80,128]{1,0:T(8,128)S(1)}, f32[80,128]{1,0:T(8,128)S(1)}, u32[]{:S(2)}, u32[]{:S(2)}) collective-permute-start(f32[80,128]{1,0:T(8,128)S(1)} %get-tuple-element.62), channel_id=1, source_target_pairs={{0,16},{16,32},{32,48},{48,64},{64,80},{80,96},{96,112},{112,128},... | collective-permute-start | bytes 122888 | tf_op jit(solution)/shard_map/ppermute | solution.py:483
  100.8 5.8 %collective-permute-start.1 = (f32[80,128]{1,0:T(8,128)S(1)}, f32[80,128]{1,0:T(8,128)S(1)}, u32[]{:S(2)}, u32[]{:S(2)}) collective-permute-start(f32[80,128]{1,0:T(8,128)S(1)} %get-tuple-element.63), channel_id=1, source_target_pairs={{16,0},{32,16},{48,32},{64,48},{80,64},{96,80},{112,96},{128,112},... | collective-permute-start | bytes 122888 | tf_op jit(solution)/shard_map/ppermute | solution.py:484
  106.9 12.8 %copy-start.5 = (bf16[256,256]{1,0:T(8,128)(2,1)S(1)}, bf16[256,256]{1,0:T(8,128)(2,1)}, u32[]{:S(2)}) copy-start(bf16[256,256]{1,0:T(8,128)(2,1)} %constant.34.clone.z_far.z_table) | copy-start | bytes 393220

commit v5 on v4

--- a/solution.py
+++ b/solution.py
@@ -99,6 +99,11 @@
 
 def swapped(value):
     return pltpu.roll(value, MODES, 1)
+
+
+def beside_z(value, lane):
+    left = jnp.where(lane == 0, 0.0, pltpu.roll(value, 1, 1))
+    return left + jnp.where(lane == GRID - 1, 0.0, pltpu.roll(value, GRID - 1, 1))
 
 
 def plane_forward(fill, z_table, y_table, stage_high, stage_low, lines, out):
@@ -166,7 +171,8 @@
     ring[0:24, :] = jnp.where(jnp.logical_and(row >= first_row, row <= last_row), 1.0, 0.0).astype(F32)
     row = lax.broadcasted_iota(jnp.int32, (8, GRID), 0)
     before, after = jnp.where(place[1] > 0, 1.0, 0.0), jnp.where(place[1] < ROWS - 1, 1.0, 0.0)
-    ring[24:32, :] = jnp.where(row == 0, before, after).astype(F32)
+    odd = jnp.where(place[1] % 2 == 1, 1.0, 0.0)
+    ring[24:32, :] = jnp.where(row == 0, before, jnp.where(row == 1, after, odd)).astype(F32)
     row = lax.broadcasted_iota(jnp.int32, (64, 128), 0)
     zero_mode = jnp.logical_and((row // HALF) % 4 == 0, place[2] == 0)
     doubling[...] = jnp.where(zero_mode, 1.0, 2.0).astype(F32)
@@ -238,14 +244,22 @@
                 total[rows, :] += read * value
     padded[0:8, :] = jnp.zeros((8, GRID), F32)
     padded[256:264, :] = jnp.zeros((8, GRID), F32)
-    padded[4:260, :] = total[...].T
-    row = lax.broadcasted_iota(jnp.int32, (24, GRID), 0)
+    value = total[...].T
+    padded[4:260, :] = value
+    beside = pltpu.roll(value, 1, 0) + pltpu.roll(value, GRID - 1, 0) + beside_z(value, lane_index((GRID, GRID)))
+    spectral[...] = 6.0 * value - beside
+    blank = jnp.zeros((1, GRID), F32)
     for c in range(COLS):
-        before, after = margin[c : c + 1, :], margin[COLS + c : COLS + c + 1, :]
-        block = padded[16 * c : 16 * c + 24, :]
-        block = jnp.where(row == 1, before, jnp.where(row == 22, after, block))
-        out[c, 0:24, :] = block[:, 0:128]
-        out[c, 24:48, :] = block[:, 128:256]
+        before, after = blank, blank
+        if c > 0:
+            before = spectral[16 * c - 1 : 16 * c, :] - margin[c : c + 1, :]
+        if c < COLS - 1:
+            after = spectral[16 * c + 16 : 16 * c + 17, :] - margin[COLS + c : COLS + c + 1, :]
+        for h in range(2):
+            lanes = slice(128 * h, 128 * h + 128)
+            out[c, 20 * h : 20 * h + 1, :] = before[:, lanes]
+            out[c, 20 * h + 1 : 20 * h + 19, :] = padded[16 * c + 3 : 16 * c + 21, lanes]
+            out[c, 20 * h + 19 : 20 * h + 20, :] = after[:, lanes]
 
 
 def gather_spectra(received, x_table, sign):
@@ -320,57 +334,58 @@
         copy.wait()
 
 
-def beside_z(value, lane):
-    left = jnp.where(lane == 0, 0.0, pltpu.roll(value, 1, 1))
-    return left + jnp.where(lane == GRID - 1, 0.0, pltpu.roll(value, GRID - 1, 1))
-
-
 def beside_y(value):
     return pltpu.roll(value, 1, 0) + pltpu.roll(value, 23, 0)
 
 
-def edge_kernel(received, field, wide, lower, upper):
+def edge_kernel(received, field, ring, wide, first, second):
     lane = lane_index((24, GRID))
     for q in range(PLANES):
+        wide[q] = jnp.zeros((24, GRID), F32)
         for h in range(2):
-            rows, lanes = slice(24 * h, 24 * h + 24), slice(128 * h, 128 * h + 128)
-            wide[q, :, lanes] = received[2 * q, rows, :] + received[2 * q + 1, rows, :]
-    for ref, edge, inner in ((lower, 0, 1), (upper, PLANES - 1, PLANES - 2)):
+            lanes = slice(128 * h, 128 * h + 128)
+            both = received[2 * q, 20 * h : 20 * h + 20, :] + received[2 * q + 1, 20 * h : 20 * h + 20, :]
+            wide[q, 3:21, lanes] = both[1:19]
+            wide[q, 1:2, lanes] = both[0:1]
+            wide[q, 22:23, lanes] = both[19:20]
+    sent = []
+    for edge, inner in ((0, 1), (PLANES - 1, PLANES - 2)):
         value = wide[edge]
         rest = 6.0 * value - (wide[inner] + beside_y(value) + beside_z(value, lane))
         rest = rest[4:20] - field[edge]
-        ref[0:24, :] = value[:, 0:128]
-        ref[24:48, :] = value[:, 128:256]
-        ref[48:64, :] = rest[:, 0:128]
-        ref[64:80, :] = rest[:, 128:256]
-
-
-def inner_kernel(wide, field, ring, rest, sources):
+        sent.append(jnp.concatenate([value[:, :128], value[:, 128:], rest[:, :128], rest[:, 128:]], axis=0))
+    odd = jnp.broadcast_to(ring[26:27, 0:128], (80, 128)) > 0.5
+    first[...] = jnp.where(odd, sent[1], sent[0])
+    second[...] = jnp.where(odd, sent[0], sent[1])
+
+
+def inner_kernel(wide, field, ring, rest):
     lane = lane_index((24, GRID))
-    inside = ring[0:24, :]
     for q in range(PLANES):
-        sources[q] = jnp.zeros((24, GRID), F32)
-        sources[q, 4:20, :] = field[q]
-        sources[q, 3:4, :] = wide[q, 1:2, :]
-        sources[q, 20:21, :] = wide[q, 22:23, :]
         centre = wide[q]
-        near = beside_y(centre) + beside_z(centre, lane) + sources[q]
+        across = jnp.zeros((24, GRID), F32)
         if q > 0:
-            near = near + wide[q - 1]
+            across = across + wide[q - 1]
         if q < PLANES - 1:
-            near = near + wide[q + 1]
-        rest[q] = inside * (6.0 * centre - near)
-
-
-def stencil_kernel(rest, wide, before, after, ring, residual, adjoint):
+            across = across + wide[q + 1]
+        value = 6.0 * centre - (beside_y(centre) + beside_z(centre, lane) + across)
+        rest[q] = value
+        rest[q, 4:20, :] = value[4:20] - field[q]
+        rest[q, 3:4, :] = ring[3:4, :] * (wide[q, 1:2, :] - across[3:4])
+        rest[q, 20:21, :] = ring[20:21, :] * (wide[q, 22:23, :] - across[20:21])
+
+
+def stencil_kernel(rest, wide, first, second, ring, residual, adjoint):
     lane = lane_index((24, GRID))
     inside = ring[0:24, :]
     values = [rest[q] for q in range(PLANES)]
+    odd = jnp.broadcast_to(ring[26:27, 0:128], (80, 128)) > 0.5
+    before, after = jnp.where(odd, second[...], first[...]), jnp.where(odd, first[...], second[...])
     outer = []
     for n, ref, edge in ((0, before, 0), (1, after, PLANES - 1)):
-        beyond = jnp.concatenate([ref[0:24, :], ref[24:48, :]], axis=1)
+        beyond = jnp.concatenate([ref[0:24], ref[24:48]], axis=1)
         values[edge] = values[edge] - inside * beyond
-        part = jnp.concatenate([ref[48:64, :], ref[64:80, :]], axis=1) - wide[edge, 4:20, :]
+        part = jnp.concatenate([ref[48:64], ref[64:80]], axis=1) - wide[edge, 4:20, :]
         outer.append(ring[24 + n : 25 + n, :] * part)
     for q in range(PLANES):
         low = outer[0] if q == 0 else values[q - 1][4:20]
@@ -465,7 +480,7 @@
         inverse_kernel,
         (mixed, margin, z_inverse, y_table, scalars, *local),
         (),
-        [shape(COLS, 48, 128)] + fields,
+        [shape(COLS, 40, 128)] + fields,
         [
             pltpu.VMEM((128, 512), F32),
             line_scratch,
@@ -475,24 +490,24 @@
         ],
     )
     message = exchange(message, COL)
-    wide, lower, upper = call(
-        edge_kernel, (message, field), (), [shape(PLANES, 24, GRID), shape(80, 128), shape(80, 128)], []
-    )
-    forward = [(i, i + 1) for i in range(ROWS - 1)]
-    backward = [(target, source) for source, target in forward]
-    before = lax.ppermute(upper, ROW, forward)
-    after = lax.ppermute(lower, ROW, backward)
+    wide, first, second = call(
+        edge_kernel, (message, field, ring), (), [shape(PLANES, 24, GRID), shape(80, 128), shape(80, 128)], []
+    )
+    odd_pairs = [(r, r + 1 if r % 2 else r - 1) for r in range(1, ROWS - 1)]
+    even_pairs = [(r, r - 1 if r % 2 else r + 1) for r in range(ROWS)]
+    first = lax.ppermute(first, ROW, odd_pairs)
+    second = lax.ppermute(second, ROW, even_pairs)
     rest = call(
         inner_kernel,
         (wide, field, ring),
         (),
         shape(PLANES, 24, GRID),
-        [pltpu.VMEM((PLANES, 24, GRID), F32)],
+        [],
         flops=1 << 22,
     )
     rest, adjoint = call(
         stencil_kernel,
-        (rest, wide, before, after, ring),
+        (rest, wide, first, second, ring),
         (),
         [shape(PLANES, COLS, GRID), shape(2 * PLANES, COLS, GRID)],
         [],

time: 152 us -> 149 us (0.980)
  waiting for transfers between devices: 20.2 us -> 17.2 us
    ppermute x2, waiting for transfers between devices: 4.15 us -> 1.16 us  [the longest x1 1.16 us: shards(): second = lax.ppermute(second, ROW, even_pairs)]
where the time goes in v5:
time: 149 us
  blocking collectives  85.6 us (57%)
  starting transfers between devices  24.2 us (16%)
  Pallas kernels  19.9 us (13%)
  waiting for transfers between devices  17.2 us (12%)
    all_to_all x4, blocking collectives, exchange(): return lax.all_to_all(value, axes, split_axis=0, concat_axis=0, tiled=True)  85.6 us
    pallas_call x11, Pallas kernels, call(): pl.pallas_call(kernel, in_specs=[smem] * len(scalars) + [vmem] * (len(ope...  19.9 us
    all_to_all x2, starting transfers between devices, exchange(): return lax.all_to_all(value, axes, split_axis=0, concat_axis=0, tiled=True)  18.7 us
    all_to_all x2, waiting for transfers between devices, exchange(): return lax.all_to_all(value, axes, split_axis=0, concat_axis=0, tiled=True)  16 us
    ppermute x1, starting transfers between devices, shards(): second = lax.ppermute(second, ROW, even_pairs)  4.85 us
  transfers between devices with their start and end apart: 4, of which 3 were waited for; matrix products, arithmetic and copies ran while one was open for 0% of the time, Pallas kernels for 5%

profile of v5, /device:TPU:1, one launch (start us, length us, event | category | flops | bytes accessed | tf_op | source)
XLA Modules:
  0.0 148.6 jit_solution(10446318323161379491)
XLA Ops:
  0.6 1.7 %shard_map.122 = f32[8,2,16,256]{3,2,1,0:T(8,128)} custom-call(f32[8,16,256]{2,1,0:T(8,128)} %bitcast.20), custom_call_target="tpu_custom_call" | custom-call | tf_op jit(solution)/shard_map/pallas_call | solution.py:410
  2.3 10.2 %all-to-all-start = ((f32[16,16,256]{2,1,0:T(8,128)}), f32[16,16,256]{2,1,0:T(8,128)S(1)}, u32[]{:S(2)}, u32[]{:S(2)}) async-start(f32[16,16,256]{2,1,0:T(8,128)} %bitcast.1), calls=%async_computation | async-start | bytes 524288 | tf_op jit(solution)/shard_map/all_to_all | solution.py:422
  12.6 0.1 pad_add_fusion.place
  12.7 0.5 copy-done.7
  13.2 1.6 %shard_map.123 = (bf16[256,256]{1,0:T(8,128)(2,1)S(1)}, bf16[256,512]{1,0:T(8,128)(2,1)S(1)}, f32[24,256]{1,0:T(8,128)S(1)}, f32[32,256]{1,0:T(8,128)S(1)}, f32[64,128]{1,0:T(8,128)S(1)}) custom-call(s32[3]{0:T(128)S(1)} %pad_add_fusion.place, f32[16]{0:T(128)S(1)} %copy-done.8, f32[16]{0:T(128)S(1)} %copy-done.9, f32[16]{0:T(128)S(1)} %copy-done.7, ...), custom_call_target="tpu_custom_call" | custom-call | flops 16777216 | bytes 4194304 | tf_op jit(solution)/shard_map/pallas_call | solution.py:410
  14.8 4.9 %all-to-all-done = f32[16,16,256]{2,1,0:T(8,128)S(1)} async-done(((f32[16,16,256]{2,1,0:T(8,128)}), f32[16,16,256]{2,1,0:T(8,128)S(1)}, u32[]{:S(2)}, u32[]{:S(2)}) %all-to-all-start) | async-done | bytes 262176 | tf_op jit(solution)/shard_map/all_to_all | solution.py:422
  19.8 2.7 %shard_map.124 = f32[512,128]{1,0:T(8,128)S(1)} custom-call(f32[256,256]{1,0:T(8,128)S(1)} %bitcast.23, bf16[256,256]{1,0:T(8,128)(2,1)S(1)} %get-tuple-element.46.z_table, bf16[256,512]{1,0:T(8,128)(2,1)S(1)} %get-tuple-element.47.y_table, f32[24,256]{1,0:T(8,128)S(1)} %get-tuple-element.48.scalars), custom_call_target="tpu_custom_call" | custom-call | tf_op jit(solution)/shard_map/pallas_call | solution.py:410
  22.5 33.2 %all_to_all.48 = f32[512,1,128]{2,1,0:T(1,128)S(1)} all-to-all(f32[512,1,128]{2,1,0:T(1,128)S(1)} %bitcast.27), channel_id=1, replica_groups=mesh['y'=8,'zh'=4,'zl'=2,'x'=4,'core'=2] {'zl','x','core','y','zh'}, dimensions={0} | all-to-all | bytes 524288 | tf_op jit(solution)/shard_map/all_to_all | solution.py:422
  55.7 1.7 %shard_map.125 = (f32[512,128]{1,0:T(8,128)}, f32[2,64,128]{2,1,0:T(8,128)S(1)}) custom-call(f32[512,128]{1,0:T(8,128)S(1)} %bitcast.26, bf16[2,4,16,16,128]{4,3,2,1,0:T(8,128)(2,1)S(1)} %copy-done.2, bf16[256,256]{1,0:T(8,128)(2,1)S(1)} %copy-done.3), custom_call_target="tpu_custom_call" | custom-call | tf_op jit(solution)/shard_map/pallas_call | solution.py:410
  57.4 8.5 %all-to-all-start.2 = ((f32[512,1,128]{2,1,0:T(1,128)}), f32[512,1,128]{2,1,0:T(1,128)S(1)}, u32[]{:S(2)}, u32[]{:S(2)}) async-start(f32[512,1,128]{2,1,0:T(1,128)} %bitcast.10), calls=%async_computation.2 | async-start | bytes 524288 | tf_op jit(solution)/shard_map/all_to_all | solution.py:422
  65.9 6.0 %shard_map.126 = (f32[32,256]{1,0:T(8,128)S(1)}, f32[256,256]{1,0:T(8,128)S(1)}, f32[256,256]{1,0:T(8,128)S(1)}, f32[256,256]{1,0:T(8,128)S(1)}, f32[256,256]{1,...) custom-call(s32[3]{0:T(128)S(1)} %pad_add_fusion.place, ...), custom_call_target="tpu_custom_call" | custom-call | flops 134217728 | bytes 4194304 | tf_op jit(solution)/shard_map/pallas_call | solution.py:410
  71.9 11.1 %all-to-all-done.2 = f32[512,1,128]{2,1,0:T(1,128)S(1)} async-done(((f32[512,1,128]{2,1,0:T(1,128)}), f32[512,1,128]{2,1,0:T(1,128)S(1)}, u32[]{:S(2)}, u32[]{:S(2)}) %all-to-all-start.2) | async-done | bytes 262176 | tf_op jit(solution)/shard_map/all_to_all | solution.py:422
  83.0 2.9 %shard_map.127 = (f32[16,40,128]{2,1,0:T(8,128)S(1)}, f32[256,256]{1,0:T(8,128)S(1)}, f32[256,256]{1,0:T(8,128)S(1)}, f32[256,256]{1,0:T(8,128)S(1)}, f32[256,25...) custom-call(f32[512,128]{1,0:T(8,128)S(1)} %bitcast.25, ...), custom_call_target="tpu_custom_call" | custom-call | tf_op jit(solution)/shard_map/pallas_call | solution.py:410
  85.8 11.1 %all_to_all.49.received = f32[16,40,128]{2,1,0:T(8,128)S(1)} all-to-all(f32[16,40,128]{2,1,0:T(8,128)S(1)} %get-tuple-element.59), channel_id=1, replica_groups=mesh['y'=8,'zh'=4,'zl'=2,'x'=4,'core'=2] {'zl','x','core'}, dimensions={0} | all-to-all | bytes 655360 | tf_op jit(solution)/shard_map/all_to_all | solution.py:422
  96.9 0.1 shard_map.128
  97.1 0.7 collective-permute-start
  97.7 4.9 %collective-permute-start.1 = (f32[80,128]{1,0:T(8,128)S(1)}, f32[80,128]{1,0:T(8,128)S(1)}, u32[]{:S(2)}, u32[]{:S(2)}) collective-permute-start(f32[80,128]{1,0:T(8,128)S(1)} %get-tuple-element.63), channel_id=1, source_target_pairs={{0,16},{16,0},{32,48},{48,32},{64,80},{80,64},{96,112},{112,96},{1... | collective-permute-start | bytes 122888 | tf_op jit(solution)/shard_map/ppermute | solution.py:499
  102.6 0.2 shard_map.129.rest
  102.8 1.2 collective-permute-done.1.second
  104.0 0.2 shard_map.130
  104.2 12.5 %all_to_all.50 = f32[16,16,256]{2,1,0:T(8,128)S(1)} all-to-all(f32[16,16,256]{2,1,0:T(8,128)S(1)} %get-tuple-element.64), channel_id=1, replica_groups=mesh['y'=8,'zh'=4,'zl'=2,'x'=4,'core'=2] {'zl','x','core'}, dimensions={0} | all-to-all | bytes 524288 | tf_op jit(solution)/shard_map/all_to_all | solution.py:422
  116.7 1.6 %shard_map.131 = (f32[512,128]{1,0:T(8,128)S(1)}, f32[8,16,256]{2,1,0:T(8,128)}) custom-call(f32[256,256]{1,0:T(8,128)S(1)} %bitcast.29, f32[8,16,256]{2,1,0:T(8,128)S(1)} %get-tuple-element.65.rest, bf16[256,256]{1,0:T(8,128)(2,1)S(1)} %copy-done.5, bf16[256,512]{1,0:T(8,128)(2,1)S(1)} %copy-done.1, f32[256,256]{1,0:T(8,128)S(1)} %get-tuple-element.66.refs_0_, ...), custom_call_target="tpu_custom_call" | custom-call | tf_op jit(solution)/shard_map/pallas_call | solution.py:410
  118.4 28.7 %all_to_all.51 = f32[512,1,128]{2,1,0:T(1,128)S(1)} all-to-all(f32[512,1,128]{2,1,0:T(1,128)S(1)} %bitcast.30), channel_id=1, replica_groups=mesh['y'=8,'zh'=4,'zl'=2,'x'=4,'core'=2] {'zl','x','core','y','zh'}, dimensions={0} | all-to-all | bytes 524288 | tf_op jit(solution)/shard_map/all_to_all | solution.py:422
  147.1 1.3 shard_map.132
  (22 shorter events, 0.1 us)
Async XLA Ops:
  2.3 17.5 %all-to-all-start = ((f32[16,16,256]{2,1,0:T(8,128)}), f32[16,16,256]{2,1,0:T(8,128)S(1)}, u32[]{:S(2)}, u32[]{:S(2)}) async-start(f32[16,16,256]{2,1,0:T(8,128)} %bitcast.1), calls=%async_computation | async-start | bytes 524288 | tf_op jit(solution)/shard_map/all_to_all | solution.py:422
  12.5 0.7 copy-start.7
  12.6 0.7 copy-start.8
  12.6 0.7 copy-start.9
  19.8 35.9 %copy-start.2 = (bf16[2,4,16,16,128]{4,3,2,1,0:T(8,128)(2,1)S(1)}, bf16[2,4,16,16,128]{4,3,2,1,0:T(8,128)(2,1)}, u32[]{:S(2)}) copy-start(bf16[2,4,16,16,128]{4,3,2,1,0:T(8,128)(2,1)} %weight.2) | copy-start | bytes 1572868
  22.5 33.2 %copy-start.3 = (bf16[256,256]{1,0:T(8,128)(2,1)S(1)}, bf16[256,256]{1,0:T(8,128)(2,1)}, u32[]{:S(2)}) copy-start(bf16[256,256]{1,0:T(8,128)(2,1)} %constant.36.clone.x_table) | copy-start | bytes 393220
  57.4 8.5 %copy-start.6 = (f32[16,16]{1,0:T(8,128)S(1)}, f32[16,16]{1,0:T(8,128)}, u32[]{:S(2)}) copy-start(f32[16,16]{1,0:T(8,128)} %weight.3) | copy-start | bytes 3076
  57.4 8.5 %copy-start.10 = (f32[16]{0:T(128)S(1)}, f32[16]{0:T(128)}, u32[]{:S(2)}) copy-start(f32[16]{0:T(128)} %bias.1) | copy-start | bytes 196
  57.4 25.6 %all-to-all-start.2 = ((f32[512,1,128]{2,1,0:T(1,128)}), f32[512,1,128]{2,1,0:T(1,128)S(1)}, u32[]{:S(2)}, u32[]{:S(2)}) async-start(f32[512,1,128]{2,1,0:T(1,128)} %bitcast.10), calls=%async_computation.2 | async-start | bytes 524288 | tf_op jit(solution)/shard_map/all_to_all | solution.py:422
  65.9 17.1 %copy-start.1 = (bf16[256,512]{1,0:T(8,128)(2,1)S(1)}, bf16[256,512]{1,0:T(8,128)(2,1)}, u32[]{:S(2)}) copy-start(bf16[256,512]{1,0:T(8,128)(2,1)} %constant.35.clone.y_far.y_table) | copy-start | bytes 786436
  65.9 17.1 %copy-start.4 = (bf16[512,256]{1,0:T(8,128)(2,1)S(1)}, bf16[512,256]{1,0:T(8,128)(2,1)}, u32[]{:S(2)}) copy-start(bf16[512,256]{1,0:T(8,128)(2,1)} %constant.37.clone.z_table) | copy-start | bytes 786436
  85.8 11.1 %copy-start = (f32[1,8,16,256]{3,2,1,0:T(8,128)S(1)}, f32[1,8,16,256]{3,2,1,0:T(8,128)}, u32[]{:S(2)}) copy-start(f32[1,8,16,256]{3,2,1,0:T(8,128)} %param.11) | copy-start | bytes 393220
  97.1 5.7 %collective-permute-start = (f32[80,128]{1,0:T(8,128)S(1)}, f32[80,128]{1,0:T(8,128)S(1)}, u32[]{:S(2)}, u32[]{:S(2)}) collective-permute-start(f32[80,128]{1,0:T(8,128)S(1)} %get-tuple-element.62), channel_id=1, source_target_pairs={{16,32},{32,16},{48,64},{64,48},{80,96},{96,80},{112,128},{128,112... | collective-permute-start | bytes 122888 | tf_op jit(solution)/shard_map/ppermute | solution.py:498
  97.7 6.2 %collective-permute-start.1 = (f32[80,128]{1,0:T(8,128)S(1)}, f32[80,128]{1,0:T(8,128)S(1)}, u32[]{:S(2)}, u32[]{:S(2)}) collective-permute-start(f32[80,128]{1,0:T(8,128)S(1)} %get-tuple-element.63), channel_id=1, source_target_pairs={{0,16},{16,0},{32,48},{48,32},{64,80},{80,64},{96,112},{112,96},{1... | collective-permute-start | bytes 122888 | tf_op jit(solution)/shard_map/ppermute | solution.py:499
  104.2 12.6 %copy-start.5 = (bf16[256,256]{1,0:T(8,128)(2,1)S(1)}, bf16[256,256]{1,0:T(8,128)(2,1)}, u32[]{:S(2)}) copy-start(bf16[256,256]{1,0:T(8,128)(2,1)} %constant.34.clone.z_far.z_table) | copy-start | bytes 393220

commit v6 on v5

--- a/solution.py
+++ b/solution.py
@@ -157,41 +157,42 @@
     copy.wait()
 
 
-def ready_kernel(place, scale, shift, readout, z_far, y_far, z_table, y_table, scalars, ring, doubling, sems):
-    copies = [pltpu.make_async_copy(z_far, z_table, sems.at[0]), pltpu.make_async_copy(y_far, y_table, sems.at[1])]
+def first_kernel(
+    far_field, far_z, far_y, far_scale, far_shift, far_readout, spread, z_table, y_table, scalars, ring, doubling, *scratch
+):
+    scale, shift, readout, sems = scratch
+    core, row_place, col_place = lax.axis_index("core"), lax.axis_index(ROW), lax.axis_index(COL)
+    pairs = [(far_scale, scale), (far_shift, shift), (far_readout, readout), (far_z, z_table), (far_y, y_table)]
+    pairs += [(far_field, spread.at[:, k]) for k in range(2)]
+    copies = [pltpu.make_async_copy(source, target, sems.at[n]) for n, (source, target) in enumerate(pairs)]
     for copy in copies:
         copy.start()
-    first = place[0] * HALF
+    row = lax.broadcasted_iota(jnp.int32, (24, GRID), 0)
+    first_row = jnp.where(col_place == 0, 4, 3)
+    last_row = jnp.where(col_place == COLS - 1, 19, 20)
+    ring[0:24, :] = jnp.where(jnp.logical_and(row >= first_row, row <= last_row), 1.0, 0.0).astype(F32)
+    row = lax.broadcasted_iota(jnp.int32, (8, GRID), 0)
+    before, after = jnp.where(row_place > 0, 1.0, 0.0), jnp.where(row_place < ROWS - 1, 1.0, 0.0)
+    odd = jnp.where(row_place % 2 == 1, 1.0, 0.0)
+    ring[24:32, :] = jnp.where(row == 0, before, jnp.where(row == 1, after, odd)).astype(F32)
+    row = lax.broadcasted_iota(jnp.int32, (64, 128), 0)
+    zero_mode = jnp.logical_and((row // HALF) % 4 == 0, col_place == 0)
+    doubling[...] = jnp.where(zero_mode, 1.0, 2.0).astype(F32)
+    for copy in copies[:3]:
+        copy.wait()
+    first = core * HALF
     for n in range(HALF):
         for m, value in enumerate((0.5 * scale[first + n], 0.5 * shift[first + n], readout[first + n])):
             scalars[HALF * m + n : HALF * m + n + 1, :] = jnp.full((1, GRID), value, F32)
-    row = lax.broadcasted_iota(jnp.int32, (24, GRID), 0)
-    first_row = jnp.where(place[2] == 0, 4, 3)
-    last_row = jnp.where(place[2] == COLS - 1, 19, 20)
-    ring[0:24, :] = jnp.where(jnp.logical_and(row >= first_row, row <= last_row), 1.0, 0.0).astype(F32)
-    row = lax.broadcasted_iota(jnp.int32, (8, GRID), 0)
-    before, after = jnp.where(place[1] > 0, 1.0, 0.0), jnp.where(place[1] < ROWS - 1, 1.0, 0.0)
-    odd = jnp.where(place[1] % 2 == 1, 1.0, 0.0)
-    ring[24:32, :] = jnp.where(row == 0, before, jnp.where(row == 1, after, odd)).astype(F32)
-    row = lax.broadcasted_iota(jnp.int32, (64, 128), 0)
-    zero_mode = jnp.logical_and((row // HALF) % 4 == 0, place[2] == 0)
-    doubling[...] = jnp.where(zero_mode, 1.0, 2.0).astype(F32)
-    for copy in copies:
+    for copy in copies[3:]:
         copy.wait()
 
 
-def spread_kernel(field, out, sems):
-    copies = [pltpu.make_async_copy(field, out.at[:, k], sems.at[k]) for k in range(2)]
-    for copy in copies:
-        copy.start()
-    for copy in copies:
-        copy.wait()
-
-
-def local_kernel(place, scale, shift, bias, weight, plane, margin, *refs):
+def local_kernel(scale, shift, bias, weight, plane, margin, *refs):
     out, turned = refs[:HALF], refs[HALF]
-    first = place[0] * HALF
-    keep = jnp.where(place[0] == 0, 1.0, 0.0).astype(F32)
+    core = lax.axis_index("core")
+    first = core * HALF
+    keep = jnp.where(core == 0, 1.0, 0.0).astype(F32)
     turned[...] = plane[...].T
     margin[...] = jnp.zeros(margin.shape, F32)
     for c in range(1, COLS):
@@ -428,32 +429,27 @@
 
 def shards(right_side, lift_scale, lift_shift, spectral_weight, local_weight, local_bias, readout):
     z_forward, z_inverse, y_table, x_table = tables()
-    place = jnp.stack([lax.axis_index("core"), lax.axis_index(ROW), lax.axis_index(COL)]).astype(jnp.int32)
     everywhere = COL + ROW
     field = right_side[0]
-    copies = pltpu.SemaphoreType.DMA((2,))
     fields = [shape(GRID, GRID)] * HALF
 
-    spread = call(spread_kernel, (field,), (), shape(PLANES, 2, COLS, GRID), [copies], far=1)
-    plane = exchange(spread.reshape(COLS, COLS, GRID), COL)
-    near = call(
-        ready_kernel,
-        (z_forward, y_table),
-        (place, lift_scale, lift_shift, readout),
+    row_of = pltpu.SMEM((WIDTH,), F32)
+    spread, z_near, y_near, scalars, ring, doubling = call(
+        first_kernel,
+        (field, z_forward, y_table, lift_scale, lift_shift, readout),
+        (),
         [
+            shape(PLANES, 2, COLS, GRID),
             jax.ShapeDtypeStruct(z_forward.shape, BF16),
             jax.ShapeDtypeStruct(y_table.shape, BF16),
             shape(24, GRID),
             shape(32, GRID),
             shape(64, 128),
         ],
-        [copies],
-        flops=1 << 24,
-        far=2,
-    )
-    plane, near = lax.optimization_barrier((plane, near))
-    z_near, y_near, scalars, ring, doubling = near
-    plane = plane.reshape(GRID, GRID)
+        [row_of, row_of, row_of, pltpu.SemaphoreType.DMA((7,))],
+        far=6,
+    )
+    plane = exchange(spread.reshape(COLS, COLS, GRID), COL).reshape(GRID, GRID)
     line_scratch = pltpu.VMEM((MODES, HALF, 2 * GRID), F32)
     plane_scratch = [
         pltpu.VMEM((GRID, GRID), F32),
@@ -466,7 +462,7 @@
     margin, *local = call(
         local_kernel,
         (plane,),
-        (place, lift_scale, lift_shift, local_bias, local_weight),
+        (lift_scale, lift_shift, local_bias, local_weight),
         [shape(2 * COLS, GRID)] + fields,
         [pltpu.VMEM((GRID, GRID), F32)],
         flops=1 << 27,

time: 149 us -> 148 us (level)
  blocking collectives: 85.6 us -> 103 us
  starting transfers between devices: 24.2 us -> 13.8 us
  waiting for transfers between devices: 17.2 us -> 12.2 us
  Pallas kernels: 19.9 us -> 17.8 us
    all_to_all x4 -> x5, blocking collectives: 85.6 us -> 103 us  [exchange(): return lax.all_to_all(value, axes, split_axis=0, concat_axis=0, tiled=True)]
    all_to_all x2 -> x1, starting transfers between devices: 18.7 us -> 8.49 us  [exchange(): return lax.all_to_all(value, axes, split_axis=0, concat_axis=0, tiled=True)]
    all_to_all x2 -> x1, waiting for transfers between devices: 16 us -> 11.1 us  [exchange(): return lax.all_to_all(value, axes, split_axis=0, concat_axis=0, tiled=True)]
    pallas_call x11 -> x10, Pallas kernels: 19.9 us -> 17.8 us  [call(): pl.pallas_call(kernel, in_specs=[smem] * len(scalars) + [vmem] * (len(ope...]
  transfers between devices with their start and end apart: 4 -> 3, of which waited for: 3 -> 2; matrix products, arithmetic and copies ran while one was open for 0% -> 0% of each run, Pallas kernels for 5% -> 4%
where the time goes in v6:
time: 148 us
  blocking collectives  103 us (70%)
  Pallas kernels  17.8 us (12%)
  starting transfers between devices  13.8 us (9%)
  waiting for transfers between devices  12.2 us (8%)
    all_to_all x5, blocking collectives, exchange(): return lax.all_to_all(value, axes, split_axis=0, concat_axis=0, tiled=True)  103 us
    pallas_call x10, Pallas kernels, call(): pl.pallas_call(kernel, in_specs=[smem] * len(scalars) + [vmem] * (len(ope...  17.8 us
    all_to_all x1, waiting for transfers between devices, exchange(): return lax.all_to_all(value, axes, split_axis=0, concat_axis=0, tiled=True)  11.1 us
    all_to_all x1, starting transfers between devices, exchange(): return lax.all_to_all(value, axes, split_axis=0, concat_axis=0, tiled=True)  8.49 us
    ppermute x1, starting transfers between devices, shards(): second = lax.ppermute(second, ROW, even_pairs)  4.67 us
  transfers between devices with their start and end apart: 3, of which 2 were waited for; matrix products, arithmetic and copies ran while one was open for 0% of the time, Pallas kernels for 4%

profile of v6, /device:TPU:1, one launch (start us, length us, event | category | flops | bytes accessed | tf_op | source)
XLA Modules:
  0.0 147.7 jit_solution(10842157237560955369)
XLA Ops:
  0.6 1.2 shard_map.122
  1.8 16.5 %all_to_all.48 = f32[16,16,256]{2,1,0:T(8,128)S(1)} all-to-all(f32[16,16,256]{2,1,0:T(8,128)S(1)} %bitcast.28), channel_id=1, replica_groups=mesh['y'=8,'zh'=4,'zl'=2,'x'=4,'core'=2] {'zl','x','core'}, dimensions={0} | all-to-all | bytes 524288 | tf_op jit(solution)/shard_map/all_to_all | solution.py:423
  18.4 2.7 %shard_map.123 = f32[512,128]{1,0:T(8,128)S(1)} custom-call(f32[256,256]{1,0:T(8,128)S(1)} %bitcast.21, bf16[256,256]{1,0:T(8,128)(2,1)S(1)} %get-tuple-element.36.z_table, bf16[256,512]{1,0:T(8,128)(2,1)S(1)} %get-tuple-element.37.y_table, f32[24,256]{1,0:T(8,128)S(1)} %get-tuple-element.38.scalars), custom_call_target="tpu_custom_call" | custom-call | tf_op jit(solution)/shard_map/pallas_call | solution.py:411
  21.0 0.0 copy-start.4
  21.1 33.9 %all_to_all.49 = f32[512,1,128]{2,1,0:T(1,128)S(1)} all-to-all(f32[512,1,128]{2,1,0:T(1,128)S(1)} %bitcast.24), channel_id=1, replica_groups=mesh['y'=8,'zh'=4,'zl'=2,'x'=4,'core'=2] {'zl','x','core','y','zh'}, dimensions={0} | all-to-all | bytes 524288 | tf_op jit(solution)/shard_map/all_to_all | solution.py:423
  55.0 1.7 %shard_map.124 = (f32[512,128]{1,0:T(8,128)}, f32[2,64,128]{2,1,0:T(8,128)S(1)}) custom-call(f32[512,128]{1,0:T(8,128)S(1)} %bitcast.23, bf16[2,4,16,16,128]{4,3,2,1,0:T(8,128)(2,1)S(1)} %copy-done.3, bf16[256,256]{1,0:T(8,128)(2,1)S(1)} %copy-done.4), custom_call_target="tpu_custom_call" | custom-call | tf_op jit(solution)/shard_map/pallas_call | solution.py:411
  56.6 8.5 %all-to-all-start.2 = ((f32[512,1,128]{2,1,0:T(1,128)}), f32[512,1,128]{2,1,0:T(1,128)S(1)}, u32[]{:S(2)}, u32[]{:S(2)}) async-start(f32[512,1,128]{2,1,0:T(1,128)} %bitcast.7), calls=%async_computation.2 | async-start | bytes 524288 | tf_op jit(solution)/shard_map/all_to_all | solution.py:423
  65.2 0.0 copy-start
  65.2 0.0 copy-start.5
  65.2 6.0 %shard_map.125 = (f32[32,256]{1,0:T(8,128)S(1)}, f32[256,256]{1,0:T(8,128)S(1)}, f32[256,256]{1,0:T(8,128)S(1)}, f32[256,256]{1,0:T(8,128)S(1)}, f32[256,256]{1,...) custom-call(f32[16]{0:T(128)S(1)} %copy-done.6, ...), custom_call_target="tpu_custom_call" | custom-call | flops 134217728 | bytes 4194304 | tf_op jit(solution)/shard_map/pallas_call | solution.py:411
  71.2 11.1 %all-to-all-done.2 = f32[512,1,128]{2,1,0:T(1,128)S(1)} async-done(((f32[512,1,128]{2,1,0:T(1,128)}), f32[512,1,128]{2,1,0:T(1,128)S(1)}, u32[]{:S(2)}, u32[]{:S(2)}) %all-to-all-start.2) | async-done | bytes 262176 | tf_op jit(solution)/shard_map/all_to_all | solution.py:423
  82.2 2.9 %shard_map.126 = (f32[16,40,128]{2,1,0:T(8,128)S(1)}, f32[256,256]{1,0:T(8,128)S(1)}, f32[256,256]{1,0:T(8,128)S(1)}, f32[256,256]{1,0:T(8,128)S(1)}, f32[256,25...) custom-call(f32[512,128]{1,0:T(8,128)S(1)} %bitcast.20, ...), custom_call_target="tpu_custom_call" | custom-call | tf_op jit(solution)/shard_map/pallas_call | solution.py:411
  85.1 11.1 %all_to_all.50.received = f32[16,40,128]{2,1,0:T(8,128)S(1)} all-to-all(f32[16,40,128]{2,1,0:T(8,128)S(1)} %get-tuple-element.49), channel_id=1, replica_groups=mesh['y'=8,'zh'=4,'zl'=2,'x'=4,'core'=2] {'zl','x','core'}, dimensions={0} | all-to-all | bytes 655360 | tf_op jit(solution)/shard_map/all_to_all | solution.py:423
  96.2 0.1 shard_map.127
  96.4 0.7 collective-permute-start
  97.0 4.7 %collective-permute-start.1 = (f32[80,128]{1,0:T(8,128)S(1)}, f32[80,128]{1,0:T(8,128)S(1)}, u32[]{:S(2)}, u32[]{:S(2)}) collective-permute-start(f32[80,128]{1,0:T(8,128)S(1)} %get-tuple-element.53), channel_id=1, source_target_pairs={{0,16},{16,0},{32,48},{48,32},{64,80},{80,64},{96,112},{112,96},{1... | collective-permute-start | bytes 122888 | tf_op jit(solution)/shard_map/ppermute | solution.py:495
  101.7 0.2 shard_map.128.rest
  101.9 1.2 collective-permute-done.1.second
  103.1 0.2 shard_map.129
  103.3 0.0 copy-start.2
  103.3 12.5 %all_to_all.51 = f32[16,16,256]{2,1,0:T(8,128)S(1)} all-to-all(f32[16,16,256]{2,1,0:T(8,128)S(1)} %get-tuple-element.54), channel_id=1, replica_groups=mesh['y'=8,'zh'=4,'zl'=2,'x'=4,'core'=2] {'zl','x','core'}, dimensions={0} | all-to-all | bytes 524288 | tf_op jit(solution)/shard_map/all_to_all | solution.py:423
  115.8 1.6 %shard_map.130 = (f32[512,128]{1,0:T(8,128)S(1)}, f32[8,16,256]{2,1,0:T(8,128)}) custom-call(f32[256,256]{1,0:T(8,128)S(1)} %bitcast.26, f32[8,16,256]{2,1,0:T(8,128)S(1)} %get-tuple-element.55.rest, bf16[256,256]{1,0:T(8,128)(2,1)S(1)} %copy-done.2, bf16[256,512]{1,0:T(8,128)(2,1)S(1)} %copy-done, f32[256,256]{1,0:T(8,128)S(1)} %get-tuple-element.56.refs_0_, ...), custom_call_target="tpu_custom_call" | custom-call | tf_op jit(solution)/shard_map/pallas_call | solution.py:411
  117.5 28.7 %all_to_all.52 = f32[512,1,128]{2,1,0:T(1,128)S(1)} all-to-all(f32[512,1,128]{2,1,0:T(1,128)S(1)} %bitcast.27), channel_id=1, replica_groups=mesh['y'=8,'zh'=4,'zl'=2,'x'=4,'core'=2] {'zl','x','core','y','zh'}, dimensions={0} | all-to-all | bytes 524288 | tf_op jit(solution)/shard_map/all_to_all | solution.py:423
  146.2 1.3 shard_map.131
  (17 shorter events, 0.0 us)
Async XLA Ops:
  18.4 36.6 %copy-start.3 = (bf16[2,4,16,16,128]{4,3,2,1,0:T(8,128)(2,1)S(1)}, bf16[2,4,16,16,128]{4,3,2,1,0:T(8,128)(2,1)}, u32[]{:S(2)}) copy-start(bf16[2,4,16,16,128]{4,3,2,1,0:T(8,128)(2,1)} %weight.2) | copy-start | bytes 1572868
  21.0 33.9 %copy-start.4 = (bf16[256,256]{1,0:T(8,128)(2,1)S(1)}, bf16[256,256]{1,0:T(8,128)(2,1)}, u32[]{:S(2)}) copy-start(bf16[256,256]{1,0:T(8,128)(2,1)} %constant.10.clone.x_table) | copy-start | bytes 393220
  56.6 8.5 %copy-start.6 = (f32[16]{0:T(128)S(1)}, f32[16]{0:T(128)}, u32[]{:S(2)}) copy-start(f32[16]{0:T(128)} %scale.1) | copy-start | bytes 196
  56.6 8.5 %copy-start.7 = (f32[16]{0:T(128)S(1)}, f32[16]{0:T(128)}, u32[]{:S(2)}) copy-start(f32[16]{0:T(128)} %shift.1) | copy-start | bytes 196
  56.6 8.5 %copy-start.8 = (f32[16,16]{1,0:T(8,128)S(1)}, f32[16,16]{1,0:T(8,128)}, u32[]{:S(2)}) copy-start(f32[16,16]{1,0:T(8,128)} %weight.3) | copy-start | bytes 3076
  56.6 8.5 %copy-start.9 = (f32[16]{0:T(128)S(1)}, f32[16]{0:T(128)}, u32[]{:S(2)}) copy-start(f32[16]{0:T(128)} %bias.1) | copy-start | bytes 196
  56.6 25.6 %all-to-all-start.2 = ((f32[512,1,128]{2,1,0:T(1,128)}), f32[512,1,128]{2,1,0:T(1,128)S(1)}, u32[]{:S(2)}, u32[]{:S(2)}) async-start(f32[512,1,128]{2,1,0:T(1,128)} %bitcast.7), calls=%async_computation.2 | async-start | bytes 524288 | tf_op jit(solution)/shard_map/all_to_all | solution.py:423
  65.2 17.1 %copy-start = (bf16[256,512]{1,0:T(8,128)(2,1)S(1)}, bf16[256,512]{1,0:T(8,128)(2,1)}, u32[]{:S(2)}) copy-start(bf16[256,512]{1,0:T(8,128)(2,1)} %constant.9.clone.far_y.y_table) | copy-start | bytes 786436
  65.2 17.1 %copy-start.5 = (bf16[512,256]{1,0:T(8,128)(2,1)S(1)}, bf16[512,256]{1,0:T(8,128)(2,1)}, u32[]{:S(2)}) copy-start(bf16[512,256]{1,0:T(8,128)(2,1)} %constant.11.clone.z_table) | copy-start | bytes 786436
  85.1 11.1 %copy-start.1 = (f32[1,8,16,256]{3,2,1,0:T(8,128)S(1)}, f32[1,8,16,256]{3,2,1,0:T(8,128)}, u32[]{:S(2)}) copy-start(f32[1,8,16,256]{3,2,1,0:T(8,128)} %param.11) | copy-start | bytes 393220
  96.4 5.6 %collective-permute-start = (f32[80,128]{1,0:T(8,128)S(1)}, f32[80,128]{1,0:T(8,128)S(1)}, u32[]{:S(2)}, u32[]{:S(2)}) collective-permute-start(f32[80,128]{1,0:T(8,128)S(1)} %get-tuple-element.52), channel_id=1, source_target_pairs={{16,32},{32,16},{48,64},{64,48},{80,96},{96,80},{112,128},{128,112... | collective-permute-start | bytes 122888 | tf_op jit(solution)/shard_map/ppermute | solution.py:494
  97.0 6.1 %collective-permute-start.1 = (f32[80,128]{1,0:T(8,128)S(1)}, f32[80,128]{1,0:T(8,128)S(1)}, u32[]{:S(2)}, u32[]{:S(2)}) collective-permute-start(f32[80,128]{1,0:T(8,128)S(1)} %get-tuple-element.53), channel_id=1, source_target_pairs={{0,16},{16,0},{32,48},{48,32},{64,80},{80,64},{96,112},{112,96},{1... | collective-permute-start | bytes 122888 | tf_op jit(solution)/shard_map/ppermute | solution.py:495
  103.3 12.6 %copy-start.2 = (bf16[256,256]{1,0:T(8,128)(2,1)S(1)}, bf16[256,256]{1,0:T(8,128)(2,1)}, u32[]{:S(2)}) copy-start(bf16[256,256]{1,0:T(8,128)(2,1)} %constant.8.clone.far_z.z_table) | copy-start | bytes 393220

commit v7 on v6

--- a/solution.py
+++ b/solution.py
@@ -70,18 +70,15 @@
 CUBE = 0.044715
 
 
-def gelu(value):
-    inner = value * (ROOT + (ROOT * CUBE) * (value * value))
-    half = 0.5 * value
-    return half + half * jnp.tanh(inner)
-
-
-def gelu_both(value):
+def gelu_double(value, square):
+    return 1.0 + jnp.tanh(value * (ROOT + (ROOT * CUBE) * square))
+
+
+def gelu_slope(value):
     square = value * value
-    bent = jnp.tanh(value * (ROOT + (ROOT * CUBE) * square))
-    slope = ROOT + (3.0 * ROOT * CUBE) * square
-    cdf = 0.5 + 0.5 * bent
-    return value * cdf, cdf + (0.5 * value) * ((1.0 - bent * bent) * slope)
+    double = gelu_double(value, square)
+    slope = (0.5 * ROOT) + (1.5 * ROOT * CUBE) * square
+    return double * (0.5 + (value * slope) * (2.0 - double))
 
 
 def bent_half(half):
@@ -214,7 +211,7 @@
 
 
 def inverse_kernel(received, margin, z_table, y_table, scalars, *refs):
-    local, out, slope = refs[:HALF], refs[HALF], refs[HALF + 1 : 2 * HALF + 1]
+    local, out, preact = refs[:HALF], refs[HALF], refs[HALF + 1 : 2 * HALF + 1]
     grid, lines, spectral, total, padded = refs[2 * HALF + 1 :]
     lane = lane_index((ROWS, 128)) // 32
     for tile in range(4):
@@ -233,16 +230,16 @@
         modes = jnp.concatenate([lines[:, o, 0:GRID], lines[:, o, GRID:]], axis=0)
         product = dot(z_table[...], jnp.concatenate(split(modes), axis=0), NN)
         spectral[...] = product[:GRID] + product[GRID:]
-        read = scalars[2 * HALF + o : 2 * HALF + o + 1, :]
+        read = 0.5 * scalars[2 * HALF + o : 2 * HALF + o + 1, :]
         for t in range(8):
             rows = slice(32 * t, 32 * t + 32)
             value = spectral[rows, :] + local[o][rows, :]
-            value, derivative = gelu_both(value)
-            slope[o][rows, :] = read * derivative
+            preact[o][rows, :] = value
+            term = (read * value) * gelu_double(value, value * value)
             if o == 0:
-                total[rows, :] = read * value
+                total[rows, :] = term
             else:
-                total[rows, :] += read * value
+                total[rows, :] += term
     padded[0:8, :] = jnp.zeros((8, GRID), F32)
     padded[256:264, :] = jnp.zeros((8, GRID), F32)
     value = total[...].T
@@ -261,6 +258,15 @@
             out[c, 20 * h : 20 * h + 1, :] = before[:, lanes]
             out[c, 20 * h + 1 : 20 * h + 19, :] = padded[16 * c + 3 : 16 * c + 21, lanes]
             out[c, 20 * h + 19 : 20 * h + 20, :] = after[:, lanes]
+
+
+def slope_kernel(scalars, *refs):
+    preact, out = refs[:HALF], refs[HALF:]
+    for o in range(HALF):
+        read = scalars[2 * HALF + o : 2 * HALF + o + 1, :]
+        for t in range(8):
+            rows = slice(32 * t, 32 * t + 32)
+            out[o][rows, :] = read * gelu_slope(preact[o][rows, :])
 
 
 def gather_spectra(received, x_table, sign):
@@ -398,7 +404,7 @@
         adjoint[2 * q + 1] = value
 
 
-def call(kernel, operands, scalars, outputs, scratch, flops=0, far=0, far_out=()):
+def call(kernel, operands, scalars, outputs, scratch, flops=0, far=0, far_out=(), aliases=None):
     many = isinstance(outputs, list)
     vmem = pl.BlockSpec(memory_space=pltpu.VMEM)
     smem = pl.BlockSpec(memory_space=pltpu.SMEM)
@@ -414,6 +420,7 @@
         out_specs=out_specs if many else out_specs[0],
         out_shape=outputs,
         scratch_shapes=scratch,
+        input_output_aliases=aliases or {},
         compiler_params=pltpu.CompilerParams(vmem_limit_bytes=VMEM_LIMIT),
         cost_estimate=cost if flops else None,
     )(*scalars, *operands)
@@ -472,7 +479,7 @@
         mix_kernel, (lifted, spectral_weight, x_table), (), [shape(512, 128), shape(2, 64, 128)], [pair, pair]
     )
     mixed = exchange(mixed, everywhere)
-    message, *slope = call(
+    message, *preact = call(
         inverse_kernel,
         (mixed, margin, z_inverse, y_table, scalars, *local),
         (),
@@ -501,6 +508,9 @@
         [],
         flops=1 << 22,
     )
+    aliases = {1 + o: o for o in range(HALF)}
+    slope = call(slope_kernel, (scalars, *preact), (), fields, [], flops=1 << 25, aliases=aliases)
+    first, second, slope = lax.optimization_barrier((first, second, slope))
     rest, adjoint = call(
         stencil_kernel,
         (rest, wide, first, second, ring),

time: 148 us -> 147 us (level)
    pallas_call x10 -> x11, Pallas kernels: 17.8 us -> 18.5 us  [call(): pl.pallas_call(kernel, in_specs=[smem] * len(scalars) + [vmem] * (len(ope...]
  transfers between devices with their start and end apart: 3 -> 3, of which waited for: 2 -> 1; matrix products, arithmetic and copies ran while one was open for 0% -> 0% of each run, Pallas kernels for 4% -> 5%
where the time goes in v7:
time: 147 us
  blocking collectives  102 us (69%)
  Pallas kernels  18.5 us (13%)
  starting transfers between devices  14 us (10%)
  waiting for transfers between devices  11.1 us (8%)
    all_to_all x5, blocking collectives, exchange(): return lax.all_to_all(value, axes, split_axis=0, concat_axis=0, tiled=True)  102 us
    pallas_call x11, Pallas kernels, call(): pl.pallas_call(kernel, in_specs=[smem] * len(scalars) + [vmem] * (len(ope...  18.5 us
    all_to_all x1, waiting for transfers between devices, exchange(): return lax.all_to_all(value, axes, split_axis=0, concat_axis=0, tiled=True)  11.1 us
    all_to_all x1, starting transfers between devices, exchange(): return lax.all_to_all(value, axes, split_axis=0, concat_axis=0, tiled=True)  8.49 us
    ppermute x1, starting transfers between devices, shards(): second = lax.ppermute(second, ROW, even_pairs)  4.86 us
  transfers between devices with their start and end apart: 3, of which 1 were waited for; matrix products, arithmetic and copies ran while one was open for 0% of the time, Pallas kernels for 5%

profile of v7, /device:TPU:1, one launch (start us, length us, event | category | flops | bytes accessed | tf_op | source)
XLA Modules:
  0.0 147.0 jit_solution(2520235730611815268)
XLA Ops:
  0.6 1.2 shard_map.122
  1.8 16.5 %all_to_all.48 = f32[16,16,256]{2,1,0:T(8,128)S(1)} all-to-all(f32[16,16,256]{2,1,0:T(8,128)S(1)} %bitcast.28), channel_id=1, replica_groups=mesh['y'=8,'zh'=4,'zl'=2,'x'=4,'core'=2] {'zl','x','core'}, dimensions={0} | all-to-all | bytes 524288 | tf_op jit(solution)/shard_map/all_to_all | solution.py:430
  18.4 2.7 %shard_map.123 = f32[512,128]{1,0:T(8,128)S(1)} custom-call(f32[256,256]{1,0:T(8,128)S(1)} %bitcast.21, bf16[256,256]{1,0:T(8,128)(2,1)S(1)} %get-tuple-element.54.z_table, bf16[256,512]{1,0:T(8,128)(2,1)S(1)} %get-tuple-element.55.y_table, f32[24,256]{1,0:T(8,128)S(1)} %get-tuple-element.56.scalars), custom_call_target="tpu_custom_call" | custom-call | tf_op jit(solution)/shard_map/pallas_call | solution.py:417
  21.0 0.0 copy-start.4
  21.1 33.9 %all_to_all.49 = f32[512,1,128]{2,1,0:T(1,128)S(1)} all-to-all(f32[512,1,128]{2,1,0:T(1,128)S(1)} %bitcast.24), channel_id=1, replica_groups=mesh['y'=8,'zh'=4,'zl'=2,'x'=4,'core'=2] {'zl','x','core','y','zh'}, dimensions={0} | all-to-all | bytes 524288 | tf_op jit(solution)/shard_map/all_to_all | solution.py:430
  55.0 1.7 %shard_map.124 = (f32[512,128]{1,0:T(8,128)}, f32[2,64,128]{2,1,0:T(8,128)S(1)}) custom-call(f32[512,128]{1,0:T(8,128)S(1)} %bitcast.23, bf16[2,4,16,16,128]{4,3,2,1,0:T(8,128)(2,1)S(1)} %copy-done.3, bf16[256,256]{1,0:T(8,128)(2,1)S(1)} %copy-done.4), custom_call_target="tpu_custom_call" | custom-call | tf_op jit(solution)/shard_map/pallas_call | solution.py:417
  56.6 8.5 %all-to-all-start.2 = ((f32[512,1,128]{2,1,0:T(1,128)}), f32[512,1,128]{2,1,0:T(1,128)S(1)}, u32[]{:S(2)}, u32[]{:S(2)}) async-start(f32[512,1,128]{2,1,0:T(1,128)} %bitcast.7), calls=%async_computation.2 | async-start | bytes 524288 | tf_op jit(solution)/shard_map/all_to_all | solution.py:430
  65.2 0.0 copy-start
  65.2 0.0 copy-start.5
  65.2 6.0 %shard_map.125 = (f32[32,256]{1,0:T(8,128)S(1)}, f32[256,256]{1,0:T(8,128)S(1)}, f32[256,256]{1,0:T(8,128)S(1)}, f32[256,256]{1,0:T(8,128)S(1)}, f32[256,256]{1,...) custom-call(f32[16]{0:T(128)S(1)} %copy-done.6, ...), custom_call_target="tpu_custom_call" | custom-call | flops 134217728 | bytes 4194304 | tf_op jit(solution)/shard_map/pallas_call | solution.py:417
  71.2 11.1 %all-to-all-done.2 = f32[512,1,128]{2,1,0:T(1,128)S(1)} async-done(((f32[512,1,128]{2,1,0:T(1,128)}), f32[512,1,128]{2,1,0:T(1,128)S(1)}, u32[]{:S(2)}, u32[]{:S(2)}) %all-to-all-start.2) | async-done | bytes 262176 | tf_op jit(solution)/shard_map/all_to_all | solution.py:430
  82.2 2.2 %shard_map.126 = (f32[16,40,128]{2,1,0:T(8,128)S(1)}, f32[256,256]{1,0:T(8,128)S(1)}, f32[256,256]{1,0:T(8,128)S(1)}, f32[256,256]{1,0:T(8,128)S(1)}, f32[256,25...) custom-call(f32[512,128]{1,0:T(8,128)S(1)} %bitcast.20, ...), custom_call_target="tpu_custom_call" | custom-call | tf_op jit(solution)/shard_map/pallas_call | solution.py:417
  84.4 11.1 %all_to_all.50.received = f32[16,40,128]{2,1,0:T(8,128)S(1)} all-to-all(f32[16,40,128]{2,1,0:T(8,128)S(1)} %get-tuple-element.67), channel_id=1, replica_groups=mesh['y'=8,'zh'=4,'zl'=2,'x'=4,'core'=2] {'zl','x','core'}, dimensions={0} | all-to-all | bytes 655360 | tf_op jit(solution)/shard_map/all_to_all | solution.py:430
  95.5 0.1 shard_map.127
  95.7 0.7 collective-permute-start
  96.3 4.9 %collective-permute-start.1 = (f32[80,128]{1,0:T(8,128)S(1)}, f32[80,128]{1,0:T(8,128)S(1)}, u32[]{:S(2)}, u32[]{:S(2)}) collective-permute-start(f32[80,128]{1,0:T(8,128)S(1)} %get-tuple-element.71), channel_id=1, source_target_pairs={{0,16},{16,0},{32,48},{48,32},{64,80},{80,64},{96,112},{112,96},{1... | collective-permute-start | bytes 122888 | tf_op jit(solution)/shard_map/ppermute | solution.py:502
  101.2 1.4 shard_map.129
  102.6 0.2 shard_map.128.rest
  102.8 0.2 shard_map.130
  103.0 0.0 copy-start.2
  103.0 12.1 %all_to_all.51 = f32[16,16,256]{2,1,0:T(8,128)S(1)} all-to-all(f32[16,16,256]{2,1,0:T(8,128)S(1)} %get-tuple-element.90), channel_id=1, replica_groups=mesh['y'=8,'zh'=4,'zl'=2,'x'=4,'core'=2] {'zl','x','core'}, dimensions={0} | all-to-all | bytes 524288 | tf_op jit(solution)/shard_map/all_to_all | solution.py:430
  115.1 1.6 %shard_map.131 = (f32[512,128]{1,0:T(8,128)S(1)}, f32[8,16,256]{2,1,0:T(8,128)}) custom-call(f32[256,256]{1,0:T(8,128)S(1)} %bitcast.26, f32[8,16,256]{2,1,0:T(8,128)S(1)} %get-tuple-element.91.rest, bf16[256,256]{1,0:T(8,128)(2,1)S(1)} %copy-done.2, bf16[256,512]{1,0:T(8,128)(2,1)S(1)} %copy-done, f32[256,256]{1,0:T(8,128)S(1)} %get-tuple-element.92.refs_0_, ...), custom_call_target="tpu_custom_call" | custom-call | tf_op jit(solution)/shard_map/pallas_call | solution.py:417
  116.8 28.7 %all_to_all.52 = f32[512,1,128]{2,1,0:T(1,128)S(1)} all-to-all(f32[512,1,128]{2,1,0:T(1,128)S(1)} %bitcast.27), channel_id=1, replica_groups=mesh['y'=8,'zh'=4,'zl'=2,'x'=4,'core'=2] {'zl','x','core','y','zh'}, dimensions={0} | all-to-all | bytes 524288 | tf_op jit(solution)/shard_map/all_to_all | solution.py:430
  145.5 1.3 shard_map.132
  (18 shorter events, 0.0 us)
Async XLA Ops:
  18.4 36.6 %copy-start.3 = (bf16[2,4,16,16,128]{4,3,2,1,0:T(8,128)(2,1)S(1)}, bf16[2,4,16,16,128]{4,3,2,1,0:T(8,128)(2,1)}, u32[]{:S(2)}) copy-start(bf16[2,4,16,16,128]{4,3,2,1,0:T(8,128)(2,1)} %weight.2) | copy-start | bytes 1572868
  21.0 33.9 %copy-start.4 = (bf16[256,256]{1,0:T(8,128)(2,1)S(1)}, bf16[256,256]{1,0:T(8,128)(2,1)}, u32[]{:S(2)}) copy-start(bf16[256,256]{1,0:T(8,128)(2,1)} %constant.10.clone.x_table) | copy-start | bytes 393220
  56.6 8.5 %copy-start.6 = (f32[16]{0:T(128)S(1)}, f32[16]{0:T(128)}, u32[]{:S(2)}) copy-start(f32[16]{0:T(128)} %scale.1) | copy-start | bytes 196
  56.6 8.5 %copy-start.7 = (f32[16]{0:T(128)S(1)}, f32[16]{0:T(128)}, u32[]{:S(2)}) copy-start(f32[16]{0:T(128)} %shift.1) | copy-start | bytes 196
  56.6 8.5 %copy-start.8 = (f32[16,16]{1,0:T(8,128)S(1)}, f32[16,16]{1,0:T(8,128)}, u32[]{:S(2)}) copy-start(f32[16,16]{1,0:T(8,128)} %weight.3) | copy-start | bytes 3076
  56.6 8.5 %copy-start.9 = (f32[16]{0:T(128)S(1)}, f32[16]{0:T(128)}, u32[]{:S(2)}) copy-start(f32[16]{0:T(128)} %bias.1) | copy-start | bytes 196
  56.6 25.6 %all-to-all-start.2 = ((f32[512,1,128]{2,1,0:T(1,128)}), f32[512,1,128]{2,1,0:T(1,128)S(1)}, u32[]{:S(2)}, u32[]{:S(2)}) async-start(f32[512,1,128]{2,1,0:T(1,128)} %bitcast.7), calls=%async_computation.2 | async-start | bytes 524288 | tf_op jit(solution)/shard_map/all_to_all | solution.py:430
  65.2 17.1 %copy-start = (bf16[256,512]{1,0:T(8,128)(2,1)S(1)}, bf16[256,512]{1,0:T(8,128)(2,1)}, u32[]{:S(2)}) copy-start(bf16[256,512]{1,0:T(8,128)(2,1)} %constant.9.clone.far_y.y_table) | copy-start | bytes 786436
  65.2 17.1 %copy-start.5 = (bf16[512,256]{1,0:T(8,128)(2,1)S(1)}, bf16[512,256]{1,0:T(8,128)(2,1)}, u32[]{:S(2)}) copy-start(bf16[512,256]{1,0:T(8,128)(2,1)} %constant.11.clone.z_table) | copy-start | bytes 786436
  84.4 11.1 %copy-start.1 = (f32[1,8,16,256]{3,2,1,0:T(8,128)S(1)}, f32[1,8,16,256]{3,2,1,0:T(8,128)}, u32[]{:S(2)}) copy-start(f32[1,8,16,256]{3,2,1,0:T(8,128)} %param.11) | copy-start | bytes 393220
  95.7 7.1 %collective-permute-start = (f32[80,128]{1,0:T(8,128)S(1)}, f32[80,128]{1,0:T(8,128)S(1)}, u32[]{:S(2)}, u32[]{:S(2)}) collective-permute-start(f32[80,128]{1,0:T(8,128)S(1)} %get-tuple-element.70), channel_id=1, source_target_pairs={{16,32},{32,16},{48,64},{64,48},{80,96},{96,80},{112,128},{128,112... | collective-permute-start | bytes 122888 | tf_op jit(solution)/shard_map/ppermute | solution.py:501
  96.3 6.4 %collective-permute-start.1 = (f32[80,128]{1,0:T(8,128)S(1)}, f32[80,128]{1,0:T(8,128)S(1)}, u32[]{:S(2)}, u32[]{:S(2)}) collective-permute-start(f32[80,128]{1,0:T(8,128)S(1)} %get-tuple-element.71), channel_id=1, source_target_pairs={{0,16},{16,0},{32,48},{48,32},{64,80},{80,64},{96,112},{112,96},{1... | collective-permute-start | bytes 122888 | tf_op jit(solution)/shard_map/ppermute | solution.py:502
  103.0 12.2 %copy-start.2 = (bf16[256,256]{1,0:T(8,128)(2,1)S(1)}, bf16[256,256]{1,0:T(8,128)(2,1)}, u32[]{:S(2)}) copy-start(bf16[256,256]{1,0:T(8,128)(2,1)} %constant.8.clone.far_z.z_table) | copy-start | bytes 393220

commit v8 on v7

--- a/solution.py
+++ b/solution.py
@@ -155,11 +155,31 @@
 
 
 def first_kernel(
-    far_field, far_z, far_y, far_scale, far_shift, far_readout, spread, z_table, y_table, scalars, ring, doubling, *scratch
+    far_field,
+    far_z,
+    far_y,
+    far_scale,
+    far_shift,
+    far_readout,
+    far_bias,
+    far_weight,
+    spread,
+    z_table,
+    y_table,
+    scalars,
+    factors,
+    ring,
+    doubling,
+    scale,
+    shift,
+    readout,
+    bias,
+    weight,
+    sems,
 ):
-    scale, shift, readout, sems = scratch
     core, row_place, col_place = lax.axis_index("core"), lax.axis_index(ROW), lax.axis_index(COL)
-    pairs = [(far_scale, scale), (far_shift, shift), (far_readout, readout), (far_z, z_table), (far_y, y_table)]
+    pairs = [(far_scale, scale), (far_shift, shift), (far_readout, readout), (far_bias, bias), (far_weight, weight)]
+    pairs += [(far_z, z_table), (far_y, y_table)]
     pairs += [(far_field, spread.at[:, k]) for k in range(2)]
     copies = [pltpu.make_async_copy(source, target, sems.at[n]) for n, (source, target) in enumerate(pairs)]
     for copy in copies:
@@ -175,21 +195,27 @@
     row = lax.broadcasted_iota(jnp.int32, (64, 128), 0)
     zero_mode = jnp.logical_and((row // HALF) % 4 == 0, col_place == 0)
     doubling[...] = jnp.where(zero_mode, 1.0, 2.0).astype(F32)
-    for copy in copies[:3]:
+    for copy in copies[:5]:
         copy.wait()
     first = core * HALF
     for n in range(HALF):
         for m, value in enumerate((0.5 * scale[first + n], 0.5 * shift[first + n], readout[first + n])):
             scalars[HALF * m + n : HALF * m + n + 1, :] = jnp.full((1, GRID), value, F32)
-    for copy in copies[3:]:
+    for i in range(WIDTH):
+        factors[i : i + 1, :] = jnp.full((1, 128), 0.5 * scale[i], F32)
+        factors[WIDTH + i : WIDTH + i + 1, :] = jnp.full((1, 128), 0.5 * shift[i], F32)
+        for o in range(HALF):
+            row = 40 + HALF * i + o
+            factors[row : row + 1, :] = jnp.full((1, 128), weight[i, first + o], F32)
+    for o in range(HALF):
+        factors[32 + o : 33 + o, :] = jnp.full((1, 128), bias[first + o], F32)
+    for copy in copies[5:]:
         copy.wait()
 
 
-def local_kernel(scale, shift, bias, weight, plane, margin, *refs):
+def local_kernel(plane, factors, margin, *refs):
     out, turned = refs[:HALF], refs[HALF]
-    core = lax.axis_index("core")
-    first = core * HALF
-    keep = jnp.where(core == 0, 1.0, 0.0).astype(F32)
+    keep = jnp.where(lax.axis_index("core") == 0, 1.0, 0.0).astype(F32)
     turned[...] = plane[...].T
     margin[...] = jnp.zeros(margin.shape, F32)
     for c in range(1, COLS):
@@ -197,17 +223,20 @@
         margin[COLS + c - 1 : COLS + c, :] = plane[16 * c : 16 * c + 1, :] * keep
 
     def step(t, carry):
-        rows = pl.ds(pl.multiple_of(t * 16, 16), 16)
-        field = turned[rows, :]
-        sums = [jnp.full((16, GRID), bias[first + o], F32) for o in range(HALF)]
-        for i in range(WIDTH):
-            lifted = lift(field, 0.5 * scale[i], 0.5 * shift[i])
-            sums = [sums[o] + weight[i, first + o] * lifted for o in range(HALF)]
-        for o in range(HALF):
-            out[o][rows, :] = sums[o]
+        rows = pl.ds(pl.multiple_of(t * 64, 64), 64)
+        for lanes in (slice(0, 128), slice(128, 256)):
+            field = turned[rows, lanes]
+            sums = [jnp.broadcast_to(factors[32 + o : 33 + o, :], (64, 128)) for o in range(HALF)]
+            for i in range(WIDTH):
+                lifted = lift(field, factors[i : i + 1, :], factors[WIDTH + i : WIDTH + i + 1, :])
+                for o in range(HALF):
+                    row = 40 + HALF * i + o
+                    sums[o] = sums[o] + factors[row : row + 1, :] * lifted
+            for o in range(HALF):
+                out[o][rows, lanes] = sums[o]
         return carry
 
-    lax.fori_loop(0, GRID // 16, step, 0)
+    lax.fori_loop(0, GRID // 64, step, 0)
 
 
 def inverse_kernel(received, margin, z_table, y_table, scalars, *refs):
@@ -441,20 +470,21 @@
     fields = [shape(GRID, GRID)] * HALF
 
     row_of = pltpu.SMEM((WIDTH,), F32)
-    spread, z_near, y_near, scalars, ring, doubling = call(
+    spread, z_near, y_near, scalars, factors, ring, doubling = call(
         first_kernel,
-        (field, z_forward, y_table, lift_scale, lift_shift, readout),
+        (field, z_forward, y_table, lift_scale, lift_shift, readout, local_bias, local_weight),
         (),
         [
             shape(PLANES, 2, COLS, GRID),
             jax.ShapeDtypeStruct(z_forward.shape, BF16),
             jax.ShapeDtypeStruct(y_table.shape, BF16),
             shape(24, GRID),
+            shape(168, 128),
             shape(32, GRID),
             shape(64, 128),
         ],
-        [row_of, row_of, row_of, pltpu.SemaphoreType.DMA((7,))],
-        far=6,
+        [row_of] * 4 + [pltpu.SMEM((WIDTH, WIDTH), F32), pltpu.SemaphoreType.DMA((9,))],
+        far=8,
     )
     plane = exchange(spread.reshape(COLS, COLS, GRID), COL).reshape(GRID, GRID)
     line_scratch = pltpu.VMEM((MODES, HALF, 2 * GRID), F32)
@@ -468,8 +498,8 @@
     lifted = exchange(lifted, everywhere)
     margin, *local = call(
         local_kernel,
-        (plane,),
-        (lift_scale, lift_shift, local_bias, local_weight),
+        (plane, factors),
+        (),
         [shape(2 * COLS, GRID)] + fields,
         [pltpu.VMEM((GRID, GRID), F32)],
         flops=1 << 27,

time: 147 us -> 147 us (level)
  transfers between devices with their start and end apart: 3 -> 3, of which waited for: 1 -> 1; matrix products, arithmetic and copies ran while one was open for 0% -> 0% of each run, Pallas kernels for 5% -> 4%
where the time goes in v8:
time: 147 us
  blocking collectives  103 us (70%)
  Pallas kernels  17.6 us (12%)
  starting transfers between devices  13.9 us (9%)
  waiting for transfers between devices  11.9 us (8%)
    all_to_all x5, blocking collectives, exchange(): return lax.all_to_all(value, axes, split_axis=0, concat_axis=0, tiled=True)  103 us
    pallas_call x11, Pallas kernels, call(): pl.pallas_call(kernel, in_specs=[smem] * len(scalars) + [vmem] * (len(ope...  17.6 us
    all_to_all x1, waiting for transfers between devices, exchange(): return lax.all_to_all(value, axes, split_axis=0, concat_axis=0, tiled=True)  11.9 us
    all_to_all x1, starting transfers between devices, exchange(): return lax.all_to_all(value, axes, split_axis=0, concat_axis=0, tiled=True)  8.53 us
    ppermute x1, starting transfers between devices, shards(): second = lax.ppermute(second, ROW, even_pairs)  4.67 us
  transfers between devices with their start and end apart: 3, of which 1 were waited for; matrix products, arithmetic and copies ran while one was open for 0% of the time, Pallas kernels for 4%

profile of v8, /device:TPU:1, one launch (start us, length us, event | category | flops | bytes accessed | tf_op | source)
XLA Modules:
  0.0 146.9 jit_solution(5213440218082712801)
XLA Ops:
  0.6 1.2 shard_map.122
  1.8 16.5 %all_to_all.48 = f32[16,16,256]{2,1,0:T(8,128)S(1)} all-to-all(f32[16,16,256]{2,1,0:T(8,128)S(1)} %bitcast.28), channel_id=1, replica_groups=mesh['y'=8,'zh'=4,'zl'=2,'x'=4,'core'=2] {'zl','x','core'}, dimensions={0} | all-to-all | bytes 524288 | tf_op jit(solution)/shard_map/all_to_all | solution.py:459
  18.4 2.7 %shard_map.123 = f32[512,128]{1,0:T(8,128)S(1)} custom-call(f32[256,256]{1,0:T(8,128)S(1)} %bitcast.21, bf16[256,256]{1,0:T(8,128)(2,1)S(1)} %get-tuple-element.55.z_table, bf16[256,512]{1,0:T(8,128)(2,1)S(1)} %get-tuple-element.56.y_table, f32[24,256]{1,0:T(8,128)S(1)} %get-tuple-element.57.scalars), custom_call_target="tpu_custom_call" | custom-call | tf_op jit(solution)/shard_map/pallas_call | solution.py:446
  21.1 0.0 copy-start.4
  21.1 33.9 %all_to_all.49 = f32[512,1,128]{2,1,0:T(1,128)S(1)} all-to-all(f32[512,1,128]{2,1,0:T(1,128)S(1)} %bitcast.24), channel_id=1, replica_groups=mesh['y'=8,'zh'=4,'zl'=2,'x'=4,'core'=2] {'zl','x','core','y','zh'}, dimensions={0} | all-to-all | bytes 524288 | tf_op jit(solution)/shard_map/all_to_all | solution.py:459
  55.0 1.7 %shard_map.124 = (f32[512,128]{1,0:T(8,128)}, f32[2,64,128]{2,1,0:T(8,128)S(1)}) custom-call(f32[512,128]{1,0:T(8,128)S(1)} %bitcast.23, bf16[2,4,16,16,128]{4,3,2,1,0:T(8,128)(2,1)S(1)} %copy-done.2, bf16[256,256]{1,0:T(8,128)(2,1)S(1)} %copy-done.4), custom_call_target="tpu_custom_call" | custom-call | tf_op jit(solution)/shard_map/pallas_call | solution.py:446
  56.7 8.5 %all-to-all-start.2 = ((f32[512,1,128]{2,1,0:T(1,128)}), f32[512,1,128]{2,1,0:T(1,128)S(1)}, u32[]{:S(2)}, u32[]{:S(2)}) async-start(f32[512,1,128]{2,1,0:T(1,128)} %bitcast.7), calls=%async_computation.2 | async-start | bytes 524288 | tf_op jit(solution)/shard_map/all_to_all | solution.py:459
  65.2 0.0 copy-start
  65.2 0.0 copy-start.5
  65.2 5.0 %shard_map.125 = (f32[32,256]{1,0:T(8,128)S(1)}, f32[256,256]{1,0:T(8,128)S(1)}, f32[256,256]{1,0:T(8,128)S(1)}, f32[256,256]{1,0:T(8,128)S(1)}, f32[256,256]{1,...) custom-call(f32[256,256]{1,0:T(8,128)S(1)} %bitcast.22, ...), custom_call_target="tpu_custom_call" | custom-call | flops 134217728 | bytes 4194304 | tf_op jit(solution)/shard_map/pallas_call | solution.py:446
  70.2 11.9 %all-to-all-done.2 = f32[512,1,128]{2,1,0:T(1,128)S(1)} async-done(((f32[512,1,128]{2,1,0:T(1,128)}), f32[512,1,128]{2,1,0:T(1,128)S(1)}, u32[]{:S(2)}, u32[]{:S(2)}) %all-to-all-start.2) | async-done | bytes 262176 | tf_op jit(solution)/shard_map/all_to_all | solution.py:459
  82.1 2.2 %shard_map.126 = (f32[16,40,128]{2,1,0:T(8,128)S(1)}, f32[256,256]{1,0:T(8,128)S(1)}, f32[256,256]{1,0:T(8,128)S(1)}, f32[256,256]{1,0:T(8,128)S(1)}, f32[256,25...) custom-call(f32[512,128]{1,0:T(8,128)S(1)} %bitcast.20, ...), custom_call_target="tpu_custom_call" | custom-call | tf_op jit(solution)/shard_map/pallas_call | solution.py:446
  84.3 11.1 %all_to_all.50.received = f32[16,40,128]{2,1,0:T(8,128)S(1)} all-to-all(f32[16,40,128]{2,1,0:T(8,128)S(1)} %get-tuple-element.69), channel_id=1, replica_groups=mesh['y'=8,'zh'=4,'zl'=2,'x'=4,'core'=2] {'zl','x','core'}, dimensions={0} | all-to-all | bytes 655360 | tf_op jit(solution)/shard_map/all_to_all | solution.py:459
  95.4 0.1 shard_map.127
  95.5 0.7 collective-permute-start
  96.2 4.7 %collective-permute-start.1 = (f32[80,128]{1,0:T(8,128)S(1)}, f32[80,128]{1,0:T(8,128)S(1)}, u32[]{:S(2)}, u32[]{:S(2)}) collective-permute-start(f32[80,128]{1,0:T(8,128)S(1)} %get-tuple-element.73), channel_id=1, source_target_pairs={{0,16},{16,0},{32,48},{48,32},{64,80},{80,64},{96,112},{112,96},{1... | collective-permute-start | bytes 122888 | tf_op jit(solution)/shard_map/ppermute | solution.py:532
  100.9 1.4 shard_map.129
  102.3 0.2 shard_map.128.rest
  102.5 0.2 shard_map.130
  102.7 0.0 copy-start.3
  102.7 12.3 %all_to_all.51 = f32[16,16,256]{2,1,0:T(8,128)S(1)} all-to-all(f32[16,16,256]{2,1,0:T(8,128)S(1)} %get-tuple-element.92), channel_id=1, replica_groups=mesh['y'=8,'zh'=4,'zl'=2,'x'=4,'core'=2] {'zl','x','core'}, dimensions={0} | all-to-all | bytes 524288 | tf_op jit(solution)/shard_map/all_to_all | solution.py:459
  115.0 1.6 %shard_map.131 = (f32[512,128]{1,0:T(8,128)S(1)}, f32[8,16,256]{2,1,0:T(8,128)}) custom-call(f32[256,256]{1,0:T(8,128)S(1)} %bitcast.26, f32[8,16,256]{2,1,0:T(8,128)S(1)} %get-tuple-element.93.rest, bf16[256,256]{1,0:T(8,128)(2,1)S(1)} %copy-done.3, bf16[256,512]{1,0:T(8,128)(2,1)S(1)} %copy-done, f32[256,256]{1,0:T(8,128)S(1)} %get-tuple-element.94.refs_0_, ...), custom_call_target="tpu_custom_call" | custom-call | tf_op jit(solution)/shard_map/pallas_call | solution.py:446
  116.7 28.7 %all_to_all.52 = f32[512,1,128]{2,1,0:T(1,128)S(1)} all-to-all(f32[512,1,128]{2,1,0:T(1,128)S(1)} %bitcast.27), channel_id=1, replica_groups=mesh['y'=8,'zh'=4,'zl'=2,'x'=4,'core'=2] {'zl','x','core','y','zh'}, dimensions={0} | all-to-all | bytes 524288 | tf_op jit(solution)/shard_map/all_to_all | solution.py:459
  145.4 1.3 shard_map.132
  (10 shorter events, 0.0 us)
Async XLA Ops:
  18.4 36.6 %copy-start.2 = (bf16[2,4,16,16,128]{4,3,2,1,0:T(8,128)(2,1)S(1)}, bf16[2,4,16,16,128]{4,3,2,1,0:T(8,128)(2,1)}, u32[]{:S(2)}) copy-start(bf16[2,4,16,16,128]{4,3,2,1,0:T(8,128)(2,1)} %weight.1) | copy-start | bytes 1572868
  21.1 33.9 %copy-start.4 = (bf16[256,256]{1,0:T(8,128)(2,1)S(1)}, bf16[256,256]{1,0:T(8,128)(2,1)}, u32[]{:S(2)}) copy-start(bf16[256,256]{1,0:T(8,128)(2,1)} %constant.10.clone.x_table) | copy-start | bytes 393220
  56.7 25.5 %all-to-all-start.2 = ((f32[512,1,128]{2,1,0:T(1,128)}), f32[512,1,128]{2,1,0:T(1,128)S(1)}, u32[]{:S(2)}, u32[]{:S(2)}) async-start(f32[512,1,128]{2,1,0:T(1,128)} %bitcast.7), calls=%async_computation.2 | async-start | bytes 524288 | tf_op jit(solution)/shard_map/all_to_all | solution.py:459
  65.2 16.9 %copy-start = (bf16[256,512]{1,0:T(8,128)(2,1)S(1)}, bf16[256,512]{1,0:T(8,128)(2,1)}, u32[]{:S(2)}) copy-start(bf16[256,512]{1,0:T(8,128)(2,1)} %constant.9.clone.far_y.y_table) | copy-start | bytes 786436
  65.2 16.9 %copy-start.5 = (bf16[512,256]{1,0:T(8,128)(2,1)S(1)}, bf16[512,256]{1,0:T(8,128)(2,1)}, u32[]{:S(2)}) copy-start(bf16[512,256]{1,0:T(8,128)(2,1)} %constant.11.clone.z_table) | copy-start | bytes 786436
  84.3 11.1 %copy-start.1 = (f32[1,8,16,256]{3,2,1,0:T(8,128)S(1)}, f32[1,8,16,256]{3,2,1,0:T(8,128)}, u32[]{:S(2)}) copy-start(f32[1,8,16,256]{3,2,1,0:T(8,128)} %param.11) | copy-start | bytes 393220
  95.5 6.9 %collective-permute-start = (f32[80,128]{1,0:T(8,128)S(1)}, f32[80,128]{1,0:T(8,128)S(1)}, u32[]{:S(2)}, u32[]{:S(2)}) collective-permute-start(f32[80,128]{1,0:T(8,128)S(1)} %get-tuple-element.72), channel_id=1, source_target_pairs={{16,32},{32,16},{48,64},{64,48},{80,96},{96,80},{112,128},{128,112... | collective-permute-start | bytes 122888 | tf_op jit(solution)/shard_map/ppermute | solution.py:531
  96.2 6.3 %collective-permute-start.1 = (f32[80,128]{1,0:T(8,128)S(1)}, f32[80,128]{1,0:T(8,128)S(1)}, u32[]{:S(2)}, u32[]{:S(2)}) collective-permute-start(f32[80,128]{1,0:T(8,128)S(1)} %get-tuple-element.73), channel_id=1, source_target_pairs={{0,16},{16,0},{32,48},{48,32},{64,80},{80,64},{96,112},{112,96},{1... | collective-permute-start | bytes 122888 | tf_op jit(solution)/shard_map/ppermute | solution.py:532
  102.7 12.3 %copy-start.3 = (bf16[256,256]{1,0:T(8,128)(2,1)S(1)}, bf16[256,256]{1,0:T(8,128)(2,1)}, u32[]{:S(2)}) copy-start(bf16[256,256]{1,0:T(8,128)(2,1)} %constant.8.clone.far_z.z_table) | copy-start | bytes 393220

commit v9 on v8

--- a/solution.py
+++ b/solution.py
@@ -273,15 +273,19 @@
     padded[256:264, :] = jnp.zeros((8, GRID), F32)
     value = total[...].T
     padded[4:260, :] = value
-    beside = pltpu.roll(value, 1, 0) + pltpu.roll(value, GRID - 1, 0) + beside_z(value, lane_index((GRID, GRID)))
-    spectral[...] = 6.0 * value - beside
     blank = jnp.zeros((1, GRID), F32)
+    lane = lane_index((8, GRID))
+    tiles = [None]
+    for m in range(1, COLS):
+        tile = padded[16 * m : 16 * m + 8, :]
+        beside = pltpu.roll(tile, 1, 0) + pltpu.roll(tile, 7, 0) + beside_z(tile, lane)
+        tiles.append(6.0 * tile - beside)
     for c in range(COLS):
         before, after = blank, blank
         if c > 0:
-            before = spectral[16 * c - 1 : 16 * c, :] - margin[c : c + 1, :]
+            before = tiles[c][3:4] - margin[c : c + 1, :]
         if c < COLS - 1:
-            after = spectral[16 * c + 16 : 16 * c + 17, :] - margin[COLS + c : COLS + c + 1, :]
+            after = tiles[c + 1][4:5] - margin[COLS + c : COLS + c + 1, :]
         for h in range(2):
             lanes = slice(128 * h, 128 * h + 128)
             out[c, 20 * h : 20 * h + 1, :] = before[:, lanes]

time: 147 us -> 147 us (level)
  no operation moved by 1% of the time
where the time goes in v9:
time: 147 us
  blocking collectives  103 us (70%)
  Pallas kernels  17.5 us (12%)
  starting transfers between devices  13.7 us (9%)
  waiting for transfers between devices  12.1 us (8%)
    all_to_all x5, blocking collectives, exchange(): return lax.all_to_all(value, axes, split_axis=0, concat_axis=0, tiled=True)  103 us
    pallas_call x11, Pallas kernels, call(): pl.pallas_call(kernel, in_specs=[smem] * len(scalars) + [vmem] * (len(ope...  17.5 us
    all_to_all x1, waiting for transfers between devices, exchange(): return lax.all_to_all(value, axes, split_axis=0, concat_axis=0, tiled=True)  12.1 us
    all_to_all x1, starting transfers between devices, exchange(): return lax.all_to_all(value, axes, split_axis=0, concat_axis=0, tiled=True)  8.35 us
    ppermute x1, starting transfers between devices, shards(): second = lax.ppermute(second, ROW, even_pairs)  4.67 us
  transfers between devices with their start and end apart: 3, of which 1 were waited for; matrix products, arithmetic and copies ran while one was open for 0% of the time, Pallas kernels for 4%

profile of v9, /device:TPU:1, one launch (start us, length us, event | category | flops | bytes accessed | tf_op | source)
XLA Modules:
  0.0 147.0 jit_solution(15703887961672678883)
XLA Ops:
  0.6 1.2 shard_map.122
  1.8 16.5 %all_to_all.48 = f32[16,16,256]{2,1,0:T(8,128)S(1)} all-to-all(f32[16,16,256]{2,1,0:T(8,128)S(1)} %bitcast.28), channel_id=1, replica_groups=mesh['y'=8,'zh'=4,'zl'=2,'x'=4,'core'=2] {'zl','x','core'}, dimensions={0} | all-to-all | bytes 524288 | tf_op jit(solution)/shard_map/all_to_all | solution.py:463
  18.4 2.7 %shard_map.123 = f32[512,128]{1,0:T(8,128)S(1)} custom-call(f32[256,256]{1,0:T(8,128)S(1)} %bitcast.21, bf16[256,256]{1,0:T(8,128)(2,1)S(1)} %get-tuple-element.55.z_table, bf16[256,512]{1,0:T(8,128)(2,1)S(1)} %get-tuple-element.56.y_table, f32[24,256]{1,0:T(8,128)S(1)} %get-tuple-element.57.scalars), custom_call_target="tpu_custom_call" | custom-call | tf_op jit(solution)/shard_map/pallas_call | solution.py:450
  21.1 0.0 copy-start.4
  21.1 33.9 %all_to_all.49 = f32[512,1,128]{2,1,0:T(1,128)S(1)} all-to-all(f32[512,1,128]{2,1,0:T(1,128)S(1)} %bitcast.24), channel_id=1, replica_groups=mesh['y'=8,'zh'=4,'zl'=2,'x'=4,'core'=2] {'zl','x','core','y','zh'}, dimensions={0} | all-to-all | bytes 524288 | tf_op jit(solution)/shard_map/all_to_all | solution.py:463
  55.0 1.7 %shard_map.124 = (f32[512,128]{1,0:T(8,128)}, f32[2,64,128]{2,1,0:T(8,128)S(1)}) custom-call(f32[512,128]{1,0:T(8,128)S(1)} %bitcast.23, bf16[2,4,16,16,128]{4,3,2,1,0:T(8,128)(2,1)S(1)} %copy-done.2, bf16[256,256]{1,0:T(8,128)(2,1)S(1)} %copy-done.4), custom_call_target="tpu_custom_call" | custom-call | tf_op jit(solution)/shard_map/pallas_call | solution.py:450
  56.7 8.3 %all-to-all-start.2 = ((f32[512,1,128]{2,1,0:T(1,128)}), f32[512,1,128]{2,1,0:T(1,128)S(1)}, u32[]{:S(2)}, u32[]{:S(2)}) async-start(f32[512,1,128]{2,1,0:T(1,128)} %bitcast.7), calls=%async_computation.2 | async-start | bytes 524288 | tf_op jit(solution)/shard_map/all_to_all | solution.py:463
  65.0 0.0 copy-start
  65.0 0.0 copy-start.5
  65.0 5.0 %shard_map.125 = (f32[32,256]{1,0:T(8,128)S(1)}, f32[256,256]{1,0:T(8,128)S(1)}, f32[256,256]{1,0:T(8,128)S(1)}, f32[256,256]{1,0:T(8,128)S(1)}, f32[256,256]{1,...) custom-call(f32[256,256]{1,0:T(8,128)S(1)} %bitcast.22, ...), custom_call_target="tpu_custom_call" | custom-call | flops 134217728 | bytes 4194304 | tf_op jit(solution)/shard_map/pallas_call | solution.py:450
  70.1 12.1 %all-to-all-done.2 = f32[512,1,128]{2,1,0:T(1,128)S(1)} async-done(((f32[512,1,128]{2,1,0:T(1,128)}), f32[512,1,128]{2,1,0:T(1,128)S(1)}, u32[]{:S(2)}, u32[]{:S(2)}) %all-to-all-start.2) | async-done | bytes 262176 | tf_op jit(solution)/shard_map/all_to_all | solution.py:463
  82.1 2.1 %shard_map.126 = (f32[16,40,128]{2,1,0:T(8,128)S(1)}, f32[256,256]{1,0:T(8,128)S(1)}, f32[256,256]{1,0:T(8,128)S(1)}, f32[256,256]{1,0:T(8,128)S(1)}, f32[256,25...) custom-call(f32[512,128]{1,0:T(8,128)S(1)} %bitcast.20, ...), custom_call_target="tpu_custom_call" | custom-call | tf_op jit(solution)/shard_map/pallas_call | solution.py:450
  84.2 11.3 %all_to_all.50.received = f32[16,40,128]{2,1,0:T(8,128)S(1)} all-to-all(f32[16,40,128]{2,1,0:T(8,128)S(1)} %get-tuple-element.69), channel_id=1, replica_groups=mesh['y'=8,'zh'=4,'zl'=2,'x'=4,'core'=2] {'zl','x','core'}, dimensions={0} | all-to-all | bytes 655360 | tf_op jit(solution)/shard_map/all_to_all | solution.py:463
  95.5 0.1 shard_map.127
  95.6 0.7 collective-permute-start
  96.3 4.7 %collective-permute-start.1 = (f32[80,128]{1,0:T(8,128)S(1)}, f32[80,128]{1,0:T(8,128)S(1)}, u32[]{:S(2)}, u32[]{:S(2)}) collective-permute-start(f32[80,128]{1,0:T(8,128)S(1)} %get-tuple-element.73), channel_id=1, source_target_pairs={{0,16},{16,0},{32,48},{48,32},{64,80},{80,64},{96,112},{112,96},{1... | collective-permute-start | bytes 122888 | tf_op jit(solution)/shard_map/ppermute | solution.py:536
  101.0 1.4 shard_map.129
  102.3 0.2 shard_map.128.rest
  102.6 0.2 shard_map.130
  102.8 0.0 copy-start.3
  102.8 12.3 %all_to_all.51 = f32[16,16,256]{2,1,0:T(8,128)S(1)} all-to-all(f32[16,16,256]{2,1,0:T(8,128)S(1)} %get-tuple-element.92), channel_id=1, replica_groups=mesh['y'=8,'zh'=4,'zl'=2,'x'=4,'core'=2] {'zl','x','core'}, dimensions={0} | all-to-all | bytes 524288 | tf_op jit(solution)/shard_map/all_to_all | solution.py:463
  115.1 1.6 %shard_map.131 = (f32[512,128]{1,0:T(8,128)S(1)}, f32[8,16,256]{2,1,0:T(8,128)}) custom-call(f32[256,256]{1,0:T(8,128)S(1)} %bitcast.26, f32[8,16,256]{2,1,0:T(8,128)S(1)} %get-tuple-element.93.rest, bf16[256,256]{1,0:T(8,128)(2,1)S(1)} %copy-done.3, bf16[256,512]{1,0:T(8,128)(2,1)S(1)} %copy-done, f32[256,256]{1,0:T(8,128)S(1)} %get-tuple-element.94.refs_0_, ...), custom_call_target="tpu_custom_call" | custom-call | tf_op jit(solution)/shard_map/pallas_call | solution.py:450
  116.7 28.7 %all_to_all.52 = f32[512,1,128]{2,1,0:T(1,128)S(1)} all-to-all(f32[512,1,128]{2,1,0:T(1,128)S(1)} %bitcast.27), channel_id=1, replica_groups=mesh['y'=8,'zh'=4,'zl'=2,'x'=4,'core'=2] {'zl','x','core','y','zh'}, dimensions={0} | all-to-all | bytes 524288 | tf_op jit(solution)/shard_map/all_to_all | solution.py:463
  145.5 1.3 shard_map.132
  (10 shorter events, 0.0 us)
Async XLA Ops:
  18.4 36.6 %copy-start.2 = (bf16[2,4,16,16,128]{4,3,2,1,0:T(8,128)(2,1)S(1)}, bf16[2,4,16,16,128]{4,3,2,1,0:T(8,128)(2,1)}, u32[]{:S(2)}) copy-start(bf16[2,4,16,16,128]{4,3,2,1,0:T(8,128)(2,1)} %weight.1) | copy-start | bytes 1572868
  21.1 33.9 %copy-start.4 = (bf16[256,256]{1,0:T(8,128)(2,1)S(1)}, bf16[256,256]{1,0:T(8,128)(2,1)}, u32[]{:S(2)}) copy-start(bf16[256,256]{1,0:T(8,128)(2,1)} %constant.10.clone.x_table) | copy-start | bytes 393220
  56.7 25.5 %all-to-all-start.2 = ((f32[512,1,128]{2,1,0:T(1,128)}), f32[512,1,128]{2,1,0:T(1,128)S(1)}, u32[]{:S(2)}, u32[]{:S(2)}) async-start(f32[512,1,128]{2,1,0:T(1,128)} %bitcast.7), calls=%async_computation.2 | async-start | bytes 524288 | tf_op jit(solution)/shard_map/all_to_all | solution.py:463
  65.0 17.1 %copy-start = (bf16[256,512]{1,0:T(8,128)(2,1)S(1)}, bf16[256,512]{1,0:T(8,128)(2,1)}, u32[]{:S(2)}) copy-start(bf16[256,512]{1,0:T(8,128)(2,1)} %constant.9.clone.far_y.y_table) | copy-start | bytes 786436
  65.0 17.1 %copy-start.5 = (bf16[512,256]{1,0:T(8,128)(2,1)S(1)}, bf16[512,256]{1,0:T(8,128)(2,1)}, u32[]{:S(2)}) copy-start(bf16[512,256]{1,0:T(8,128)(2,1)} %constant.11.clone.z_table) | copy-start | bytes 786436
  84.2 11.3 %copy-start.1 = (f32[1,8,16,256]{3,2,1,0:T(8,128)S(1)}, f32[1,8,16,256]{3,2,1,0:T(8,128)}, u32[]{:S(2)}) copy-start(f32[1,8,16,256]{3,2,1,0:T(8,128)} %param.11) | copy-start | bytes 393220
  95.6 6.9 %collective-permute-start = (f32[80,128]{1,0:T(8,128)S(1)}, f32[80,128]{1,0:T(8,128)S(1)}, u32[]{:S(2)}, u32[]{:S(2)}) collective-permute-start(f32[80,128]{1,0:T(8,128)S(1)} %get-tuple-element.72), channel_id=1, source_target_pairs={{16,32},{32,16},{48,64},{64,48},{80,96},{96,80},{112,128},{128,112... | collective-permute-start | bytes 122888 | tf_op jit(solution)/shard_map/ppermute | solution.py:535
  96.3 6.3 %collective-permute-start.1 = (f32[80,128]{1,0:T(8,128)S(1)}, f32[80,128]{1,0:T(8,128)S(1)}, u32[]{:S(2)}, u32[]{:S(2)}) collective-permute-start(f32[80,128]{1,0:T(8,128)S(1)} %get-tuple-element.73), channel_id=1, source_target_pairs={{0,16},{16,0},{32,48},{48,32},{64,80},{80,64},{96,112},{112,96},{1... | collective-permute-start | bytes 122888 | tf_op jit(solution)/shard_map/ppermute | solution.py:536
  102.8 12.3 %copy-start.3 = (bf16[256,256]{1,0:T(8,128)(2,1)S(1)}, bf16[256,256]{1,0:T(8,128)(2,1)}, u32[]{:S(2)}) copy-start(bf16[256,256]{1,0:T(8,128)(2,1)} %constant.8.clone.far_z.z_table) | copy-start | bytes 393220

commit v10 on v9

--- a/solution.py
+++ b/solution.py
@@ -393,8 +393,9 @@
         value = wide[edge]
         rest = 6.0 * value - (wide[inner] + beside_y(value) + beside_z(value, lane))
         rest = rest[4:20] - field[edge]
+        value = value[2:22]
         sent.append(jnp.concatenate([value[:, :128], value[:, 128:], rest[:, :128], rest[:, 128:]], axis=0))
-    odd = jnp.broadcast_to(ring[26:27, 0:128], (80, 128)) > 0.5
+    odd = jnp.broadcast_to(ring[26:27, 0:128], (72, 128)) > 0.5
     first[...] = jnp.where(odd, sent[1], sent[0])
     second[...] = jnp.where(odd, sent[0], sent[1])
 
@@ -419,13 +420,14 @@
     lane = lane_index((24, GRID))
     inside = ring[0:24, :]
     values = [rest[q] for q in range(PLANES)]
-    odd = jnp.broadcast_to(ring[26:27, 0:128], (80, 128)) > 0.5
+    odd = jnp.broadcast_to(ring[26:27, 0:128], (72, 128)) > 0.5
     before, after = jnp.where(odd, second[...], first[...]), jnp.where(odd, first[...], second[...])
     outer = []
+    blank = jnp.zeros((2, GRID), F32)
     for n, ref, edge in ((0, before, 0), (1, after, PLANES - 1)):
-        beyond = jnp.concatenate([ref[0:24], ref[24:48]], axis=1)
+        beyond = jnp.concatenate([blank, jnp.concatenate([ref[0:20], ref[20:40]], axis=1), blank], axis=0)
         values[edge] = values[edge] - inside * beyond
-        part = jnp.concatenate([ref[48:64], ref[64:80]], axis=1) - wide[edge, 4:20, :]
+        part = jnp.concatenate([ref[40:56], ref[56:72]], axis=1) - wide[edge, 4:20, :]
         outer.append(ring[24 + n : 25 + n, :] * part)
     for q in range(PLANES):
         low = outer[0] if q == 0 else values[q - 1][4:20]
@@ -528,7 +530,7 @@
     )
     message = exchange(message, COL)
     wide, first, second = call(
-        edge_kernel, (message, field, ring), (), [shape(PLANES, 24, GRID), shape(80, 128), shape(80, 128)], []
+        edge_kernel, (message, field, ring), (), [shape(PLANES, 24, GRID), shape(72, 128), shape(72, 128)], []
     )
     odd_pairs = [(r, r + 1 if r % 2 else r - 1) for r in range(1, ROWS - 1)]
     even_pairs = [(r, r - 1 if r % 2 else r + 1) for r in range(ROWS)]

time: 147 us -> 147 us (level)
  no operation moved by 1% of the time
where the time goes in v10:
time: 147 us
  blocking collectives  103 us (70%)
  Pallas kernels  17.5 us (12%)
  starting transfers between devices  13.7 us (9%)
  waiting for transfers between devices  12.1 us (8%)
    all_to_all x5, blocking collectives, exchange(): return lax.all_to_all(value, axes, split_axis=0, concat_axis=0, tiled=True)  103 us
    pallas_call x11, Pallas kernels, call(): pl.pallas_call(kernel, in_specs=[smem] * len(scalars) + [vmem] * (len(ope...  17.5 us
    all_to_all x1, waiting for transfers between devices, exchange(): return lax.all_to_all(value, axes, split_axis=0, concat_axis=0, tiled=True)  12.1 us
    all_to_all x1, starting transfers between devices, exchange(): return lax.all_to_all(value, axes, split_axis=0, concat_axis=0, tiled=True)  8.35 us
    ppermute x1, starting transfers between devices, shards(): second = lax.ppermute(second, ROW, even_pairs)  4.67 us
  transfers between devices with their start and end apart: 3, of which 1 were waited for; matrix products, arithmetic and copies ran while one was open for 0% of the time, Pallas kernels for 4%

profile of v10, /device:TPU:1, one launch (start us, length us, event | category | flops | bytes accessed | tf_op | source)
XLA Modules:
  0.0 146.9 jit_solution(1456033357905397632)
XLA Ops:
  0.6 1.2 shard_map.122
  1.8 16.5 %all_to_all.48 = f32[16,16,256]{2,1,0:T(8,128)S(1)} all-to-all(f32[16,16,256]{2,1,0:T(8,128)S(1)} %bitcast.28), channel_id=1, replica_groups=mesh['y'=8,'zh'=4,'zl'=2,'x'=4,'core'=2] {'zl','x','core'}, dimensions={0} | all-to-all | bytes 524288 | tf_op jit(solution)/shard_map/all_to_all | solution.py:465
  18.4 2.7 %shard_map.123 = f32[512,128]{1,0:T(8,128)S(1)} custom-call(f32[256,256]{1,0:T(8,128)S(1)} %bitcast.21, bf16[256,256]{1,0:T(8,128)(2,1)S(1)} %get-tuple-element.55.z_table, bf16[256,512]{1,0:T(8,128)(2,1)S(1)} %get-tuple-element.56.y_table, f32[24,256]{1,0:T(8,128)S(1)} %get-tuple-element.57.scalars), custom_call_target="tpu_custom_call" | custom-call | tf_op jit(solution)/shard_map/pallas_call | solution.py:452
  21.1 0.0 copy-start.4
  21.1 33.9 %all_to_all.49 = f32[512,1,128]{2,1,0:T(1,128)S(1)} all-to-all(f32[512,1,128]{2,1,0:T(1,128)S(1)} %bitcast.24), channel_id=1, replica_groups=mesh['y'=8,'zh'=4,'zl'=2,'x'=4,'core'=2] {'zl','x','core','y','zh'}, dimensions={0} | all-to-all | bytes 524288 | tf_op jit(solution)/shard_map/all_to_all | solution.py:465
  55.0 1.7 %shard_map.124 = (f32[512,128]{1,0:T(8,128)}, f32[2,64,128]{2,1,0:T(8,128)S(1)}) custom-call(f32[512,128]{1,0:T(8,128)S(1)} %bitcast.23, bf16[2,4,16,16,128]{4,3,2,1,0:T(8,128)(2,1)S(1)} %copy-done.2, bf16[256,256]{1,0:T(8,128)(2,1)S(1)} %copy-done.4), custom_call_target="tpu_custom_call" | custom-call | tf_op jit(solution)/shard_map/pallas_call | solution.py:452
  56.7 8.3 %all-to-all-start.2 = ((f32[512,1,128]{2,1,0:T(1,128)}), f32[512,1,128]{2,1,0:T(1,128)S(1)}, u32[]{:S(2)}, u32[]{:S(2)}) async-start(f32[512,1,128]{2,1,0:T(1,128)} %bitcast.7), calls=%async_computation.2 | async-start | bytes 524288 | tf_op jit(solution)/shard_map/all_to_all | solution.py:465
  65.0 0.0 copy-start
  65.0 0.0 copy-start.5
  65.0 5.0 %shard_map.125 = (f32[32,256]{1,0:T(8,128)S(1)}, f32[256,256]{1,0:T(8,128)S(1)}, f32[256,256]{1,0:T(8,128)S(1)}, f32[256,256]{1,0:T(8,128)S(1)}, f32[256,256]{1,...) custom-call(f32[256,256]{1,0:T(8,128)S(1)} %bitcast.22, ...), custom_call_target="tpu_custom_call" | custom-call | flops 134217728 | bytes 4194304 | tf_op jit(solution)/shard_map/pallas_call | solution.py:452
  70.1 12.1 %all-to-all-done.2 = f32[512,1,128]{2,1,0:T(1,128)S(1)} async-done(((f32[512,1,128]{2,1,0:T(1,128)}), f32[512,1,128]{2,1,0:T(1,128)S(1)}, u32[]{:S(2)}, u32[]{:S(2)}) %all-to-all-start.2) | async-done | bytes 262176 | tf_op jit(solution)/shard_map/all_to_all | solution.py:465
  82.1 2.1 %shard_map.126 = (f32[16,40,128]{2,1,0:T(8,128)S(1)}, f32[256,256]{1,0:T(8,128)S(1)}, f32[256,256]{1,0:T(8,128)S(1)}, f32[256,256]{1,0:T(8,128)S(1)}, f32[256,25...) custom-call(f32[512,128]{1,0:T(8,128)S(1)} %bitcast.20, ...), custom_call_target="tpu_custom_call" | custom-call | tf_op jit(solution)/shard_map/pallas_call | solution.py:452
  84.2 11.3 %all_to_all.50.received = f32[16,40,128]{2,1,0:T(8,128)S(1)} all-to-all(f32[16,40,128]{2,1,0:T(8,128)S(1)} %get-tuple-element.69), channel_id=1, replica_groups=mesh['y'=8,'zh'=4,'zl'=2,'x'=4,'core'=2] {'zl','x','core'}, dimensions={0} | all-to-all | bytes 655360 | tf_op jit(solution)/shard_map/all_to_all | solution.py:465
  95.5 0.1 shard_map.127
  95.6 0.7 collective-permute-start
  96.3 4.7 %collective-permute-start.1 = (f32[72,128]{1,0:T(8,128)S(1)}, f32[72,128]{1,0:T(8,128)S(1)}, u32[]{:S(2)}, u32[]{:S(2)}) collective-permute-start(f32[72,128]{1,0:T(8,128)S(1)} %get-tuple-element.73), channel_id=1, source_target_pairs={{0,16},{16,0},{32,48},{48,32},{64,80},{80,64},{96,112},{112,96},{1... | collective-permute-start | bytes 110600 | tf_op jit(solution)/shard_map/ppermute | solution.py:538
  101.0 1.4 shard_map.129
  102.3 0.2 shard_map.128.rest
  102.6 0.2 shard_map.130
  102.8 0.0 copy-start.3
  102.8 12.3 %all_to_all.51 = f32[16,16,256]{2,1,0:T(8,128)S(1)} all-to-all(f32[16,16,256]{2,1,0:T(8,128)S(1)} %get-tuple-element.92), channel_id=1, replica_groups=mesh['y'=8,'zh'=4,'zl'=2,'x'=4,'core'=2] {'zl','x','core'}, dimensions={0} | all-to-all | bytes 524288 | tf_op jit(solution)/shard_map/all_to_all | solution.py:465
  115.0 1.6 %shard_map.131 = (f32[512,128]{1,0:T(8,128)S(1)}, f32[8,16,256]{2,1,0:T(8,128)}) custom-call(f32[256,256]{1,0:T(8,128)S(1)} %bitcast.26, f32[8,16,256]{2,1,0:T(8,128)S(1)} %get-tuple-element.93.rest, bf16[256,256]{1,0:T(8,128)(2,1)S(1)} %copy-done.3, bf16[256,512]{1,0:T(8,128)(2,1)S(1)} %copy-done, f32[256,256]{1,0:T(8,128)S(1)} %get-tuple-element.94.refs_0_, ...), custom_call_target="tpu_custom_call" | custom-call | tf_op jit(solution)/shard_map/pallas_call | solution.py:452
  116.7 28.7 %all_to_all.52 = f32[512,1,128]{2,1,0:T(1,128)S(1)} all-to-all(f32[512,1,128]{2,1,0:T(1,128)S(1)} %bitcast.27), channel_id=1, replica_groups=mesh['y'=8,'zh'=4,'zl'=2,'x'=4,'core'=2] {'zl','x','core','y','zh'}, dimensions={0} | all-to-all | bytes 524288 | tf_op jit(solution)/shard_map/all_to_all | solution.py:465
  145.4 1.3 shard_map.132
  (10 shorter events, 0.0 us)
Async XLA Ops:
  18.4 36.6 %copy-start.2 = (bf16[2,4,16,16,128]{4,3,2,1,0:T(8,128)(2,1)S(1)}, bf16[2,4,16,16,128]{4,3,2,1,0:T(8,128)(2,1)}, u32[]{:S(2)}) copy-start(bf16[2,4,16,16,128]{4,3,2,1,0:T(8,128)(2,1)} %weight.1) | copy-start | bytes 1572868
  21.1 33.9 %copy-start.4 = (bf16[256,256]{1,0:T(8,128)(2,1)S(1)}, bf16[256,256]{1,0:T(8,128)(2,1)}, u32[]{:S(2)}) copy-start(bf16[256,256]{1,0:T(8,128)(2,1)} %constant.10.clone.x_table) | copy-start | bytes 393220
  56.7 25.5 %all-to-all-start.2 = ((f32[512,1,128]{2,1,0:T(1,128)}), f32[512,1,128]{2,1,0:T(1,128)S(1)}, u32[]{:S(2)}, u32[]{:S(2)}) async-start(f32[512,1,128]{2,1,0:T(1,128)} %bitcast.7), calls=%async_computation.2 | async-start | bytes 524288 | tf_op jit(solution)/shard_map/all_to_all | solution.py:465
  65.0 17.1 %copy-start = (bf16[256,512]{1,0:T(8,128)(2,1)S(1)}, bf16[256,512]{1,0:T(8,128)(2,1)}, u32[]{:S(2)}) copy-start(bf16[256,512]{1,0:T(8,128)(2,1)} %constant.9.clone.far_y.y_table) | copy-start | bytes 786436
  65.0 17.1 %copy-start.5 = (bf16[512,256]{1,0:T(8,128)(2,1)S(1)}, bf16[512,256]{1,0:T(8,128)(2,1)}, u32[]{:S(2)}) copy-start(bf16[512,256]{1,0:T(8,128)(2,1)} %constant.11.clone.z_table) | copy-start | bytes 786436
  84.2 11.3 %copy-start.1 = (f32[1,8,16,256]{3,2,1,0:T(8,128)S(1)}, f32[1,8,16,256]{3,2,1,0:T(8,128)}, u32[]{:S(2)}) copy-start(f32[1,8,16,256]{3,2,1,0:T(8,128)} %param.11) | copy-start | bytes 393220
  95.6 6.9 %collective-permute-start = (f32[72,128]{1,0:T(8,128)S(1)}, f32[72,128]{1,0:T(8,128)S(1)}, u32[]{:S(2)}, u32[]{:S(2)}) collective-permute-start(f32[72,128]{1,0:T(8,128)S(1)} %get-tuple-element.72), channel_id=1, source_target_pairs={{16,32},{32,16},{48,64},{64,48},{80,96},{96,80},{112,128},{128,112... | collective-permute-start | bytes 110600 | tf_op jit(solution)/shard_map/ppermute | solution.py:537
  96.3 6.3 %collective-permute-start.1 = (f32[72,128]{1,0:T(8,128)S(1)}, f32[72,128]{1,0:T(8,128)S(1)}, u32[]{:S(2)}, u32[]{:S(2)}) collective-permute-start(f32[72,128]{1,0:T(8,128)S(1)} %get-tuple-element.73), channel_id=1, source_target_pairs={{0,16},{16,0},{32,48},{48,32},{64,80},{80,64},{96,112},{112,96},{1... | collective-permute-start | bytes 110600 | tf_op jit(solution)/shard_map/ppermute | solution.py:538
  102.8 12.3 %copy-start.3 = (bf16[256,256]{1,0:T(8,128)(2,1)S(1)}, bf16[256,256]{1,0:T(8,128)(2,1)}, u32[]{:S(2)}) copy-start(bf16[256,256]{1,0:T(8,128)(2,1)} %constant.8.clone.far_z.z_table) | copy-start | bytes 393220
